TPU v7x, 1024 devices: a whole 8x8x8 slice. The times are simulated.
1024 devices in a mesh: dom: 16 (over x, core), grp: 64 (over y, z).
Axes of the slice: x: 8, y: 8, z: 8, core: 2. Of those that a mesh axis runs over, the one named last changes fastest.
Arguments:
- features: bfloat16 [16, 32768, 256], P('dom', 'grp'), may hold values from -6 to 6
- send_list: int32 [16, 64, 16, 2], P('dom', 'grp'), may hold values from -1 to 3, as said below
- nbr_count: int32 [16, 64, 4], P('dom', 'grp'), may hold values from 9 to 12, as said below
- nbr_index: int32 [16, 64, 4, 12], P('dom', 'grp'), may hold values from 0 to 37, as said below
- tiles: bfloat16 [16, 256, 12, 128, 128], P('dom', 'grp'), as said below
- degree: int32 [16, 32768], P('dom', 'grp'), may hold values from 1 to 36, as said below
- w_self: bfloat16 [256, 256], replicated, may hold values from -0.375 to 0.375
- w_nbr: bfloat16 [256, 256], replicated, may hold values from -0.375 to 0.375
- bias: float32 [256], replicated, may hold values from -4 to 4
- cotangent: bfloat16 [16, 32768, 256], P('dom', 'grp'), may hold values from -6 to 6
Outputs:
- hidden_out: bfloat16 [16, 32768, 256], P('dom', 'grp')
- feat_grad: float32 [16, 32768, 256], P('dom', 'grp')
- w_self_grad: float32 [256, 256], replicated
- w_nbr_grad: float32 [256, 256], replicated
- bias_grad: float32 [256], replicated
Inputs may be any that keep to these rules, and one draw needn't show every extreme that they name: send_list[d, g, p, s] is the local block that the device at dom index d and grp index g sends to dom peer p in slot s, or -1 for an empty slot; for each peer the live slots come first; a device sends nothing to itself; in every slab one device is sent all 2 slots by every other peer, and every device fills all 2 slots for at least one peer. nbr_count[d, g, b] is how many leading entries of block b's source list are live; on every device some block has all 12 live. `nbr_index`: entries past the count are ignored and hold arbitrary table entries; every table entry from 4 on is named by at least one live entry of the device's lists. `tiles`: each row of a tile has at most 3 nonzero entries. degree of a node is the number of nonzero entries of its row in the tiles of its block's live source list, or 1 where there are none.
All inputs are finite; a program needn't handle non-finite values.
Results may differ from a plain program's by a relative error of at most 0.0075.
Values may be sent and summed in bfloat16 or wider, within the bound.
No kernel may reach another device: no remote copies, remote signals or barrier semaphores. Data moves between devices by JAX's collectives and lax.ppermute only.
A program may use at most 64 MiB of HBM per device.

v0:
```python
import math

import jax
import jax.numpy as jnp
from jax import lax
from jax.sharding import PartitionSpec as P

BLK = 128


def with_halo(block, sides, width):
    for axis, dim in sides:
        count = lax.axis_size(axis)
        forward = [(i, i + 1) for i in range(count - 1)]
        backward = [(target, source) for source, target in forward]
        low = lax.ppermute(
            lax.slice_in_dim(block, block.shape[dim] - width, None, axis=dim), axis, forward
        )
        high = lax.ppermute(lax.slice_in_dim(block, 0, width, axis=dim), axis, backward)
        block = jnp.concatenate([low, block, high], axis=dim)
    return block


def send_blocks(bucket):
    return lax.all_to_all(bucket, "dom", split_axis=0, concat_axis=0, tiled=True)


def return_grads(bucket):
    return lax.all_to_all(bucket, "dom", split_axis=0, concat_axis=0, tiled=True)


def on_device(
    features, send_list, nbr_count, nbr_index, tiles, degree, w_self, w_nbr, bias, cotangent
):
    own_rows = features[0]
    row_total, width = own_rows.shape
    blocks_n = row_total // BLK
    peers_n = lax.axis_size("dom")
    slots_n = send_list.shape[-1]
    own_blocks = own_rows.reshape(blocks_n, BLK, width)
    padded = with_halo(own_rows, (("grp", 0),), BLK)
    below_rim = padded[:BLK]
    above_rim = padded[row_total + BLK :]
    sent_ids = send_list[0, 0]
    filled = (sent_ids >= 0)[:, :, None, None]
    outgoing = jnp.where(
        filled, jnp.take(own_blocks, jnp.maximum(sent_ids, 0), axis=0), jnp.zeros((), jnp.bfloat16)
    )
    incoming = send_blocks(outgoing)
    source_table = jnp.concatenate(
        [
            own_blocks,
            below_rim[None],
            above_rim[None],
            incoming.reshape(peers_n * slots_n, BLK, width),
        ],
        axis=0,
    )
    table_size = source_table.shape[0]
    sources = nbr_index[0, 0]
    links_n = sources.shape[1]
    live_links = jnp.arange(links_n, dtype=jnp.int32)[None, :] < nbr_count[0, 0][:, None]
    weights = jnp.where(live_links[:, :, None, None], tiles[0], jnp.zeros((), jnp.bfloat16))
    picked = jnp.take(source_table, sources, axis=0)
    summed = jnp.einsum("bkij,bkjf->bif", weights, picked, preferred_element_type=jnp.float32)
    rows_deg = degree[0].astype(jnp.float32)[:, None]
    mean_rows = (summed.reshape(row_total, width) / rows_deg).astype(jnp.bfloat16)
    pre_act = (
        jnp.dot(own_rows, w_self, preferred_element_type=jnp.float32)
        + jnp.dot(mean_rows, w_nbr, preferred_element_type=jnp.float32)
        + bias
    )
    hidden = jax.nn.silu(pre_act).astype(jnp.bfloat16)
    gate_sig = jax.nn.sigmoid(pre_act)
    silu_slope = gate_sig * (1.0 + pre_act * (1.0 - gate_sig))
    pre_grad = (cotangent[0].astype(jnp.float32) * silu_slope).astype(jnp.bfloat16)
    grad_self = jnp.dot(own_rows.T, pre_grad, preferred_element_type=jnp.float32)
    grad_nbr = jnp.dot(mean_rows.T, pre_grad, preferred_element_type=jnp.float32)
    grad_bias = jnp.sum(pre_grad.astype(jnp.float32), axis=0)
    weight_sums = lax.psum((grad_self, grad_nbr, grad_bias), ("dom", "grp"))
    self_grad = jnp.dot(pre_grad, w_self.T, preferred_element_type=jnp.float32)
    mean_grad = jnp.dot(pre_grad, w_nbr.T, preferred_element_type=jnp.float32)
    sum_grad = (mean_grad / rows_deg).astype(jnp.bfloat16).reshape(blocks_n, BLK, width)
    link_grad = jnp.einsum("bkij,bif->bkjf", weights, sum_grad, preferred_element_type=jnp.float32)
    table_grad = (
        jnp.zeros((table_size, BLK, width), jnp.float32)
        .at[sources.reshape(blocks_n * links_n)]
        .add(link_grad.reshape(blocks_n * links_n, BLK, width))
    )
    rim_grads = jnp.concatenate(
        [table_grad[blocks_n].astype(jnp.bfloat16), table_grad[blocks_n + 1].astype(jnp.bfloat16)],
        axis=0,
    )
    rim_padded = with_halo(rim_grads, (("grp", 0),), BLK)
    from_below = rim_padded[:BLK].astype(jnp.float32)
    from_above = rim_padded[3 * BLK :].astype(jnp.float32)
    slot_grads = (
        table_grad[blocks_n + 2 :].reshape(peers_n, slots_n, BLK, width).astype(jnp.bfloat16)
    )
    returned = return_grads(slot_grads)
    owner_pick = (
        sent_ids.reshape(1, peers_n * slots_n) == jnp.arange(blocks_n, dtype=jnp.int32)[:, None]
    )
    collected = jnp.dot(
        owner_pick.astype(jnp.bfloat16),
        returned.reshape(peers_n * slots_n, BLK * width),
        preferred_element_type=jnp.float32,
    ).reshape(blocks_n, BLK, width)
    block_grad = self_grad.reshape(blocks_n, BLK, width) + table_grad[:blocks_n] + collected
    block_grad = block_grad.at[0].add(from_below)
    block_grad = block_grad.at[blocks_n - 1].add(from_above)
    total_nodes = row_total * peers_n * lax.axis_size("grp")
    factor = 1.0 / math.sqrt(total_nodes)
    sum_self, sum_nbr, sum_bias = weight_sums
    return (
        hidden[None],
        block_grad.reshape(1, row_total, width),
        sum_self * factor,
        sum_nbr * factor,
        sum_bias * factor,
    )


def solution(mesh):
    in_specs = (
        P("dom", "grp", None),
        P("dom", "grp", None, None),
        P("dom", "grp", None),
        P("dom", "grp", None, None),
        P("dom", "grp", None, None, None),
        P("dom", "grp"),
        P(),
        P(),
        P(),
        P("dom", "grp", None),
    )
    out_specs = (P("dom", "grp", None), P("dom", "grp", None), P(), P(), P())
    return jax.shard_map(
        on_device, mesh=mesh, in_specs=in_specs, out_specs=out_specs, check_vma=False
    )
```

profile of v0, /device:TPU:1, one launch (start us, length us, event | category | flops | bytes accessed | tf_op | source)
XLA Modules:
  0.0 449.9 jit_solution(17698190659135924517)
XLA Ops:
  9.0 1.6 gather_fusion
  10.6 1.7 select_select_fusion
  12.3 17.8 %all-to-all-start = ((bf16[16,2,128,256]{3,2,1,0:T(8,128)(2,1)}), bf16[16,2,128,256]{3,2,1,0:T(8,128)(2,1)S(1)}, u32[]{:S(2)}, u32[]{:S(2)}) async-start(bf16[16,2,128,256]{3,2,1,0:T(8,128)(2,1)} %select_select_fusion), calls=%async_computation | async-start | bytes 4194304 | tf_op jit(solution)/shard_map/all_to_all | solution.py:25
  30.1 1.3 collective-permute-start
  31.4 1.3 collective-permute-start.1
  34.1 2.7 collective-permute-done.1
  36.8 42.3 %all-to-all-done = bf16[16,2,128,256]{3,2,1,0:T(8,128)(2,1)S(1)} async-done(((bf16[16,2,128,256]{3,2,1,0:T(8,128)(2,1)}), bf16[16,2,128,256]{3,2,1,0:T(8,128)(2,1)S(1)}, u32[]{:S(2)}, u32[]{:S(2)}) %all-to-all-start) | async-done | bytes 2097184 | tf_op jit(solution)/shard_map/all_to_all | solution.py:25
  79.1 1.3 copy-done.2
  80.4 1.8 pad_maximum_fusion
  82.2 2.5 gather_fusion.1
  84.7 3.2 fusion
  89.5 4.1 fusion.7
  93.7 2.9 broadcast_in_dim.74
  96.6 15.0 %scatter_fusion = f32[38,128,256]{2,1,0:T(8,128)} fusion(f32[38,128,256]{2,1,0:T(8,128)} %broadcast_in_dim.74, s32[48]{0:T(128)S(1)} %fusion.24, f32[48,128,256]{2,1,0:T(8,128)} %bitcast.100), kind=kCustom, calls=%fused_computation.2 | custom fusion | flops 1572864 | bytes 18874560 | tf_op jit(solution)/shard_map/scatter-add | solution.py:88
  111.5 2.7 convert.12
  114.3 1.5 slice.86
  115.7 5.1 %all-to-all-start.1 = ((bf16[16,2,128,256]{3,2,1,0:T(8,128)(2,1)}), bf16[16,2,128,256]{3,2,1,0:T(8,128)(2,1)}, u32[]{:S(2)}, u32[]{:S(2)}) async-start(bf16[16,2,128,256]{3,2,1,0:T(8,128)(2,1)} %bitcast.102), calls=%async_computation.1 | async-start | bytes 4194304 | tf_op jit(solution)/shard_map/all_to_all | solution.py:29
  124.5 1.3 collective-permute-start.2
  125.8 1.3 collective-permute-start.3
  127.1 153.5 %psum.23 = f32[256]{0:T(256)S(1)} all-reduce(f32[256]{0:T(256)S(1)} %get-tuple-element.41), channel_id=1, replica_groups=mesh['dom'=16,'grp'=64] {'dom','grp'}, use_global_device_ids=true, to_apply=%region_4.5 | all-reduce | flops 256 | bytes 2048 | tf_op jit(solution)/shard_map/psum | solution.py:80
  281.1 150.2 %all-reduce.3.cloned.1.call-done = (f32[256,256]{0,1:T(8,128)}, f32[256,256]{0,1:T(8,128)}) async-done(((f32[256,256]{0,1:T(8,128)}, f32[256,256]{0,1:T(8,128)}), (f32[256,256]{0,1:T(8,128)}, f32[256,256]{0,1:T(8,128)})) %all-reduce.3.cloned.1.call-update) | async-done | bytes 524304 | tf_op jit(solution)/shard_map/psum | solution.py:80
  435.0 3.0 fusion.8
  438.3 1.8 scatter-add.18
  440.3 1.8 scatter-add.19
  (66 shorter events, 13.8 us)
Async XLA Ops:
  7.2 80.9 %copy-start = (bf16[256,256]{1,0:T(8,128)(2,1)S(1)}, bf16[256,256]{1,0:T(8,128)(2,1)}, u32[]{:S(2)}) copy-start(bf16[256,256]{1,0:T(8,128)(2,1)} %param.21) | copy-start | bytes 393220
  12.3 17.8 %copy-start.1 = (bf16[1,512,256]{2,1,0:T(8,128)(2,1)S(1)}, bf16[1,512,256]{2,1,0:T(8,128)(2,1)}, u32[]{:S(2)}) copy-start(bf16[1,512,256]{2,1,0:T(8,128)(2,1)} %param.14) | copy-start | bytes 786436
  12.3 20.5 %copy-start.6 = (s32[1,1,4,12]{3,2,1,0:T(4,128)S(1)}, s32[1,1,4,12]{3,2,1,0:T(4,128)}, u32[]{:S(2)}) copy-start(s32[1,1,4,12]{3,2,1,0:T(4,128)} %param.17) | copy-start | bytes 580
  12.3 20.6 %copy-start.8 = (s32[1,512]{1,0:T(1,128)S(1)}, s32[1,512]{1,0:T(1,128)}, u32[]{:S(2)}) copy-start(s32[1,512]{1,0:T(1,128)} %param.19) | copy-start | bytes 6148
  12.3 20.6 %copy-start.9 = (s32[1,1,4]{2,1,0:T(1,128)S(1)}, s32[1,1,4]{2,1,0:T(1,128)}, u32[]{:S(2)}) copy-start(s32[1,1,4]{2,1,0:T(1,128)} %param.16) | copy-start | bytes 52
  12.3 20.7 %copy-start.4 = (bf16[256,256]{1,0:T(8,128)(2,1)S(1)}, bf16[256,256]{1,0:T(8,128)(2,1)}, u32[]{:S(2)}) copy-start(bf16[256,256]{1,0:T(8,128)(2,1)} %param.20) | copy-start | bytes 393220
  12.3 66.8 %all-to-all-start = ((bf16[16,2,128,256]{3,2,1,0:T(8,128)(2,1)}), bf16[16,2,128,256]{3,2,1,0:T(8,128)(2,1)S(1)}, u32[]{:S(2)}, u32[]{:S(2)}) async-start(bf16[16,2,128,256]{3,2,1,0:T(8,128)(2,1)} %select_select_fusion), calls=%async_computation | async-start | bytes 4194304 | tf_op jit(solution)/shard_map/all_to_all | solution.py:25
  30.1 3.9 collective-permute-start
  31.4 5.4 %collective-permute-start.1 = (bf16[128,256]{1,0:T(8,128)(2,1)S(1)}, bf16[128,256]{1,0:T(8,128)(2,1)S(1)}, u32[]{:S(2)}, u32[]{:S(2)}) collective-permute-start(bf16[128,256]{1,0:T(8,128)(2,1)S(1)} %get-tuple-element.47), channel_id=1, source_target_pairs={{1,0},{2,1},{3,2},{4,3},{5,4},{6,5},{7,6},{8,7},{9,8},{10,9},{11,1... | collective-permute-start | bytes 196616 | tf_op jit(solution)/shard_map/ppermute | solution.py:19
  79.1 1.3 copy-start.2
  84.7 3.3 copy-start.5
  84.7 3.3 copy-start.10
  84.7 3.3 copy-start.11
  88.1 1.4 copy-start.3
  115.7 5.2 %copy-start.7 = (s32[1,1,16,2]{2,3,1,0:T(2,128)S(1)}, s32[1,1,16,2]{2,3,1,0:T(2,128)}, u32[]{:S(2)}) copy-start(s32[1,1,16,2]{2,3,1,0:T(2,128)} %param.15) | copy-start | bytes 388
  115.7 319.2 %all-to-all-start.1 = ((bf16[16,2,128,256]{3,2,1,0:T(8,128)(2,1)}), bf16[16,2,128,256]{3,2,1,0:T(8,128)(2,1)}, u32[]{:S(2)}, u32[]{:S(2)}) async-start(bf16[16,2,128,256]{3,2,1,0:T(8,128)(2,1)} %bitcast.102), calls=%async_computation.1 | async-start | bytes 4194304 | tf_op jit(solution)/shard_map/all_to_all | solution.py:29
  120.9 310.5 %all-reduce.3.cloned.1.call-start = ((), (), s32[]{:S(2)}) async-start(), calls=%async_computation.2 | async-start | bytes 1048576 | tf_op jit(solution)/shard_map/psum | solution.py:80
  124.5 313.7 %collective-permute-start.2 = (bf16[128,256]{1,0:T(8,128)(2,1)S(1)}, bf16[128,256]{1,0:T(8,128)(2,1)S(1)}, u32[]{:S(2)}, u32[]{:S(2)}) collective-permute-start(bf16[128,256]{1,0:T(8,128)(2,1)S(1)} %get-tuple-element.44), channel_id=1, source_target_pairs={{0,1},{1,2},{2,3},{3,4},{4,5},{5,6},{6,7},{7,8},{8,9},{9,10},{10,1... | collective-permute-start | bytes 196616 | tf_op jit(solution)/shard_map/ppermute | solution.py:16
  125.8 155.3 %collective-permute-start.3 = (bf16[128,256]{1,0:T(8,128)(2,1)S(1)}, bf16[128,256]{1,0:T(8,128)(2,1)S(1)}, u32[]{:S(2)}, u32[]{:S(2)}) collective-permute-start(bf16[128,256]{1,0:T(8,128)(2,1)S(1)} %get-tuple-element.43), channel_id=1, source_target_pairs={{1,0},{2,1},{3,2},{4,3},{5,4},{6,5},{7,6},{8,7},{9,8},{10,9},{11,1... | collective-permute-start | bytes 196616 | tf_op jit(solution)/shard_map/ppermute | solution.py:19
Sparse Core Ops, SparseCore 0:
  127.2 304.0 all-reduce.2
where the time goes:
time: 451 us; the launch traced here: 450 us
  waiting for transfers between devices  195 us (43%)
  blocking collectives  153 us (34%)
  starting transfers between devices  28.1 us (6%)
  other arithmetic  26.7 us (6%)
  local copies, waits for them, and re-layouts  17.1 us (4%)
  matrix products  15 us (3%)
  between operations  14.3 us (3%)
    psum x1, blocking collectives, on_device(): weight_sums = lax.psum((grad_self, grad_nbr, grad_bias), ('dom', 'grp'))  153 us
    psum x1, waiting for transfers between devices, on_device(): weight_sums = lax.psum((grad_self, grad_nbr, grad_bias), ('dom', 'grp'))  150 us
    all_to_all x1, waiting for transfers between devices, send_blocks(): lax.all_to_all(bucket, 'dom', split_axis=0, concat_axis=0, tiled=True)  42.3 us
    all_to_all x1, starting transfers between devices, send_blocks(): lax.all_to_all(bucket, 'dom', split_axis=0, concat_axis=0, tiled=True)  17.8 us
    scatter-add x1, other arithmetic, on_device(): table_grad = jnp.zeros((table_size, BLK, width), jnp.float32).at[sources....  15 us
  transfers between devices with their start and end apart: 7, of which 3 were waited for; matrix products, arithmetic and copies ran while one was open for 3% of the time, Pallas kernels for 0%

commit v1 on v0

v1 whole, which is shorter than its diff:
```python
import functools
import math

import jax
import jax.numpy as jnp
from jax import lax
from jax.experimental import pallas as pl
from jax.experimental.pallas import tpu as pltpu
from jax.sharding import PartitionSpec as P

BLK = 128
F32 = jnp.float32
BF16 = jnp.bfloat16
ROWS_T = (((0,), (0,)), ((), ()))
COLS_T = (((1,), (1,)), ((), ()))


def dot(a, b, dims=(((1,), (0,)), ((), ()))):
    return lax.dot_general(a, b, dims, preferred_element_type=F32)


def block(t):
    return pl.ds(pl.multiple_of(t * BLK, BLK), BLK)


def layer_kernel(
    blocks_n,
    links_n,
    slots_n,
    recv_ref,
    count_ref,
    index_ref,
    gathered_ref,
    below_ref,
    above_ref,
    rows_ref,
    tiles_ref,
    degree_ref,
    w_self_ref,
    w_nbr_ref,
    bias_ref,
    cot_ref,
    hidden_ref,
    base_ref,
    rims_ref,
    sends_ref,
    weights_ref,
    table,
    grads,
    sems,
):
    rows_n, width = rows_ref.shape
    halo = blocks_n + 2
    table_n = halo + slots_n
    copies = [
        pltpu.make_async_copy(below_ref, table.at[pl.ds(blocks_n * BLK, BLK)], sems.at[0]),
        pltpu.make_async_copy(above_ref, table.at[pl.ds((blocks_n + 1) * BLK, BLK)], sems.at[1]),
    ]
    peers_n, per_peer = recv_ref.shape
    for slot in range(slots_n):
        peer = slot // per_peer
        source = peer * blocks_n + jnp.maximum(recv_ref[peer, slot % per_peer], 0)
        copies.append(
            pltpu.make_async_copy(
                gathered_ref.at[block(source)],
                table.at[pl.ds((halo + slot) * BLK, BLK)],
                sems.at[2 + slot],
            )
        )
    for copy in copies:
        copy.start()

    rows = rows_ref[...]
    table[pl.ds(0, rows_n)] = rows
    table[pl.ds(table_n * BLK, BLK)] = jnp.zeros((BLK, width), BF16)
    grads[...] = jnp.zeros_like(grads)
    self_act = dot(rows, w_self_ref[...])
    spreads = []
    for b in range(blocks_n):
        line = degree_ref[pl.ds(b, 1), :].astype(F32)
        column = jnp.transpose(jnp.broadcast_to(line, (BLK, BLK)))
        spreads.append(jnp.concatenate([column] * (width // BLK), axis=1))
    entries = []
    owners = []
    for b in range(blocks_n):
        for k in range(links_n):
            entry = index_ref[b, k]
            slot = jnp.maximum(entry - halo, 0)
            peer = slot // per_peer
            owner = recv_ref[peer, slot % per_peer]
            is_slot = entry >= halo
            dead = (k >= count_ref[b]) | (is_slot & (owner < 0))
            entries.append(jnp.where(dead, table_n, entry))
            owner = jnp.where(is_slot, halo + peer * blocks_n + owner, entry)
            owners.append(jnp.where(dead, halo + peers_n * blocks_n, owner))

    for copy in copies:
        copy.wait()

    means = []
    for b in range(blocks_n):
        total = None
        for k in range(0, links_n, 2):
            at = b * links_n + k
            left = jnp.concatenate([tiles_ref[at], tiles_ref[at + 1]], axis=1)
            right = jnp.concatenate([table[block(entries[at])], table[block(entries[at + 1])]], axis=0)
            term = dot(left, right)
            total = term if total is None else total + term
        means.append((total / spreads[b]).astype(BF16))
    mean_rows = jnp.concatenate(means, axis=0)
    pre_act = self_act + dot(mean_rows, w_nbr_ref[...]) + bias_ref[...]
    gate = jax.nn.sigmoid(pre_act)
    hidden_ref[...] = (pre_act * gate).astype(BF16)
    slope = gate * (1.0 + pre_act * (1.0 - gate))
    pre_grad = (cot_ref[...].astype(F32) * slope).astype(BF16)
    parts, each = weights_ref.shape[:2]
    grad_self = dot(rows, pre_grad, ROWS_T)
    grad_nbr = dot(mean_rows, pre_grad, ROWS_T)
    half = parts // 2
    weights_ref[pl.ds(0, half), :, pl.ds(0, width)] = grad_self.reshape(half, each, width)
    weights_ref[pl.ds(half, half), :, pl.ds(0, width)] = grad_nbr.reshape(half, each, width)
    bias_sum = jnp.sum(pre_grad.astype(F32), axis=0, keepdims=True)
    lines = [bias_sum[:, i * BLK : (i + 1) * BLK] for i in range(width // BLK)]
    lines.append(jnp.zeros((each - len(lines), BLK), F32))
    bias_tile = jnp.concatenate(lines, axis=0)
    weights_ref[:, :, pl.ds(width, BLK)] = jnp.broadcast_to(bias_tile[None], (parts, each, BLK))

    mean_grad = dot(pre_grad, w_nbr_ref[...], COLS_T)
    for b in range(blocks_n):
        sum_grad = (mean_grad[b * BLK : (b + 1) * BLK] / spreads[b]).astype(BF16)
        for k in range(links_n):
            at = b * links_n + k
            where = block(owners[at])
            grads[where] += dot(tiles_ref[at], sum_grad, ROWS_T)
    base_ref[...] = dot(pre_grad, w_self_ref[...], COLS_T) + grads[pl.ds(0, rows_n)]
    rims_ref[...] = grads[pl.ds(rows_n, 2 * BLK)].astype(BF16)
    for p in range(peers_n):
        sends_ref[pl.ds(p * rows_n, rows_n)] = grads[pl.ds(halo * BLK + p * rows_n, rows_n)].astype(BF16)


def layer(recv, count, index, gathered, below, above, rows, tiles, degree, w_self, w_nbr, bias, cot, parts):
    blocks_n, links_n = index.shape
    slots_n = recv.size
    rows_n, width = rows.shape
    table_n = blocks_n + 2 + slots_n
    owners_n = blocks_n + 2 + recv.shape[0] * blocks_n
    smem = pl.BlockSpec(memory_space=pltpu.SMEM)
    hbm = pl.BlockSpec(memory_space=pl.ANY)
    vmem = pl.BlockSpec(memory_space=pltpu.VMEM)
    each = 2 * width // parts
    return pl.pallas_call(
        functools.partial(layer_kernel, blocks_n, links_n, slots_n),
        out_shape=(
            jax.ShapeDtypeStruct((rows_n, width), BF16),
            jax.ShapeDtypeStruct((rows_n, width), F32),
            jax.ShapeDtypeStruct((2 * BLK, width), BF16),
            jax.ShapeDtypeStruct((recv.shape[0] * rows_n, width), BF16),
            jax.ShapeDtypeStruct((parts, each, width + BLK), F32),
        ),
        in_specs=[smem] * 3 + [hbm] * 3 + [vmem] * 7,
        out_specs=(vmem,) * 5,
        scratch_shapes=[
            pltpu.VMEM(((table_n + 1) * BLK, width), BF16),
            pltpu.VMEM(((owners_n + 1) * BLK, width), F32),
            pltpu.SemaphoreType.DMA((2 + slots_n,)),
        ],
        compiler_params=pltpu.CompilerParams(vmem_limit_bytes=48 * 2**20),
        cost_estimate=pl.CostEstimate(
            flops=1_300_000_000, bytes_accessed=12_000_000, transcendentals=rows_n * width
        ),
        name="layer",
    )(recv, count, index, gathered, below, above, rows, tiles, degree, w_self, w_nbr, bias, cot)


def shift(block_rows, axis, step):
    count = lax.axis_size(axis)
    pairs = [(i, i + step) for i in range(count) if 0 <= i + step < count]
    return lax.ppermute(block_rows, axis, pairs)


def swap(array, axis):
    return lax.all_to_all(array, axis, split_axis=0, concat_axis=0, tiled=True)


def on_device(
    features, send_list, nbr_count, nbr_index, tiles, degree, w_self, w_nbr, bias, cotangent
):
    rows = features[0]
    rows_n, width = rows.shape
    blocks_n = rows_n // BLK
    links_n = nbr_index.shape[-1]
    groups = lax.axis_size("grp")
    doms = lax.axis_size("dom")

    with jax.named_scope("gather_rows"):
        gathered = lax.all_gather(rows, "dom", tiled=True)
    with jax.named_scope("send_lists"):
        recv = swap(send_list[0, 0], "dom")
    with jax.named_scope("rims"):
        below = shift(rows[rows_n - BLK :], "grp", 1)
        above = shift(rows[:BLK], "grp", -1)

    hidden, base, rims, sends, partial = layer(
        recv,
        nbr_count[0, 0],
        nbr_index[0, 0],
        gathered,
        below,
        above,
        rows,
        tiles.reshape(blocks_n * links_n, BLK, BLK),
        degree.reshape(blocks_n, BLK),
        w_self,
        w_nbr,
        bias.reshape(1, width),
        cotangent[0],
        groups,
    )

    with jax.named_scope("return_slots"):
        returned = lax.psum_scatter(sends, "dom", tiled=True)
    with jax.named_scope("return_rims"):
        from_above = shift(rims[:BLK], "grp", -1)
        from_below = shift(rims[BLK:], "grp", 1)
    with jax.named_scope("weight_sums"):
        chunk = jnp.sum(swap(partial, "grp"), axis=0)
        chunk = jnp.sum(lax.all_gather(chunk, "dom"), axis=0)
        chunk = chunk * (1.0 / math.sqrt(rows_n * doms * groups))
        bias_grad = chunk[: width // BLK, width:].reshape(width)
        whole = swap(jnp.broadcast_to(chunk[None, :, :width], (groups,) + chunk[:, :width].shape), "grp")
        whole = whole.reshape(2 * width, width)
    edges = jnp.concatenate(
        [from_below, jnp.zeros((rows_n - 2 * BLK, width), BF16), from_above], axis=0
    )
    feat_grad = base + returned.astype(F32) + edges.astype(F32)
    return hidden[None], feat_grad[None], whole[:width], whole[width:], bias_grad


def solution(mesh):
    in_specs = (
        P("dom", "grp", None),
        P("dom", "grp", None, None),
        P("dom", "grp", None),
        P("dom", "grp", None, None),
        P("dom", "grp", None, None, None),
        P("dom", "grp"),
        P(),
        P(),
        P(),
        P("dom", "grp", None),
    )
    out_specs = (P("dom", "grp", None), P("dom", "grp", None), P(), P(), P())
    return jax.shard_map(
        on_device, mesh=mesh, in_specs=in_specs, out_specs=out_specs, check_vma=False
    )
```

time: 451 us -> 177 us (0.39)
  waiting for transfers between devices: 195 us -> 47.8 us
  blocking collectives: 153 us -> 74.1 us
  other arithmetic: 26.7 us -> 1.99 us
  matrix products: 15 us -> 0 us
  starting transfers between devices: 28.1 us -> 17.7 us
  Pallas kernels: 0 us -> 7.45 us
  local copies, waits for them, and re-layouts: 17.1 us -> 11.7 us
    psum x1 -> x0, blocking collectives: 153 us -> none  [on_device(): weight_sums = lax.psum((grad_self, grad_nbr, grad_bias), ('dom', 'grp'))]
    psum x1 -> x0, waiting for transfers between devices: 150 us -> none  [on_device(): weight_sums = lax.psum((grad_self, grad_nbr, grad_bias), ('dom', 'grp'))]
    all_to_all x0 -> x2, blocking collectives: none -> 54.6 us  [swap(): return lax.all_to_all(array, axis, split_axis=0, concat_axis=0, tiled=True)]
    all_gather x0 -> x1, waiting for transfers between devices: none -> 34.6 us  [on_device(): gathered = lax.all_gather(rows, 'dom', tiled=True)]
    all_to_all x2 -> x1, waiting for transfers between devices: 42.3 us -> 12.5 us  [swap(): return lax.all_to_all(array, axis, split_axis=0, concat_axis=0, tiled=True)]
    all_gather x0 -> x1, blocking collectives: none -> 19.5 us  [on_device(): chunk = jnp.sum(lax.all_gather(chunk, 'dom'), axis=0)]
    all_to_all x2 -> x1, starting transfers between devices: 22.9 us -> 6.35 us  [swap(): return lax.all_to_all(array, axis, split_axis=0, concat_axis=0, tiled=True)]
    scatter-add x1 -> x0, other arithmetic: 15 us -> none  [on_device(): table_grad = jnp.zeros((table_size, BLK, width), jnp.float32).at[sources....]
  transfers between devices with their start and end apart: 7 -> 7, of which waited for: 3 -> 2; matrix products, arithmetic and copies ran while one was open for 3% -> 2% of each run, Pallas kernels for 0% -> 0%
where the time goes in v1:
time: 177 us; the launch traced here: 175 us
  blocking collectives  74.1 us (42%)
  waiting for transfers between devices  47.8 us (27%)
  starting transfers between devices  17.7 us (10%)
  between operations  14.2 us (8%)
  local copies, waits for them, and re-layouts  11.7 us (7%)
  Pallas kernels  7.45 us (4%)
  other arithmetic  1.99 us (1%)
    all_to_all x2, blocking collectives, swap(): return lax.all_to_all(array, axis, split_axis=0, concat_axis=0, tiled=True)  54.6 us
    all_gather x1, waiting for transfers between devices, on_device(): gathered = lax.all_gather(rows, 'dom', tiled=True)  34.6 us
    all_gather x1, blocking collectives, on_device(): chunk = jnp.sum(lax.all_gather(chunk, 'dom'), axis=0)  19.5 us
    all_to_all x1, waiting for transfers between devices, swap(): return lax.all_to_all(array, axis, split_axis=0, concat_axis=0, tiled=True)  12.5 us
    ppermute x4, starting transfers between devices, shift(): return lax.ppermute(block_rows, axis, pairs)  11.2 us
    unnamed x18, local copies, waits for them, and re-layouts  7.81 us
    pallas_call x1, Pallas kernels, layer(): pl.pallas_call(functools.partial(layer_kernel, blocks_n, links_n, slots_n...  7.45 us
    all_to_all x1, starting transfers between devices, swap(): return lax.all_to_all(array, axis, split_axis=0, concat_axis=0, tiled=True)  6.35 us
  transfers between devices with their start and end apart: 7, of which 2 were waited for; matrix products, arithmetic and copies ran while one was open for 2% of the time, Pallas kernels for 0%

profile of v1, /device:TPU:1, one launch (start us, length us, event | category | flops | bytes accessed | tf_op | source)
XLA Modules:
  0.0 174.9 jit_solution(2751575093268534235)
XLA Ops:
  7.2 0.7 all-gather.4.cloned.1.call-update
  7.9 0.9 slice_bitcast_fusion.2
  8.8 5.7 %collective-permute-start = (bf16[128,256]{1,0:T(8,128)(2,1)S(1)}, bf16[128,256]{1,0:T(8,128)(2,1)S(1)}, u32[]{:S(2)}, u32[]{:S(2)}) collective-permute-start(bf16[128,256]{1,0:T(8,128)(2,1)S(1)} %get-tuple-element.18), channel_id=1, source_target_pairs={{0,1},{1,2},{2,3},{3,4},{4,5},{5,6},{6,7},{7,8},{8,9},{9,10},{10,1... | collective-permute-start | bytes 196616 | tf_op jit(solution)/shard_map/rims/ppermute | solution.py:178
  14.6 1.3 collective-permute-start.1
  15.9 0.8 copy.19
  16.6 19.1 %all_to_all.21 = s32[16,1,2]{2,1,0:T(1,128)S(1)} all-to-all(s32[16,1,2]{2,1,0:T(1,128)S(1)} %copy.19), channel_id=1, replica_groups=mesh['dom'=16,'grp'=64] {'dom'}, dimensions={0} | all-to-all | bytes 256 | tf_op jit(solution)/shard_map/send_lists/all_to_all | solution.py:182
  35.8 34.6 %all-gather.4.cloned.1.call-done = bf16[1,8192,256]{2,1,0:T(8,128)(2,1)} async-done(((bf16[1,512,256]{2,1,0:T(8,128)(2,1)}), bf16[1,8192,256]{2,1,0:T(8,128)(2,1)}) %all-gather.4.cloned.1.call-update) | async-done | bytes 4194320 | tf_op jit(solution)/shard_map/gather_rows/all_gather | solution.py:196
  70.4 0.9 copy-done
  71.4 1.4 copy-done.1
  72.8 0.9 copy-done.2
  73.7 0.9 copy-done.3
  74.6 0.9 copy-done.4
  75.6 0.7 copy-done.5
  76.2 0.7 copy-done.6
  78.2 7.5 %layer.1 = (bf16[512,256]{1,0:T(8,128)(2,1)}, f32[512,256]{1,0:T(8,128)S(1)}, bf16[256,256]{1,0:T(8,128)(2,1)S(1)}, bf16[8192,256]{1,0:T(8,128)(2,1)}, f32[64,8,384]{2,1,0:T(8,128)S(1)}) custom-call(s32[16,2]{1,0:T(8,128)S(1)} %bitcast.28, s32[4]{0:T(128)S(1)} %bitcast.32, s32[4,12]{1,0:T(4,128)S(1)} %bitcast.29, bf16[8192,256]{1,0:T(8,128)(2,1)} %bitcast.33, ...), custom_call_target="tpu_custom_call" | custom-call | flops 1300000000 | bytes 12000000 | tf_op jit(solution)/shard_map/layer/pallas_call | solution.py:151
  85.7 35.4 %all_to_all.22 = f32[64,8,384]{2,1,0:T(8,128)S(1)} all-to-all(f32[64,8,384]{2,1,0:T(8,128)S(1)} %get-tuple-element.14), channel_id=1, replica_groups=mesh['dom'=16,'grp'=64] {'grp'}, dimensions={0} | all-to-all | bytes 1572864 | tf_op jit(solution)/shard_map/weight_sums/all_to_all | solution.py:182
  121.2 19.5 %all-gather.1 = f32[128,384]{1,0:T(8,128)S(1)} all-gather(f32[8,384]{1,0:T(8,128)S(1)} %reduce_sum.18), channel_id=3, replica_groups=mesh['dom'=16,'grp'=64] {'dom'}, dimensions={0}, use_global_device_ids=true | all-gather | bytes 208896 | tf_op jit(solution)/shard_map/weight_sums/all_gather | solution.py:227
  140.8 0.8 broadcast_in_dim.18
  141.6 6.4 %all-to-all-start.2 = ((f32[64,8,256]{2,1,0:T(8,128)}), f32[64,8,256]{2,1,0:T(8,128)S(1)}, u32[]{:S(2)}, u32[]{:S(2)}) async-start(f32[64,8,256]{2,1,0:T(8,128)} %broadcast_in_dim.18), calls=%async_computation.3 | async-start | bytes 1048576 | tf_op jit(solution)/shard_map/weight_sums/all_to_all | solution.py:182
  148.0 2.9 %collective-permute-start.2 = (bf16[128,256]{1,0:T(8,128)(2,1)S(1)}, bf16[128,256]{1,0:T(8,128)(2,1)S(1)}, u32[]{:S(2)}, u32[]{:S(2)}) collective-permute-start(bf16[128,256]{1,0:T(8,128)(2,1)S(1)} %get-tuple-element.19), channel_id=1, source_target_pairs={{0,1},{1,2},{2,3},{3,4},{4,5},{5,6},{6,7},{7,8},{8,9},{9,10},{10,1... | collective-permute-start | bytes 196616 | tf_op jit(solution)/shard_map/return_rims/ppermute | solution.py:178
  151.0 1.3 collective-permute-start.3
  152.8 12.5 %all-to-all-done.2 = f32[64,8,256]{2,1,0:T(8,128)S(1)} async-done(((f32[64,8,256]{2,1,0:T(8,128)}), f32[64,8,256]{2,1,0:T(8,128)S(1)}, u32[]{:S(2)}, u32[]{:S(2)}) %all-to-all-start.2) | async-done | bytes 524320 | tf_op jit(solution)/shard_map/weight_sums/all_to_all | solution.py:182
  165.3 0.8 slice_bitcast_fusion
  166.2 1.9 %add_bitcast_fusion = f32[1,512,256]{2,1,0:T(8,128)} fusion(f32[512,256]{1,0:T(8,128)S(1)} %get-tuple-element.11, bf16[512,256]{1,0:T(8,128)(2,1)} %reduce-scatter.2.cloned.1.call-done, bf16[128,256]{1,0:T(8,128)(2,1)S(1)} %collective-permute-done.3, bf16[128,256]{1,0:T(8,128)(2,1)S(1)} %collective-permute-done.2, bf16[512]{0:T(512)(128)(2,1)S(1)} %pad.1.clone), kind=kLoop, calls=%fused_computation | loop fusion | flops 1179648 | bytes 1442816 | tf_op jit(solution)/shard_map/broadcast_in_dim | solution.py:236
  (27 shorter events, 2.2 us)
Async XLA Ops:
  7.2 63.3 %all-gather.4.cloned.1.call-start = ((), (), s32[]{:S(2)}) async-start(), calls=%async_computation.5 | async-start | bytes 4456448 | tf_op jit(solution)/shard_map/gather_rows/all_gather | solution.py:196
  7.9 158.2 %reduce-scatter.2.cloned.1.call-start = ((), (), s32[]{:S(2)}) async-start(), calls=%async_computation.4 | async-start | bytes 4456448 | tf_op jit(solution)/shard_map/return_slots/reduce_scatter | solution.py:221
  8.8 27.0 %collective-permute-start = (bf16[128,256]{1,0:T(8,128)(2,1)S(1)}, bf16[128,256]{1,0:T(8,128)(2,1)S(1)}, u32[]{:S(2)}, u32[]{:S(2)}) collective-permute-start(bf16[128,256]{1,0:T(8,128)(2,1)S(1)} %get-tuple-element.18), channel_id=1, source_target_pairs={{0,1},{1,2},{2,3},{3,4},{4,5},{5,6},{6,7},{7,8},{8,9},{9,10},{10,1... | collective-permute-start | bytes 196616 | tf_op jit(solution)/shard_map/rims/ppermute | solution.py:178
  14.6 21.2 %collective-permute-start.1 = (bf16[128,256]{1,0:T(8,128)(2,1)S(1)}, bf16[128,256]{1,0:T(8,128)(2,1)S(1)}, u32[]{:S(2)}, u32[]{:S(2)}) collective-permute-start(bf16[128,256]{1,0:T(8,128)(2,1)S(1)} %get-tuple-element.17), channel_id=1, source_target_pairs={{1,0},{2,1},{3,2},{4,3},{5,4},{6,5},{7,6},{8,7},{9,8},{10,9},{11,1... | collective-permute-start | bytes 196616 | tf_op jit(solution)/shard_map/rims/ppermute | solution.py:178
  70.4 0.9 copy-start
  71.4 1.4 copy-start.1
  72.8 0.9 copy-start.2
  73.7 0.9 copy-start.3
  74.6 0.9 copy-start.4
  75.5 0.7 copy-start.5
  76.2 0.7 copy-start.6
  76.9 0.7 copy-start.7
  77.6 0.7 copy-start.8
  141.6 23.7 %all-to-all-start.2 = ((f32[64,8,256]{2,1,0:T(8,128)}), f32[64,8,256]{2,1,0:T(8,128)S(1)}, u32[]{:S(2)}, u32[]{:S(2)}) async-start(f32[64,8,256]{2,1,0:T(8,128)} %broadcast_in_dim.18), calls=%async_computation.3 | async-start | bytes 1048576 | tf_op jit(solution)/shard_map/weight_sums/all_to_all | solution.py:182
  148.0 18.1 %collective-permute-start.2 = (bf16[128,256]{1,0:T(8,128)(2,1)S(1)}, bf16[128,256]{1,0:T(8,128)(2,1)S(1)}, u32[]{:S(2)}, u32[]{:S(2)}) collective-permute-start(bf16[128,256]{1,0:T(8,128)(2,1)S(1)} %get-tuple-element.19), channel_id=1, source_target_pairs={{0,1},{1,2},{2,3},{3,4},{4,5},{5,6},{6,7},{7,8},{8,9},{9,10},{10,1... | collective-permute-start | bytes 196616 | tf_op jit(solution)/shard_map/return_rims/ppermute | solution.py:178
  151.0 15.2 %collective-permute-start.3 = (bf16[128,256]{1,0:T(8,128)(2,1)S(1)}, bf16[128,256]{1,0:T(8,128)(2,1)S(1)}, u32[]{:S(2)}, u32[]{:S(2)}) collective-permute-start(bf16[128,256]{1,0:T(8,128)(2,1)S(1)} %get-tuple-element.20), channel_id=1, source_target_pairs={{1,0},{2,1},{3,2},{4,3},{5,4},{6,5},{7,6},{8,7},{9,8},{10,9},{11,1... | collective-permute-start | bytes 196616 | tf_op jit(solution)/shard_map/return_rims/ppermute | solution.py:178
Sparse Core Ops, SparseCore 0:
  10.7 59.6 all-gather.3
  85.9 67.1 reduce-scatter.1

commit v2 on v1

v2 whole, which is shorter than its diff:
```python
import functools
import math

import jax
import jax.numpy as jnp
from jax import lax
from jax.experimental import pallas as pl
from jax.experimental.pallas import tpu as pltpu
from jax.sharding import PartitionSpec as P

BLK = 128
PAD = 16
SCALE = 8192.0
F32 = jnp.float32
BF16 = jnp.bfloat16
ROWS_T = (((0,), (0,)), ((), ()))
COLS_T = (((1,), (1,)), ((), ()))


def dot(a, b, dims=(((1,), (0,)), ((), ()))):
    return lax.dot_general(a, b, dims, preferred_element_type=F32)


def block(t):
    return pl.ds(pl.multiple_of(t * BLK, BLK), BLK)


def layer_kernel(
    blocks_n,
    links_n,
    peers_n,
    per_peer,
    plan_ref,
    gathered_ref,
    below_ref,
    above_ref,
    rows_hbm,
    tiles_hbm,
    degree_hbm,
    w_self_hbm,
    w_nbr_hbm,
    bias_hbm,
    cot_hbm,
    hidden_ref,
    base_ref,
    rims_ref,
    sends_ref,
    weights_ref,
    tiles_ref,
    degree_ref,
    w_self_ref,
    w_nbr_ref,
    bias_ref,
    cot_ref,
    table,
    grads,
    own_sems,
    tile_sems,
    table_sems,
):
    rows_n, width = cot_ref.shape
    halo = blocks_n + 2
    slots_n = peers_n * per_peer
    table_n = halo + slots_n
    rows_ref = table.at[pl.ds(0, rows_n)]
    own = [
        pltpu.make_async_copy(source, target, own_sems.at[i])
        for i, (source, target) in enumerate(
            (
                (rows_hbm, rows_ref),
                (w_self_hbm, w_self_ref),
                (degree_hbm, degree_ref),
                (bias_hbm, bias_ref),
                (w_nbr_hbm, w_nbr_ref),
                (cot_hbm, cot_ref),
            )
        )
    ]
    tile_copies = [
        pltpu.make_async_copy(
            tiles_hbm.at[pl.ds(b * links_n, links_n)],
            tiles_ref.at[pl.ds(b * links_n, links_n)],
            tile_sems.at[b],
        )
        for b in range(blocks_n)
    ]
    table_copies = [
        pltpu.make_async_copy(below_ref, table.at[pl.ds(blocks_n * BLK, BLK)], table_sems.at[0]),
        pltpu.make_async_copy(above_ref, table.at[pl.ds((blocks_n + 1) * BLK, BLK)], table_sems.at[1]),
    ]
    for slot in range(slots_n):
        source = (slot // per_peer) * (rows_n + PAD) + jnp.maximum(plan_ref[slot], 0) * BLK
        table_copies.append(
            pltpu.make_async_copy(
                gathered_ref.at[pl.ds(pl.multiple_of(source, PAD), BLK)],
                table.at[pl.ds((halo + slot) * BLK, BLK)],
                table_sems.at[2 + slot],
            )
        )
    for copy in own + table_copies + tile_copies:
        copy.start()

    table[pl.ds(table_n * BLK, BLK)] = jnp.zeros((BLK, width), BF16)
    grads[...] = jnp.zeros_like(grads)
    entries = []
    owners = []
    for b in range(blocks_n):
        count = plan_ref[slots_n + b]
        for k in range(links_n):
            entry = plan_ref[slots_n + blocks_n + b * links_n + k]
            is_slot = entry >= halo
            slot = jnp.maximum(entry - halo, 0)
            owner = plan_ref[slot]
            dead = (k >= count) | (is_slot & (owner < 0))
            entries.append(jnp.where(dead, table_n, entry))
            owner = jnp.where(is_slot, halo + (slot // per_peer) * blocks_n + owner, entry)
            owners.append(jnp.where(dead, halo + peers_n * blocks_n, owner))

    for copy in own:
        copy.wait()
    rows = rows_ref[...]
    self_act = dot(rows, w_self_ref[...]) + bias_ref[...]
    spreads = []
    for b in range(blocks_n):
        line = degree_ref[pl.ds(b, 1), :].astype(F32)
        column = jnp.transpose(jnp.broadcast_to(line, (BLK, BLK)))
        spreads.append(jnp.concatenate([column] * (width // BLK), axis=1))
    for copy in table_copies:
        copy.wait()

    means = []
    for b in range(blocks_n):
        tile_copies[b].wait()
        total = None
        for k in range(0, links_n, 2):
            at = b * links_n + k
            left = jnp.concatenate([tiles_ref[at], tiles_ref[at + 1]], axis=1)
            right = jnp.concatenate([table[block(entries[at])], table[block(entries[at + 1])]], axis=0)
            term = dot(left, right)
            total = term if total is None else total + term
        means.append((total / spreads[b]).astype(BF16))
    mean_rows = jnp.concatenate(means, axis=0)
    pre_act = self_act + dot(mean_rows, w_nbr_ref[...])
    gate = jax.nn.sigmoid(pre_act)
    hidden_ref[...] = (pre_act * gate).astype(BF16)
    slope = gate * (1.0 + pre_act * (1.0 - gate))
    pre_grad = (cot_ref[...].astype(F32) * slope).astype(BF16)
    grad_all = jnp.concatenate([dot(rows, pre_grad, ROWS_T), dot(mean_rows, pre_grad, ROWS_T)], axis=0)
    grad_all = grad_all.astype(BF16)
    bias_sum = jnp.sum(pre_grad.astype(F32), axis=0, keepdims=True)
    parts, each = weights_ref.shape[0], weights_ref.shape[1] // 2
    halves = width // BLK
    lines = [bias_sum[:, i * BLK : (i + 1) * BLK] for i in range(halves)]
    lines.append(jnp.zeros((each - halves, BLK), F32))
    bias_tile = jnp.concatenate(lines, axis=0).astype(BF16)
    stride = parts // halves
    for i in range(halves):
        chunk = grad_all[:, i * BLK : (i + 1) * BLK].reshape(stride, each, BLK)
        weights_ref[pl.ds(i * stride, stride), pl.ds(0, each), :] = chunk
    weights_ref[:, pl.ds(each, each), :] = jnp.broadcast_to(bias_tile[None], (parts, each, BLK))

    mean_grad = dot(pre_grad, w_nbr_ref[...], COLS_T)
    for b in range(blocks_n):
        sum_grad = (mean_grad[b * BLK : (b + 1) * BLK] / spreads[b]).astype(BF16)
        for k in range(links_n):
            at = b * links_n + k
            where = block(owners[at])
            grads[where] += dot(tiles_ref[at], sum_grad, ROWS_T)
    base_ref[...] = dot(pre_grad, w_self_ref[...], COLS_T) + grads[pl.ds(0, rows_n)]
    rims_ref[...] = grads[pl.ds(rows_n, 2 * BLK)].astype(BF16)
    for p in range(peers_n):
        sends_ref[pl.ds(p * rows_n, rows_n)] = grads[pl.ds(halo * BLK + p * rows_n, rows_n)].astype(BF16)


def layer(recv, count, index, gathered, below, above, rows, tiles, degree, w_self, w_nbr, bias, cot, parts):
    blocks_n, links_n = index.shape
    peers_n, per_peer = recv.shape
    rows_n, width = rows.shape
    table_n = blocks_n + 2 + recv.size
    owners_n = blocks_n + 2 + peers_n * blocks_n
    plan = jnp.concatenate([recv.reshape(-1), count, index.reshape(-1)])
    smem = pl.BlockSpec(memory_space=pltpu.SMEM)
    hbm = pl.BlockSpec(memory_space=pl.ANY)
    vmem = pl.BlockSpec(memory_space=pltpu.VMEM)
    each = 2 * width * (width // BLK) // parts
    return pl.pallas_call(
        functools.partial(layer_kernel, blocks_n, links_n, peers_n, per_peer),
        out_shape=(
            jax.ShapeDtypeStruct((rows_n, width), BF16),
            jax.ShapeDtypeStruct((rows_n, width), F32),
            jax.ShapeDtypeStruct((2 * BLK, width), BF16),
            jax.ShapeDtypeStruct((peers_n * rows_n, width), BF16),
            jax.ShapeDtypeStruct((parts, 2 * each, BLK), BF16),
        ),
        in_specs=[smem] + [hbm] * 10,
        out_specs=(vmem,) * 5,
        scratch_shapes=[
            pltpu.VMEM(tiles.shape, BF16),
            pltpu.VMEM(degree.shape, degree.dtype),
            pltpu.VMEM(w_self.shape, BF16),
            pltpu.VMEM(w_nbr.shape, BF16),
            pltpu.VMEM(bias.shape, F32),
            pltpu.VMEM(cot.shape, BF16),
            pltpu.VMEM(((table_n + 1) * BLK, width), BF16),
            pltpu.VMEM(((owners_n + 1) * BLK, width), F32),
            pltpu.SemaphoreType.DMA((6,)),
            pltpu.SemaphoreType.DMA((blocks_n,)),
            pltpu.SemaphoreType.DMA((2 + recv.size,)),
        ],
        compiler_params=pltpu.CompilerParams(vmem_limit_bytes=56 * 2**20),
        cost_estimate=pl.CostEstimate(
            flops=1_300_000_000, bytes_accessed=12_000_000, transcendentals=rows_n * width
        ),
        name="layer",
    )(plan, gathered, below, above, rows, tiles, degree, w_self, w_nbr, bias, cot)


def shift(block_rows, axis, step):
    count = lax.axis_size(axis)
    pairs = [(i, i + step) for i in range(count) if 0 <= i + step < count]
    return lax.ppermute(block_rows, axis, pairs)


def swap(array, axis):
    return lax.all_to_all(array, axis, split_axis=0, concat_axis=0, tiled=True)


def on_device(
    features, send_list, nbr_count, nbr_index, tiles, degree, w_self, w_nbr, bias, cotangent
):
    rows = features[0]
    rows_n, width = rows.shape
    blocks_n = rows_n // BLK
    links_n = nbr_index.shape[-1]
    groups = lax.axis_size("grp")
    doms = lax.axis_size("dom")

    with jax.named_scope("gather_rows"):
        lists = jnp.pad(send_list.reshape(1, -1).astype(BF16), ((0, PAD - 1), (0, width - send_list.size)))
        wide = jnp.concatenate([rows, lists], axis=0).astype(F32) * SCALE
        packed = lax.all_gather(wide.astype(jnp.float16), "dom", tiled=True)
        gathered = (packed.astype(F32) * (1.0 / SCALE)).astype(BF16)
        lists = packed.reshape(doms, rows_n + PAD, width)[:, rows_n]
        slots = send_list.shape[-1]
        recv = lax.dynamic_slice_in_dim(lists, lax.axis_index("dom") * slots, slots, axis=1)
        recv = jnp.round(recv.astype(F32) * (1.0 / SCALE)).astype(jnp.int32)
    with jax.named_scope("rims"):
        below = shift(rows[rows_n - BLK :], "grp", 1)
        above = shift(rows[:BLK], "grp", -1)

    hidden, base, rims, sends, partial = layer(
        recv,
        nbr_count[0, 0],
        nbr_index[0, 0],
        gathered,
        below,
        above,
        rows,
        tiles.reshape(blocks_n * links_n, BLK, BLK),
        degree.reshape(blocks_n, BLK),
        w_self,
        w_nbr,
        bias.reshape(1, width),
        cotangent[0],
        groups,
    )

    with jax.named_scope("return_slots"):
        returned = lax.psum_scatter(sends, "dom", tiled=True)
    with jax.named_scope("return_rims"):
        from_above = shift(rims[:BLK], "grp", -1)
        from_below = shift(rims[BLK:], "grp", 1)
    with jax.named_scope("weight_sums"):
        chunk = jnp.sum(swap(partial, "grp").astype(F32), axis=0)
        chunk = jnp.sum(lax.all_gather(chunk, "dom"), axis=0)
        chunk = chunk * (1.0 / math.sqrt(rows_n * doms * groups))
        halves = width // BLK
        each = chunk.shape[0] // 2
        bias_grad = chunk[each : each + halves].reshape(width)
        finished = chunk[:each].astype(BF16)
        whole = swap(jnp.broadcast_to(finished[None], (groups, each, BLK)), "grp")
        whole = whole.reshape(halves, 2 * width, BLK).astype(F32)
        whole = jnp.concatenate([whole[i] for i in range(halves)], axis=1)
    edges = jnp.concatenate(
        [from_below, jnp.zeros((rows_n - 2 * BLK, width), BF16), from_above], axis=0
    )
    feat_grad = base + returned.astype(F32) + edges.astype(F32)
    return hidden[None], feat_grad[None], whole[:width], whole[width:], bias_grad


def solution(mesh):
    in_specs = (
        P("dom", "grp", None),
        P("dom", "grp", None, None),
        P("dom", "grp", None),
        P("dom", "grp", None, None),
        P("dom", "grp", None, None, None),
        P("dom", "grp"),
        P(),
        P(),
        P(),
        P("dom", "grp", None),
    )
    out_specs = (P("dom", "grp", None), P("dom", "grp", None), P(), P(), P())
    return jax.shard_map(
        on_device, mesh=mesh, in_specs=in_specs, out_specs=out_specs, check_vma=False
    )
```

time: 177 us -> 153 us (0.86)
  waiting for transfers between devices: 47.8 us -> 8.55 us
  blocking collectives: 74.1 us -> 91.2 us
  local copies, waits for them, and re-layouts: 11.7 us -> 4.35 us
  other arithmetic: 1.99 us -> 7.7 us
  Pallas kernels: 7.45 us -> 9.25 us
    all_gather x0 -> x1, blocking collectives: none -> 41.7 us  [on_device(): packed = lax.all_gather(wide.astype(jnp.float16), 'dom', tiled=True)]
    all_gather x1 -> x0, waiting for transfers between devices: 34.6 us -> none  [on_device(): gathered = lax.all_gather(rows, 'dom', tiled=True)]
    all_to_all x2 -> x1, blocking collectives: 54.6 us -> 31.6 us  [swap(): return lax.all_to_all(array, axis, split_axis=0, concat_axis=0, tiled=True)]
    unnamed x18 -> x14, local copies, waits for them, and re-layouts: 7.81 us -> 1.64 us
    convert_element_type x0 -> x4, other arithmetic: none -> 4.28 us  [the longest x1 2.57 us: on_device(): gathered = (packed.astype(F32) * (1.0 / SCALE)).astype(BF16)]
    all_to_all x1, waiting for transfers between devices: 12.5 us -> 8.51 us  [swap(): return lax.all_to_all(array, axis, split_axis=0, concat_axis=0, tiled=True)]
    pallas_call x1, Pallas kernels: 7.45 us -> 9.25 us  [layer(): pl.pallas_call(functools.partial(layer_kernel, blocks_n, links_n, peers_n...]
  transfers between devices with their start and end apart: 7 -> 6, of which waited for: 2 -> 1; matrix products, arithmetic and copies ran while one was open for 2% -> 5% of each run, Pallas kernels for 0% -> 0%
where the time goes in v2:
time: 153 us; the launch traced here: 152 us
  blocking collectives  91.2 us (60%)
  starting transfers between devices  16.9 us (11%)
  between operations  14.2 us (9%)
  Pallas kernels  9.25 us (6%)
  waiting for transfers between devices  8.55 us (6%)
  other arithmetic  7.7 us (5%)
  local copies, waits for them, and re-layouts  4.35 us (3%)
    all_gather x1, blocking collectives, on_device(): packed = lax.all_gather(wide.astype(jnp.float16), 'dom', tiled=True)  41.7 us
    all_to_all x1, blocking collectives, swap(): return lax.all_to_all(array, axis, split_axis=0, concat_axis=0, tiled=True)  31.6 us
    all_gather x1, blocking collectives, on_device(): chunk = jnp.sum(lax.all_gather(chunk, 'dom'), axis=0)  17.9 us
    ppermute x4, starting transfers between devices, shift(): return lax.ppermute(block_rows, axis, pairs)  11.2 us
    pallas_call x1, Pallas kernels, layer(): pl.pallas_call(functools.partial(layer_kernel, blocks_n, links_n, peers_n...  9.25 us
    all_to_all x1, waiting for transfers between devices, swap(): return lax.all_to_all(array, axis, split_axis=0, concat_axis=0, tiled=True)  8.51 us
    all_to_all x1, starting transfers between devices, swap(): return lax.all_to_all(array, axis, split_axis=0, concat_axis=0, tiled=True)  5.65 us
  transfers between devices with their start and end apart: 6, of which 1 were waited for; matrix products, arithmetic and copies ran while one was open for 5% of the time, Pallas kernels for 0%

profile of v2, /device:TPU:1, one launch (start us, length us, event | category | flops | bytes accessed | tf_op | source)
XLA Modules:
  0.0 152.2 jit_solution(15769956279587390216)
XLA Ops:
  7.2 0.9 slice_bitcast_fusion
  8.1 5.7 %collective-permute-start = (bf16[128,256]{1,0:T(8,128)(2,1)S(1)}, bf16[128,256]{1,0:T(8,128)(2,1)S(1)}, u32[]{:S(2)}, u32[]{:S(2)}) collective-permute-start(bf16[128,256]{1,0:T(8,128)(2,1)S(1)} %get-tuple-element.20), channel_id=1, source_target_pairs={{0,1},{1,2},{2,3},{3,4},{4,5},{5,6},{6,7},{7,8},{8,9},{9,10},{10,1... | collective-permute-start | bytes 196616 | tf_op jit(solution)/shard_map/rims/ppermute | solution.py:221
  13.8 1.3 collective-permute-start.1
  15.1 0.7 convert_element_type.54
  15.8 0.1 copy.19
  15.9 0.1 convert_element_type.55
  16.0 1.0 multiply_convert_fusion.1
  17.1 41.7 %all-gather.2 = f16[8448,256]{1,0:T(8,128)(2,1)S(1)} all-gather(f16[528,256]{1,0:T(8,128)(2,1)S(1)} %multiply_convert_fusion.1), channel_id=1, replica_groups=mesh['dom'=16,'grp'=64] {'dom'}, dimensions={0}, use_global_device_ids=true | all-gather | bytes 4595712 | tf_op jit(solution)/shard_map/gather_rows/all_gather | solution.py:241
  58.8 2.6 %multiply_convert_fusion.gathered_ref = bf16[8448,256]{1,0:T(8,128)(2,1)} fusion(f16[8448,256]{1,0:T(8,128)(2,1)S(1)} %all-gather.2), kind=kLoop, calls=%fused_computation | loop fusion | flops 6488064 | bytes 8650752 | tf_op jit(solution)/shard_map/gather_rows/convert_element_type | solution.py:242
  61.6 0.6 pad_add_fusion.plan_ref
  62.2 0.6 copy-done.3
  62.9 9.3 %layer.1 = (bf16[512,256]{1,0:T(8,128)(2,1)}, f32[512,256]{1,0:T(8,128)}, bf16[256,256]{1,0:T(8,128)(2,1)}, bf16[8192,256]{1,0:T(8,128)(2,1)}, bf16[64,32,128]{2,1,0:T(8,128)(2,1)}) custom-call(s32[84]{0:T(128)} %pad_add_fusion.plan_ref, bf16[8448,256]{1,0:T(8,128)(2,1)} %multiply_convert_fusion.gathered_ref, bf16[128,256]{1,0:T(8,128)(2,1)} %copy-done.3, ...), custom_call_target="tpu_custom_call" | custom-call | flops 1300000000 | bytes 12000000 | tf_op jit(solution)/shard_map/layer/pallas_call | solution.py:186
  72.2 1.0 copy-done.1
  73.2 31.6 %all_to_all.10 = bf16[64,32,128]{2,1,0:T(8,128)(2,1)S(1)} all-to-all(bf16[64,32,128]{2,1,0:T(8,128)(2,1)S(1)} %copy-done.1), channel_id=1, replica_groups=mesh['dom'=16,'grp'=64] {'grp'}, dimensions={0} | all-to-all | bytes 1048576 | tf_op jit(solution)/shard_map/weight_sums/all_to_all | solution.py:225
  104.8 0.1 convert_reduce_fusion
  104.9 17.9 %all-gather = f32[512,128]{1,0:T(8,128)S(1)} all-gather(f32[32,128]{1,0:T(8,128)S(1)} %convert_reduce_fusion), channel_id=2, replica_groups=mesh['dom'=16,'grp'=64] {'dom'}, dimensions={0}, use_global_device_ids=true | all-gather | bytes 278528 | tf_op jit(solution)/shard_map/weight_sums/all_gather | solution.py:275
  122.8 0.7 broadcast_in_dim.18
  123.5 5.6 %all-to-all-start.1 = ((bf16[64,16,128]{2,1,0:T(8,128)(2,1)}), bf16[64,16,128]{2,1,0:T(8,128)(2,1)S(1)}, u32[]{:S(2)}, u32[]{:S(2)}) async-start(bf16[64,16,128]{2,1,0:T(8,128)(2,1)} %broadcast_in_dim.18), calls=%async_computation.2 | async-start | bytes 524288 | tf_op jit(solution)/shard_map/weight_sums/all_to_all | solution.py:225
  129.2 2.9 %collective-permute-start.2 = (bf16[128,256]{1,0:T(8,128)(2,1)S(1)}, bf16[128,256]{1,0:T(8,128)(2,1)S(1)}, u32[]{:S(2)}, u32[]{:S(2)}) collective-permute-start(bf16[128,256]{1,0:T(8,128)(2,1)S(1)} %get-tuple-element.21), channel_id=1, source_target_pairs={{0,1},{1,2},{2,3},{3,4},{4,5},{5,6},{6,7},{7,8},{8,9},{9,10},{10,1... | collective-permute-start | bytes 196616 | tf_op jit(solution)/shard_map/return_rims/ppermute | solution.py:221
  132.2 1.3 collective-permute-start.3
  133.5 0.6 slice_bitcast_fusion.2
  134.0 8.5 %all-to-all-done.1 = bf16[64,16,128]{2,1,0:T(8,128)(2,1)S(1)} async-done(((bf16[64,16,128]{2,1,0:T(8,128)(2,1)}), bf16[64,16,128]{2,1,0:T(8,128)(2,1)S(1)}, u32[]{:S(2)}, u32[]{:S(2)}) %all-to-all-start.1) | async-done | bytes 262176 | tf_op jit(solution)/shard_map/weight_sums/all_to_all | solution.py:225
  142.6 0.8 pad_maximum_fusion
  143.4 1.9 %add_bitcast_fusion = f32[1,512,256]{2,1,0:T(8,128)} fusion(f32[512,256]{1,0:T(8,128)S(1)} %copy-done, bf16[512,256]{1,0:T(8,128)(2,1)} %reduce-scatter.2.cloned.1.call-done, bf16[128,256]{1,0:T(8,128)(2,1)S(1)} %collective-permute-done.3, bf16[128,256]{1,0:T(8,128)(2,1)S(1)} %collective-permute-done.2, bf16[512]{0:T(512)(128)(2,1)S(1)} %pad.8.clone), kind=kLoop, calls=%fused_computation.7 | loop fusion | flops 1179648 | bytes 1442816 | tf_op jit(solution)/shard_map/broadcast_in_dim | solution.py:288
  (31 shorter events, 0.5 us)
Async XLA Ops:
  7.2 136.3 %reduce-scatter.2.cloned.1.call-start = ((), (), s32[]{:S(2)}) async-start(), calls=%async_computation.3 | async-start | bytes 4456448 | tf_op jit(solution)/shard_map/return_slots/reduce_scatter | solution.py:269
  8.1 54.1 %collective-permute-start = (bf16[128,256]{1,0:T(8,128)(2,1)S(1)}, bf16[128,256]{1,0:T(8,128)(2,1)S(1)}, u32[]{:S(2)}, u32[]{:S(2)}) collective-permute-start(bf16[128,256]{1,0:T(8,128)(2,1)S(1)} %get-tuple-element.20), channel_id=1, source_target_pairs={{0,1},{1,2},{2,3},{3,4},{4,5},{5,6},{6,7},{7,8},{8,9},{9,10},{10,1... | collective-permute-start | bytes 196616 | tf_op jit(solution)/shard_map/rims/ppermute | solution.py:221
  13.8 48.4 %collective-permute-start.1 = (bf16[128,256]{1,0:T(8,128)(2,1)S(1)}, bf16[128,256]{1,0:T(8,128)(2,1)S(1)}, u32[]{:S(2)}, u32[]{:S(2)}) collective-permute-start(bf16[128,256]{1,0:T(8,128)(2,1)S(1)} %get-tuple-element.19), channel_id=1, source_target_pairs={{1,0},{2,1},{3,2},{4,3},{5,4},{6,5},{7,6},{8,7},{9,8},{10,9},{11,1... | collective-permute-start | bytes 196616 | tf_op jit(solution)/shard_map/rims/ppermute | solution.py:221
  58.8 2.8 %copy-start.5 = (s32[1,1,4,12]{3,2,1,0:T(4,128)S(1)}, s32[1,1,4,12]{3,2,1,0:T(4,128)}, u32[]{:S(2)}) copy-start(s32[1,1,4,12]{3,2,1,0:T(4,128)} %param.13) | copy-start | bytes 580
  58.8 2.9 %copy-start.6 = (s32[1,1,4]{2,1,0:T(1,128)S(1)}, s32[1,1,4]{2,1,0:T(1,128)}, u32[]{:S(2)}) copy-start(s32[1,1,4]{2,1,0:T(1,128)} %param.12) | copy-start | bytes 52
  62.2 0.6 copy-start.3
  62.2 0.6 copy-start.4
  72.1 1.0 copy-start.1
  72.2 57.1 %copy-start.2 = (bf16[256,256]{1,0:T(8,128)(2,1)S(1)}, bf16[256,256]{1,0:T(8,128)(2,1)}, u32[]{:S(2)}) copy-start(bf16[256,256]{1,0:T(8,128)(2,1)} %get-tuple-element.13) | copy-start | bytes 393220
  72.2 71.3 %copy-start = (f32[512,256]{1,0:T(8,128)S(1)}, f32[512,256]{1,0:T(8,128)}, u32[]{:S(2)}) copy-start(f32[512,256]{1,0:T(8,128)} %get-tuple-element.11) | copy-start | bytes 1572868
  123.5 19.0 %all-to-all-start.1 = ((bf16[64,16,128]{2,1,0:T(8,128)(2,1)}), bf16[64,16,128]{2,1,0:T(8,128)(2,1)S(1)}, u32[]{:S(2)}, u32[]{:S(2)}) async-start(bf16[64,16,128]{2,1,0:T(8,128)(2,1)} %broadcast_in_dim.18), calls=%async_computation.2 | async-start | bytes 524288 | tf_op jit(solution)/shard_map/weight_sums/all_to_all | solution.py:225
  129.2 14.2 %collective-permute-start.2 = (bf16[128,256]{1,0:T(8,128)(2,1)S(1)}, bf16[128,256]{1,0:T(8,128)(2,1)S(1)}, u32[]{:S(2)}, u32[]{:S(2)}) collective-permute-start(bf16[128,256]{1,0:T(8,128)(2,1)S(1)} %get-tuple-element.21), channel_id=1, source_target_pairs={{0,1},{1,2},{2,3},{3,4},{4,5},{5,6},{6,7},{7,8},{8,9},{9,10},{10,1... | collective-permute-start | bytes 196616 | tf_op jit(solution)/shard_map/return_rims/ppermute | solution.py:221
  132.2 11.2 %collective-permute-start.3 = (bf16[128,256]{1,0:T(8,128)(2,1)S(1)}, bf16[128,256]{1,0:T(8,128)(2,1)S(1)}, u32[]{:S(2)}, u32[]{:S(2)}) collective-permute-start(bf16[128,256]{1,0:T(8,128)(2,1)S(1)} %get-tuple-element.22), channel_id=1, source_target_pairs={{1,0},{2,1},{3,2},{4,3},{5,4},{6,5},{7,6},{8,7},{9,8},{10,9},{11,1... | collective-permute-start | bytes 196616 | tf_op jit(solution)/shard_map/return_rims/ppermute | solution.py:221
Sparse Core Ops, SparseCore 0:
  72.3 68.4 reduce-scatter.1

commit v3 on v2

--- a/solution.py
+++ b/solution.py
@@ -43,21 +43,15 @@
     cot_hbm,
     hidden_ref,
     base_ref,
-    rims_ref,
-    sends_ref,
-    weights_ref,
-    tiles_ref,
-    degree_ref,
-    w_self_ref,
-    w_nbr_ref,
-    bias_ref,
-    cot_ref,
-    table,
-    grads,
-    own_sems,
-    tile_sems,
-    table_sems,
+    to_above_ref,
+    to_below_ref,
+    slots_ref,
+    *rest,
 ):
+    parts_refs = rest[:-12]
+    tiles_ref, degree_ref, w_self_ref, w_nbr_ref, bias_ref, cot_ref = rest[-12:-6]
+    table, grads, weights = rest[-6:-3]
+    own_sems, tile_sems, table_sems = rest[-3:]
     rows_n, width = cot_ref.shape
     halo = blocks_n + 2
     slots_n = peers_n * per_peer
@@ -84,37 +78,32 @@
         )
         for b in range(blocks_n)
     ]
-    table_copies = [
-        pltpu.make_async_copy(below_ref, table.at[pl.ds(blocks_n * BLK, BLK)], table_sems.at[0]),
-        pltpu.make_async_copy(above_ref, table.at[pl.ds((blocks_n + 1) * BLK, BLK)], table_sems.at[1]),
-    ]
+    table_copies = []
     for slot in range(slots_n):
         source = (slot // per_peer) * (rows_n + PAD) + jnp.maximum(plan_ref[slot], 0) * BLK
         table_copies.append(
             pltpu.make_async_copy(
                 gathered_ref.at[pl.ds(pl.multiple_of(source, PAD), BLK)],
                 table.at[pl.ds((halo + slot) * BLK, BLK)],
-                table_sems.at[2 + slot],
+                table_sems.at[slot],
             )
         )
     for copy in own + table_copies + tile_copies:
         copy.start()
 
+    table[pl.ds(blocks_n * BLK, BLK)] = below_ref[...]
+    table[pl.ds((blocks_n + 1) * BLK, BLK)] = above_ref[...]
     table[pl.ds(table_n * BLK, BLK)] = jnp.zeros((BLK, width), BF16)
     grads[...] = jnp.zeros_like(grads)
     entries = []
-    owners = []
     for b in range(blocks_n):
         count = plan_ref[slots_n + b]
         for k in range(links_n):
             entry = plan_ref[slots_n + blocks_n + b * links_n + k]
             is_slot = entry >= halo
             slot = jnp.maximum(entry - halo, 0)
-            owner = plan_ref[slot]
-            dead = (k >= count) | (is_slot & (owner < 0))
+            dead = (k >= count) | (is_slot & (plan_ref[slot] < 0))
             entries.append(jnp.where(dead, table_n, entry))
-            owner = jnp.where(is_slot, halo + (slot // per_peer) * blocks_n + owner, entry)
-            owners.append(jnp.where(dead, halo + peers_n * blocks_n, owner))
 
     for copy in own:
         copy.wait()
@@ -146,54 +135,53 @@
     slope = gate * (1.0 + pre_act * (1.0 - gate))
     pre_grad = (cot_ref[...].astype(F32) * slope).astype(BF16)
     grad_all = jnp.concatenate([dot(rows, pre_grad, ROWS_T), dot(mean_rows, pre_grad, ROWS_T)], axis=0)
-    grad_all = grad_all.astype(BF16)
     bias_sum = jnp.sum(pre_grad.astype(F32), axis=0, keepdims=True)
-    parts, each = weights_ref.shape[0], weights_ref.shape[1] // 2
-    halves = width // BLK
-    lines = [bias_sum[:, i * BLK : (i + 1) * BLK] for i in range(halves)]
-    lines.append(jnp.zeros((each - halves, BLK), F32))
-    bias_tile = jnp.concatenate(lines, axis=0).astype(BF16)
-    stride = parts // halves
-    for i in range(halves):
-        chunk = grad_all[:, i * BLK : (i + 1) * BLK].reshape(stride, each, BLK)
-        weights_ref[pl.ds(i * stride, stride), pl.ds(0, each), :] = chunk
-    weights_ref[:, pl.ds(each, each), :] = jnp.broadcast_to(bias_tile[None], (parts, each, BLK))
+    bias_rows = jnp.concatenate([bias_sum, jnp.zeros((PAD - 1, width), F32)], axis=0).astype(BF16)
+    weights[...] = grad_all
+    parts = len(parts_refs)
+    each = 2 * width // parts
+    mine = plan_ref[slots_n + blocks_n + blocks_n * links_n]
+    for step, part_ref in enumerate(parts_refs):
+        start = pl.multiple_of(lax.rem(mine + step, parts) * each, each)
+        part_ref[pl.ds(0, each)] = weights[pl.ds(start, each)].astype(BF16)
+        part_ref[pl.ds(each, PAD)] = bias_rows
 
     mean_grad = dot(pre_grad, w_nbr_ref[...], COLS_T)
     for b in range(blocks_n):
         sum_grad = (mean_grad[b * BLK : (b + 1) * BLK] / spreads[b]).astype(BF16)
         for k in range(links_n):
             at = b * links_n + k
-            where = block(owners[at])
+            where = block(entries[at])
             grads[where] += dot(tiles_ref[at], sum_grad, ROWS_T)
     base_ref[...] = dot(pre_grad, w_self_ref[...], COLS_T) + grads[pl.ds(0, rows_n)]
-    rims_ref[...] = grads[pl.ds(rows_n, 2 * BLK)].astype(BF16)
-    for p in range(peers_n):
-        sends_ref[pl.ds(p * rows_n, rows_n)] = grads[pl.ds(halo * BLK + p * rows_n, rows_n)].astype(BF16)
-
-
-def layer(recv, count, index, gathered, below, above, rows, tiles, degree, w_self, w_nbr, bias, cot, parts):
+    to_below_ref[...] = grads[pl.ds(rows_n, BLK)].astype(BF16)
+    to_above_ref[...] = grads[pl.ds(rows_n + BLK, BLK)].astype(BF16)
+    for slot in range(slots_n):
+        slots_ref[pl.ds(slot * BLK, BLK)] = grads[pl.ds((halo + slot) * BLK, BLK)].astype(BF16)
+
+
+def layer(recv, count, index, mine, gathered, below, above, rows, tiles, degree, w_self, w_nbr, bias, cot, parts):
     blocks_n, links_n = index.shape
     peers_n, per_peer = recv.shape
     rows_n, width = rows.shape
     table_n = blocks_n + 2 + recv.size
-    owners_n = blocks_n + 2 + peers_n * blocks_n
-    plan = jnp.concatenate([recv.reshape(-1), count, index.reshape(-1)])
+    plan = jnp.concatenate([recv.reshape(-1), count, index.reshape(-1), mine.reshape(1)])
     smem = pl.BlockSpec(memory_space=pltpu.SMEM)
     hbm = pl.BlockSpec(memory_space=pl.ANY)
     vmem = pl.BlockSpec(memory_space=pltpu.VMEM)
-    each = 2 * width * (width // BLK) // parts
+    each = 2 * width // parts
+    outs = [
+        jax.ShapeDtypeStruct((rows_n, width), BF16),
+        jax.ShapeDtypeStruct((rows_n, width), F32),
+        jax.ShapeDtypeStruct((BLK, width), BF16),
+        jax.ShapeDtypeStruct((BLK, width), BF16),
+        jax.ShapeDtypeStruct((recv.size * BLK, width), BF16),
+    ] + [jax.ShapeDtypeStruct((each + PAD, width), BF16)] * parts
     return pl.pallas_call(
         functools.partial(layer_kernel, blocks_n, links_n, peers_n, per_peer),
-        out_shape=(
-            jax.ShapeDtypeStruct((rows_n, width), BF16),
-            jax.ShapeDtypeStruct((rows_n, width), F32),
-            jax.ShapeDtypeStruct((2 * BLK, width), BF16),
-            jax.ShapeDtypeStruct((peers_n * rows_n, width), BF16),
-            jax.ShapeDtypeStruct((parts, 2 * each, BLK), BF16),
-        ),
-        in_specs=[smem] + [hbm] * 10,
-        out_specs=(vmem,) * 5,
+        out_shape=outs,
+        in_specs=[smem, hbm, vmem, vmem] + [hbm] * 7,
+        out_specs=[vmem] * len(outs),
         scratch_shapes=[
             pltpu.VMEM(tiles.shape, BF16),
             pltpu.VMEM(degree.shape, degree.dtype),
@@ -202,10 +190,11 @@
             pltpu.VMEM(bias.shape, F32),
             pltpu.VMEM(cot.shape, BF16),
             pltpu.VMEM(((table_n + 1) * BLK, width), BF16),
-            pltpu.VMEM(((owners_n + 1) * BLK, width), F32),
+            pltpu.VMEM(((table_n + 1) * BLK, width), F32),
+            pltpu.VMEM((2 * width, width), F32),
             pltpu.SemaphoreType.DMA((6,)),
             pltpu.SemaphoreType.DMA((blocks_n,)),
-            pltpu.SemaphoreType.DMA((2 + recv.size,)),
+            pltpu.SemaphoreType.DMA((recv.size,)),
         ],
         compiler_params=pltpu.CompilerParams(vmem_limit_bytes=56 * 2**20),
         cost_estimate=pl.CostEstimate(
@@ -213,6 +202,72 @@
         ),
         name="layer",
     )(plan, gathered, below, above, rows, tiles, degree, w_self, w_nbr, bias, cot)
+
+
+def collect_kernel(blocks_n, sent_ref, base_ref, returned_ref, below_ref, above_ref, out_ref, total):
+    rows_n, width = base_ref.shape
+    total[pl.ds(0, rows_n)] = base_ref[...]
+    total[pl.ds(rows_n, BLK)] = jnp.zeros((BLK, width), F32)
+    total[pl.ds(0, BLK)] += below_ref[...].astype(F32)
+    total[pl.ds(rows_n - BLK, BLK)] += above_ref[...].astype(F32)
+    peers_n, per_peer = sent_ref.shape
+    for p in range(peers_n):
+        for s in range(per_peer):
+            owner = sent_ref[p, s]
+            where = block(jnp.where(owner < 0, blocks_n, owner))
+            total[where] += returned_ref[pl.ds((p * per_peer + s) * BLK, BLK)].astype(F32)
+    out_ref[...] = total[pl.ds(0, rows_n)]
+
+
+def collect(sent, base, returned, below, above):
+    rows_n, width = base.shape
+    smem = pl.BlockSpec(memory_space=pltpu.SMEM)
+    vmem = pl.BlockSpec(memory_space=pltpu.VMEM)
+    return pl.pallas_call(
+        functools.partial(collect_kernel, rows_n // BLK),
+        out_shape=jax.ShapeDtypeStruct((rows_n, width), F32),
+        in_specs=[smem] + [vmem] * 4,
+        out_specs=vmem,
+        scratch_shapes=[pltpu.VMEM((rows_n + BLK, width), F32)],
+        compiler_params=pltpu.CompilerParams(vmem_limit_bytes=16 * 2**20),
+        cost_estimate=pl.CostEstimate(flops=5_000_000, bytes_accessed=4_000_000, transcendentals=0),
+        name="collect",
+    )(sent, base, returned, below, above)
+
+
+def assemble_kernel(mine_ref, *refs):
+    *pieces, self_ref, nbr_ref, whole = refs
+    each, width = pieces[0].shape
+    parts = len(pieces)
+    for step, piece in enumerate(pieces):
+        start = lax.rem(mine_ref[0] + parts - step, parts) * each
+        whole[pl.ds(pl.multiple_of(start, each), each)] = piece[...].astype(F32)
+    self_ref[...] = whole[pl.ds(0, width)]
+    nbr_ref[...] = whole[pl.ds(width, width)]
+
+
+def assemble(mine, pieces):
+    width = pieces[0].shape[1]
+    smem = pl.BlockSpec(memory_space=pltpu.SMEM)
+    vmem = pl.BlockSpec(memory_space=pltpu.VMEM)
+    return pl.pallas_call(
+        assemble_kernel,
+        out_shape=(jax.ShapeDtypeStruct((width, width), F32),) * 2,
+        in_specs=[smem] + [vmem] * len(pieces),
+        out_specs=(vmem,) * 2,
+        scratch_shapes=[pltpu.VMEM((2 * width, width), F32)],
+        compiler_params=pltpu.CompilerParams(vmem_limit_bytes=8 * 2**20),
+        cost_estimate=pl.CostEstimate(flops=0, bytes_accessed=1_000_000, transcendentals=0),
+        name="assemble",
+    )(mine.reshape(1), *pieces)
+
+
+def rotation_sum(terms):
+    terms = [term.astype(F32) for term in terms]
+    while len(terms) > 1:
+        half = len(terms) // 2
+        terms = [terms[i] + terms[i + half] for i in range(half)]
+    return terms[0]
 
 
 def shift(block_rows, axis, step):
@@ -248,10 +303,23 @@
         below = shift(rows[rows_n - BLK :], "grp", 1)
         above = shift(rows[:BLK], "grp", -1)
 
-    hidden, base, rims, sends, partial = layer(
+    inner = 1 << ((groups.bit_length()) // 2)
+    outer = groups // inner
+
+    def turn(array, far, near):
+        pairs = [
+            (y * inner + z, (y + far) % outer * inner + (z + near) % inner)
+            for y in range(outer)
+            for z in range(inner)
+        ]
+        return lax.ppermute(array, "grp", pairs)
+
+    mine = lax.rem(lax.axis_index("grp"), inner)
+    hidden, base, to_above, to_below, slot_grads, *partial = layer(
         recv,
         nbr_count[0, 0],
         nbr_index[0, 0],
+        mine,
         gathered,
         below,
         above,
@@ -262,30 +330,26 @@
         w_nbr,
         bias.reshape(1, width),
         cotangent[0],
-        groups,
+        inner,
     )
 
     with jax.named_scope("return_slots"):
-        returned = lax.psum_scatter(sends, "dom", tiled=True)
+        returned = swap(slot_grads, "dom")
     with jax.named_scope("return_rims"):
-        from_above = shift(rims[:BLK], "grp", -1)
-        from_below = shift(rims[BLK:], "grp", 1)
+        from_above = shift(to_below, "grp", -1)
+        from_below = shift(to_above, "grp", 1)
     with jax.named_scope("weight_sums"):
-        chunk = jnp.sum(swap(partial, "grp").astype(F32), axis=0)
-        chunk = jnp.sum(lax.all_gather(chunk, "dom"), axis=0)
-        chunk = chunk * (1.0 / math.sqrt(rows_n * doms * groups))
-        halves = width // BLK
-        each = chunk.shape[0] // 2
-        bias_grad = chunk[each : each + halves].reshape(width)
-        finished = chunk[:each].astype(BF16)
-        whole = swap(jnp.broadcast_to(finished[None], (groups, each, BLK)), "grp")
-        whole = whole.reshape(halves, 2 * width, BLK).astype(F32)
-        whole = jnp.concatenate([whole[i] for i in range(halves)], axis=1)
-    edges = jnp.concatenate(
-        [from_below, jnp.zeros((rows_n - 2 * BLK, width), BF16), from_above], axis=0
-    )
-    feat_grad = base + returned.astype(F32) + edges.astype(F32)
-    return hidden[None], feat_grad[None], whole[:width], whole[width:], bias_grad
+        chunk = rotation_sum([partial[0]] + [turn(partial[k], 0, k) for k in range(1, inner)])
+        chunk = chunk.astype(BF16)
+        chunk = rotation_sum([chunk] + [turn(chunk, k, 0) for k in range(1, outer)])
+        chunk = lax.all_gather(chunk.astype(BF16), "dom").astype(F32)
+        chunk = jnp.sum(chunk, axis=0) * (1.0 / math.sqrt(rows_n * doms * groups))
+        bias_grad = chunk[chunk.shape[0] - PAD]
+        chunk = chunk[: chunk.shape[0] - PAD].astype(BF16)
+        pieces = [chunk] + [turn(chunk, 0, k) for k in range(1, inner)]
+        grad_self, grad_nbr = assemble(mine, pieces)
+    feat_grad = collect(send_list[0, 0], base, returned, from_below, from_above)
+    return hidden[None], feat_grad[None], grad_self, grad_nbr, bias_grad
 
 
 def solution(mesh):

time: 153 us -> 200 us (1.31)
  starting transfers between devices: 16.9 us -> 104 us
  blocking collectives: 91.2 us -> 65.6 us
  between operations: 14.2 us -> 1.11 us
    ppermute x0 -> x21, starting transfers between devices: none -> 89.8 us  [turn(): return lax.ppermute(array, 'grp', pairs)]
    all_to_all x1 -> x0, blocking collectives: 31.6 us -> none  [swap(): return lax.all_to_all(array, axis, split_axis=0, concat_axis=0, tiled=True)]
    all_to_all x1, waiting for transfers between devices: 8.51 us -> 0.01 us  [swap(): return lax.all_to_all(array, axis, split_axis=0, concat_axis=0, tiled=True)]
    ppermute x0 -> x21, waiting for transfers between devices: none -> 6.79 us  [turn(): return lax.ppermute(array, 'grp', pairs)]
    all_gather x1, blocking collectives: 17.9 us -> 23.9 us  [on_device(): chunk = lax.all_gather(chunk.astype(BF16), 'dom').astype(F32)]
    pallas_call x0 -> x2, Pallas kernels: none -> 2.77 us  [the longest x1 1.92 us: collect(): pl.pallas_call(functools.partial(collect_kernel, rows_n // BLK), out_shap...]
  transfers between devices with their start and end apart: 6 -> 26, of which waited for: 1 -> 3; matrix products, arithmetic and copies ran while one was open for 5% -> 4% of each run, Pallas kernels for 0% -> 0%
where the time goes in v3:
time: 200 us; the launch traced here: 198 us
  starting transfers between devices  104 us (52%)
  blocking collectives  65.6 us (33%)
  Pallas kernels  11.2 us (6%)
  waiting for transfers between devices  6.8 us (3%)
  other arithmetic  5.88 us (3%)
  local copies, waits for them, and re-layouts  2.67 us (1%)
    ppermute x21, starting transfers between devices, turn(): return lax.ppermute(array, 'grp', pairs)  89.8 us
    all_gather x1, blocking collectives, on_device(): packed = lax.all_gather(wide.astype(jnp.float16), 'dom', tiled=True)  41.7 us
    all_gather x1, blocking collectives, on_device(): chunk = lax.all_gather(chunk.astype(BF16), 'dom').astype(F32)  23.9 us
    ppermute x4, starting transfers between devices, shift(): return lax.ppermute(block_rows, axis, pairs)  10.9 us
    pallas_call x1, Pallas kernels, layer(): pl.pallas_call(functools.partial(layer_kernel, blocks_n, links_n, peers_n...  8.39 us
    ppermute x21, waiting for transfers between devices, turn(): return lax.ppermute(array, 'grp', pairs)  6.79 us
  transfers between devices with their start and end apart: 26, of which 3 were waited for; matrix products, arithmetic and copies ran while one was open for 4% of the time, Pallas kernels for 0%

profile of v3, /device:TPU:1, one launch (start us, length us, event | category | flops | bytes accessed | tf_op | source)
XLA Modules:
  0.0 197.7 jit_solution(424947013478932891)
XLA Ops:
  1.5 5.7 %collective-permute-start = (bf16[128,256]{1,0:T(8,128)(2,1)S(1)}, bf16[128,256]{1,0:T(8,128)(2,1)S(1)}, u32[]{:S(2)}, u32[]{:S(2)}) collective-permute-start(bf16[128,256]{1,0:T(8,128)(2,1)S(1)} %get-tuple-element.36), channel_id=1, source_target_pairs={{0,1},{1,2},{2,3},{3,4},{4,5},{5,6},{6,7},{7,8},{8,9},{9,10},{10,1... | collective-permute-start | bytes 196616 | tf_op jit(solution)/shard_map/rims/ppermute | solution.py:276
  10.5 41.7 %all-gather.2 = f16[8448,256]{1,0:T(8,128)(2,1)S(1)} all-gather(f16[528,256]{1,0:T(8,128)(2,1)S(1)} %multiply_convert_fusion.1), channel_id=1, replica_groups=mesh['dom'=16,'grp'=64] {'dom'}, dimensions={0}, use_global_device_ids=true | all-gather | bytes 4595712 | tf_op jit(solution)/shard_map/gather_rows/all_gather | solution.py:296
  52.2 2.6 %multiply_convert_fusion.gathered_ref = bf16[8448,256]{1,0:T(8,128)(2,1)} fusion(f16[8448,256]{1,0:T(8,128)(2,1)S(1)} %all-gather.2), kind=kLoop, calls=%fused_computation | loop fusion | flops 6488064 | bytes 8650752 | tf_op jit(solution)/shard_map/gather_rows/convert_element_type | solution.py:297
  56.3 8.4 %layer.1 = (bf16[512,256]{1,0:T(8,128)(2,1)}, f32[512,256]{1,0:T(8,128)}, bf16[128,256]{1,0:T(8,128)(2,1)}, bf16[128,256]{1,0:T(8,128)(2,1)}, bf16[4096,256]{1,0...) custom-call(s32[85]{0:T(128)} %pad_add_fusion.plan_ref, ...), custom_call_target="tpu_custom_call" | custom-call | flops 1300000000 | bytes 12000000 | tf_op jit(solution)/shard_map/layer/pallas_call | solution.py:180
  64.8 3.8 %all-to-all-start = ((bf16[16,256,256]{2,1,0:T(8,128)(2,1)}), bf16[16,256,256]{2,1,0:T(8,128)(2,1)S(1)}, u32[]{:S(2)}, u32[]{:S(2)}) async-start(bf16[16,256,256]{2,1,0:T(8,128)(2,1)} %bitcast.27), calls=%async_computation | async-start | bytes 4194304 | tf_op jit(solution)/shard_map/return_slots/all_to_all | solution.py:280
  68.6 10.1 %collective-permute-start.10 = (bf16[80,256]{1,0:T(8,128)(2,1)}, bf16[80,256]{1,0:T(8,128)(2,1)S(1)}, u32[]{:S(2)}, u32[]{:S(2)}) collective-permute-start(bf16[80,256]{1,0:T(8,128)(2,1)} %get-tuple-element.32), channel_id=1, source_target_pairs={{0,7},{1,0},{2,1},{3,2},{4,3},{5,4},{6,5},{7,6},{8,15},{9,8},{10,9... | collective-permute-start | bytes 122888 | tf_op jit(solution)/shard_map/weight_sums/ppermute | solution.py:315
  80.6 3.8 %collective-permute-start.5 = (bf16[80,256]{1,0:T(8,128)(2,1)}, bf16[80,256]{1,0:T(8,128)(2,1)S(1)}, u32[]{:S(2)}, u32[]{:S(2)}) collective-permute-start(bf16[80,256]{1,0:T(8,128)(2,1)} %get-tuple-element.27), channel_id=1, source_target_pairs={{0,2},{1,3},{2,4},{3,5},{4,6},{5,7},{6,0},{7,1},{8,10},{9,11},{10,... | collective-permute-start | bytes 122888 | tf_op jit(solution)/shard_map/weight_sums/ppermute | solution.py:315
  84.4 3.6 %collective-permute-start.6 = (bf16[80,256]{1,0:T(8,128)(2,1)}, bf16[80,256]{1,0:T(8,128)(2,1)S(1)}, u32[]{:S(2)}, u32[]{:S(2)}) collective-permute-start(bf16[80,256]{1,0:T(8,128)(2,1)} %get-tuple-element.28), channel_id=1, source_target_pairs={{0,6},{1,7},{2,0},{3,1},{4,2},{5,3},{6,4},{7,5},{8,14},{9,15},{10,... | collective-permute-start | bytes 122888 | tf_op jit(solution)/shard_map/weight_sums/ppermute | solution.py:315
  90.0 5.2 %collective-permute-start.8 = (bf16[80,256]{1,0:T(8,128)(2,1)}, bf16[80,256]{1,0:T(8,128)(2,1)S(1)}, u32[]{:S(2)}, u32[]{:S(2)}) collective-permute-start(bf16[80,256]{1,0:T(8,128)(2,1)} %get-tuple-element.30), channel_id=1, source_target_pairs={{0,5},{1,6},{2,7},{3,0},{4,1},{5,2},{6,3},{7,4},{8,13},{9,14},{10,... | collective-permute-start | bytes 122888 | tf_op jit(solution)/shard_map/weight_sums/ppermute | solution.py:315
  95.1 4.3 %collective-permute-start.9 = (bf16[80,256]{1,0:T(8,128)(2,1)}, bf16[80,256]{1,0:T(8,128)(2,1)S(1)}, u32[]{:S(2)}, u32[]{:S(2)}) collective-permute-start(bf16[80,256]{1,0:T(8,128)(2,1)} %get-tuple-element.31), channel_id=1, source_target_pairs={{0,3},{1,4},{2,5},{3,6},{4,7},{5,0},{6,1},{7,2},{8,11},{9,12},{10,... | collective-permute-start | bytes 122888 | tf_op jit(solution)/shard_map/weight_sums/ppermute | solution.py:315
  99.5 3.9 %collective-permute-done.9 = bf16[80,256]{1,0:T(8,128)(2,1)S(1)} collective-permute-done((bf16[80,256]{1,0:T(8,128)(2,1)}, bf16[80,256]{1,0:T(8,128)(2,1)S(1)}, u32[]{:S(2)}, u32[]{:S(2)}) %collective-permute-start.9) | collective-permute-done | bytes 40992 | tf_op jit(solution)/shard_map/weight_sums/ppermute | solution.py:315
  104.2 8.9 %collective-permute-start.11 = (bf16[80,256]{1,0:T(8,128)(2,1)S(1)}, bf16[80,256]{1,0:T(8,128)(2,1)S(1)}, u32[]{:S(2)}, u32[]{:S(2)}) collective-permute-start(bf16[80,256]{1,0:T(8,128)(2,1)S(1)} %add_convert_fusion.1), channel_id=1, source_target_pairs={{0,32},{1,33},{2,34},{3,35},{4,36},{5,37},{6,38},{7,39},{8,40},{9,... | collective-permute-start | bytes 122888 | tf_op jit(solution)/shard_map/weight_sums/ppermute | solution.py:315
  113.2 3.4 %collective-permute-start.12 = (bf16[80,256]{1,0:T(8,128)(2,1)S(1)}, bf16[80,256]{1,0:T(8,128)(2,1)S(1)}, u32[]{:S(2)}, u32[]{:S(2)}) collective-permute-start(bf16[80,256]{1,0:T(8,128)(2,1)S(1)} %add_convert_fusion.1), channel_id=1, source_target_pairs={{0,16},{1,17},{2,18},{3,19},{4,20},{5,21},{6,22},{7,23},{8,24},{9,... | collective-permute-start | bytes 122888 | tf_op jit(solution)/shard_map/weight_sums/ppermute | solution.py:315
  116.6 4.0 %collective-permute-start.13 = (bf16[80,256]{1,0:T(8,128)(2,1)S(1)}, bf16[80,256]{1,0:T(8,128)(2,1)S(1)}, u32[]{:S(2)}, u32[]{:S(2)}) collective-permute-start(bf16[80,256]{1,0:T(8,128)(2,1)S(1)} %add_convert_fusion.1), channel_id=1, source_target_pairs={{0,48},{1,49},{2,50},{3,51},{4,52},{5,53},{6,54},{7,55},{8,56},{9,... | collective-permute-start | bytes 122888 | tf_op jit(solution)/shard_map/weight_sums/ppermute | solution.py:315
  120.6 3.2 %collective-permute-start.14 = (bf16[80,256]{1,0:T(8,128)(2,1)S(1)}, bf16[80,256]{1,0:T(8,128)(2,1)S(1)}, u32[]{:S(2)}, u32[]{:S(2)}) collective-permute-start(bf16[80,256]{1,0:T(8,128)(2,1)S(1)} %add_convert_fusion.1), channel_id=1, source_target_pairs={{0,8},{1,9},{2,10},{3,11},{4,12},{5,13},{6,14},{7,15},{8,16},{9,17... | collective-permute-start | bytes 122888 | tf_op jit(solution)/shard_map/weight_sums/ppermute | solution.py:315
  125.7 5.2 %collective-permute-start.16 = (bf16[80,256]{1,0:T(8,128)(2,1)S(1)}, bf16[80,256]{1,0:T(8,128)(2,1)S(1)}, u32[]{:S(2)}, u32[]{:S(2)}) collective-permute-start(bf16[80,256]{1,0:T(8,128)(2,1)S(1)} %add_convert_fusion.1), channel_id=1, source_target_pairs={{0,24},{1,25},{2,26},{3,27},{4,28},{5,29},{6,30},{7,31},{8,32},{9,... | collective-permute-start | bytes 122888 | tf_op jit(solution)/shard_map/weight_sums/ppermute | solution.py:315
  130.9 4.5 %collective-permute-start.17 = (bf16[80,256]{1,0:T(8,128)(2,1)S(1)}, bf16[80,256]{1,0:T(8,128)(2,1)S(1)}, u32[]{:S(2)}, u32[]{:S(2)}) collective-permute-start(bf16[80,256]{1,0:T(8,128)(2,1)S(1)} %add_convert_fusion.1), channel_id=1, source_target_pairs={{0,56},{1,57},{2,58},{3,59},{4,60},{5,61},{6,62},{7,63},{8,0},{9,1... | collective-permute-start | bytes 122888 | tf_op jit(solution)/shard_map/weight_sums/ppermute | solution.py:315
  136.5 23.9 %all-gather = bf16[1280,256]{1,0:T(8,128)(2,1)S(1)} all-gather(bf16[80,256]{1,0:T(8,128)(2,1)S(1)} %add_convert_fusion), channel_id=2, replica_groups=mesh['dom'=16,'grp'=64] {'dom'}, dimensions={0}, use_global_device_ids=true | all-gather | bytes 696320 | tf_op jit(solution)/shard_map/weight_sums/all_gather | solution.py:345
  160.6 2.2 %collective-permute-start.18 = (bf16[64,256]{1,0:T(8,128)(2,1)S(1)}, bf16[64,256]{1,0:T(8,128)(2,1)S(1)}, u32[]{:S(2)}, u32[]{:S(2)}) collective-permute-start(bf16[64,256]{1,0:T(8,128)(2,1)S(1)} %slice.35.refs_0_), channel_id=1, source_target_pairs={{0,1},{1,2},{2,3},{3,4},{4,5},{5,6},{6,7},{7,0},{8,9},{9,10},{10,1... | collective-permute-start | bytes 98312 | tf_op jit(solution)/shard_map/weight_sums/ppermute | solution.py:315
  162.8 2.9 %collective-permute-start.19 = (bf16[64,256]{1,0:T(8,128)(2,1)S(1)}, bf16[64,256]{1,0:T(8,128)(2,1)S(1)}, u32[]{:S(2)}, u32[]{:S(2)}) collective-permute-start(bf16[64,256]{1,0:T(8,128)(2,1)S(1)} %slice.35.refs_0_), channel_id=1, source_target_pairs={{0,2},{1,3},{2,4},{3,5},{4,6},{5,7},{6,0},{7,1},{8,10},{9,11},{10,... | collective-permute-start | bytes 98312 | tf_op jit(solution)/shard_map/weight_sums/ppermute | solution.py:315
  165.7 6.9 %collective-permute-start.20 = (bf16[64,256]{1,0:T(8,128)(2,1)S(1)}, bf16[64,256]{1,0:T(8,128)(2,1)S(1)}, u32[]{:S(2)}, u32[]{:S(2)}) collective-permute-start(bf16[64,256]{1,0:T(8,128)(2,1)S(1)} %slice.35.refs_0_), channel_id=1, source_target_pairs={{0,3},{1,4},{2,5},{3,6},{4,7},{5,0},{6,1},{7,2},{8,11},{9,12},{10,... | collective-permute-start | bytes 98312 | tf_op jit(solution)/shard_map/weight_sums/ppermute | solution.py:315
  174.5 2.6 %collective-permute-start.2 = (bf16[128,256]{1,0:T(8,128)(2,1)S(1)}, bf16[128,256]{1,0:T(8,128)(2,1)S(1)}, u32[]{:S(2)}, u32[]{:S(2)}) collective-permute-start(bf16[128,256]{1,0:T(8,128)(2,1)S(1)} %copy-done.7), channel_id=1, source_target_pairs={{0,1},{1,2},{2,3},{3,4},{4,5},{5,6},{6,7},{7,8},{8,9},{9,10},{10,1... | collective-permute-start | bytes 196616 | tf_op jit(solution)/shard_map/return_rims/ppermute | solution.py:276
  178.5 7.5 %collective-permute-start.22 = (bf16[64,256]{1,0:T(8,128)(2,1)S(1)}, bf16[64,256]{1,0:T(8,128)(2,1)S(1)}, u32[]{:S(2)}, u32[]{:S(2)}) collective-permute-start(bf16[64,256]{1,0:T(8,128)(2,1)S(1)} %slice.35.refs_0_), channel_id=1, source_target_pairs={{0,5},{1,6},{2,7},{3,0},{4,1},{5,2},{6,3},{7,4},{8,13},{9,14},{10,... | collective-permute-start | bytes 98312 | tf_op jit(solution)/shard_map/weight_sums/ppermute | solution.py:315
  186.0 4.3 %collective-permute-start.23 = (bf16[64,256]{1,0:T(8,128)(2,1)S(1)}, bf16[64,256]{1,0:T(8,128)(2,1)S(1)}, u32[]{:S(2)}, u32[]{:S(2)}) collective-permute-start(bf16[64,256]{1,0:T(8,128)(2,1)S(1)} %slice.35.refs_0_), channel_id=1, source_target_pairs={{0,6},{1,7},{2,0},{3,1},{4,2},{5,3},{6,4},{7,5},{8,14},{9,15},{10,... | collective-permute-start | bytes 98312 | tf_op jit(solution)/shard_map/weight_sums/ppermute | solution.py:315
  (68 shorter events, 24.1 us)
Async XLA Ops:
  1.5 54.2 %collective-permute-start = (bf16[128,256]{1,0:T(8,128)(2,1)S(1)}, bf16[128,256]{1,0:T(8,128)(2,1)S(1)}, u32[]{:S(2)}, u32[]{:S(2)}) collective-permute-start(bf16[128,256]{1,0:T(8,128)(2,1)S(1)} %get-tuple-element.36), channel_id=1, source_target_pairs={{0,1},{1,2},{2,3},{3,4},{4,5},{5,6},{6,7},{7,8},{8,9},{9,10},{10,1... | collective-permute-start | bytes 196616 | tf_op jit(solution)/shard_map/rims/ppermute | solution.py:276
  7.3 48.4 %collective-permute-start.1 = (bf16[128,256]{1,0:T(8,128)(2,1)S(1)}, bf16[128,256]{1,0:T(8,128)(2,1)S(1)}, u32[]{:S(2)}, u32[]{:S(2)}) collective-permute-start(bf16[128,256]{1,0:T(8,128)(2,1)S(1)} %get-tuple-element.35), channel_id=1, source_target_pairs={{1,0},{2,1},{3,2},{4,3},{5,4},{6,5},{7,6},{8,7},{9,8},{10,9},{11,1... | collective-permute-start | bytes 196616 | tf_op jit(solution)/shard_map/rims/ppermute | solution.py:276
  64.8 131.0 %all-to-all-start = ((bf16[16,256,256]{2,1,0:T(8,128)(2,1)}), bf16[16,256,256]{2,1,0:T(8,128)(2,1)S(1)}, u32[]{:S(2)}, u32[]{:S(2)}) async-start(bf16[16,256,256]{2,1,0:T(8,128)(2,1)} %bitcast.27), calls=%async_computation | async-start | bytes 4194304 | tf_op jit(solution)/shard_map/return_slots/all_to_all | solution.py:280
  68.6 21.4 %collective-permute-start.10 = (bf16[80,256]{1,0:T(8,128)(2,1)}, bf16[80,256]{1,0:T(8,128)(2,1)S(1)}, u32[]{:S(2)}, u32[]{:S(2)}) collective-permute-start(bf16[80,256]{1,0:T(8,128)(2,1)} %get-tuple-element.32), channel_id=1, source_target_pairs={{0,7},{1,0},{2,1},{3,2},{4,3},{5,4},{6,5},{7,6},{8,15},{9,8},{10,9... | collective-permute-start | bytes 122888 | tf_op jit(solution)/shard_map/weight_sums/ppermute | solution.py:315
  78.7 16.4 %collective-permute-start.4 = (bf16[80,256]{1,0:T(8,128)(2,1)}, bf16[80,256]{1,0:T(8,128)(2,1)S(1)}, u32[]{:S(2)}, u32[]{:S(2)}) collective-permute-start(bf16[80,256]{1,0:T(8,128)(2,1)} %get-tuple-element.26), channel_id=1, source_target_pairs={{0,4},{1,5},{2,6},{3,7},{4,0},{5,1},{6,2},{7,3},{8,12},{9,13},{10,... | collective-permute-start | bytes 122888 | tf_op jit(solution)/shard_map/weight_sums/ppermute | solution.py:315
  80.6 18.8 %collective-permute-start.5 = (bf16[80,256]{1,0:T(8,128)(2,1)}, bf16[80,256]{1,0:T(8,128)(2,1)S(1)}, u32[]{:S(2)}, u32[]{:S(2)}) collective-permute-start(bf16[80,256]{1,0:T(8,128)(2,1)} %get-tuple-element.27), channel_id=1, source_target_pairs={{0,2},{1,3},{2,4},{3,5},{4,6},{5,7},{6,0},{7,1},{8,10},{9,11},{10,... | collective-permute-start | bytes 122888 | tf_op jit(solution)/shard_map/weight_sums/ppermute | solution.py:315
  84.4 15.1 %collective-permute-start.6 = (bf16[80,256]{1,0:T(8,128)(2,1)}, bf16[80,256]{1,0:T(8,128)(2,1)S(1)}, u32[]{:S(2)}, u32[]{:S(2)}) collective-permute-start(bf16[80,256]{1,0:T(8,128)(2,1)} %get-tuple-element.28), channel_id=1, source_target_pairs={{0,6},{1,7},{2,0},{3,1},{4,2},{5,3},{6,4},{7,5},{8,14},{9,15},{10,... | collective-permute-start | bytes 122888 | tf_op jit(solution)/shard_map/weight_sums/ppermute | solution.py:315
  88.0 11.4 %collective-permute-start.7 = (bf16[80,256]{1,0:T(8,128)(2,1)}, bf16[80,256]{1,0:T(8,128)(2,1)S(1)}, u32[]{:S(2)}, u32[]{:S(2)}) collective-permute-start(bf16[80,256]{1,0:T(8,128)(2,1)} %get-tuple-element.29), channel_id=1, source_target_pairs={{0,1},{1,2},{2,3},{3,4},{4,5},{5,6},{6,7},{7,0},{8,9},{9,10},{10,1... | collective-permute-start | bytes 122888 | tf_op jit(solution)/shard_map/weight_sums/ppermute | solution.py:315
  90.0 9.5 %collective-permute-start.8 = (bf16[80,256]{1,0:T(8,128)(2,1)}, bf16[80,256]{1,0:T(8,128)(2,1)S(1)}, u32[]{:S(2)}, u32[]{:S(2)}) collective-permute-start(bf16[80,256]{1,0:T(8,128)(2,1)} %get-tuple-element.30), channel_id=1, source_target_pairs={{0,5},{1,6},{2,7},{3,0},{4,1},{5,2},{6,3},{7,4},{8,13},{9,14},{10,... | collective-permute-start | bytes 122888 | tf_op jit(solution)/shard_map/weight_sums/ppermute | solution.py:315
  95.1 8.3 %collective-permute-start.9 = (bf16[80,256]{1,0:T(8,128)(2,1)}, bf16[80,256]{1,0:T(8,128)(2,1)S(1)}, u32[]{:S(2)}, u32[]{:S(2)}) collective-permute-start(bf16[80,256]{1,0:T(8,128)(2,1)} %get-tuple-element.31), channel_id=1, source_target_pairs={{0,3},{1,4},{2,5},{3,6},{4,7},{5,0},{6,1},{7,2},{8,11},{9,12},{10,... | collective-permute-start | bytes 122888 | tf_op jit(solution)/shard_map/weight_sums/ppermute | solution.py:315
  104.2 21.5 %collective-permute-start.11 = (bf16[80,256]{1,0:T(8,128)(2,1)S(1)}, bf16[80,256]{1,0:T(8,128)(2,1)S(1)}, u32[]{:S(2)}, u32[]{:S(2)}) collective-permute-start(bf16[80,256]{1,0:T(8,128)(2,1)S(1)} %add_convert_fusion.1), channel_id=1, source_target_pairs={{0,32},{1,33},{2,34},{3,35},{4,36},{5,37},{6,38},{7,39},{8,40},{9,... | collective-permute-start | bytes 122888 | tf_op jit(solution)/shard_map/weight_sums/ppermute | solution.py:315
  113.2 17.7 %collective-permute-start.12 = (bf16[80,256]{1,0:T(8,128)(2,1)S(1)}, bf16[80,256]{1,0:T(8,128)(2,1)S(1)}, u32[]{:S(2)}, u32[]{:S(2)}) collective-permute-start(bf16[80,256]{1,0:T(8,128)(2,1)S(1)} %add_convert_fusion.1), channel_id=1, source_target_pairs={{0,16},{1,17},{2,18},{3,19},{4,20},{5,21},{6,22},{7,23},{8,24},{9,... | collective-permute-start | bytes 122888 | tf_op jit(solution)/shard_map/weight_sums/ppermute | solution.py:315
  116.6 18.8 %collective-permute-start.13 = (bf16[80,256]{1,0:T(8,128)(2,1)S(1)}, bf16[80,256]{1,0:T(8,128)(2,1)S(1)}, u32[]{:S(2)}, u32[]{:S(2)}) collective-permute-start(bf16[80,256]{1,0:T(8,128)(2,1)S(1)} %add_convert_fusion.1), channel_id=1, source_target_pairs={{0,48},{1,49},{2,50},{3,51},{4,52},{5,53},{6,54},{7,55},{8,56},{9,... | collective-permute-start | bytes 122888 | tf_op jit(solution)/shard_map/weight_sums/ppermute | solution.py:315
  120.6 14.8 %collective-permute-start.14 = (bf16[80,256]{1,0:T(8,128)(2,1)S(1)}, bf16[80,256]{1,0:T(8,128)(2,1)S(1)}, u32[]{:S(2)}, u32[]{:S(2)}) collective-permute-start(bf16[80,256]{1,0:T(8,128)(2,1)S(1)} %add_convert_fusion.1), channel_id=1, source_target_pairs={{0,8},{1,9},{2,10},{3,11},{4,12},{5,13},{6,14},{7,15},{8,16},{9,17... | collective-permute-start | bytes 122888 | tf_op jit(solution)/shard_map/weight_sums/ppermute | solution.py:315
  123.8 11.7 %collective-permute-start.15 = (bf16[80,256]{1,0:T(8,128)(2,1)S(1)}, bf16[80,256]{1,0:T(8,128)(2,1)S(1)}, u32[]{:S(2)}, u32[]{:S(2)}) collective-permute-start(bf16[80,256]{1,0:T(8,128)(2,1)S(1)} %add_convert_fusion.1), channel_id=1, source_target_pairs={{0,40},{1,41},{2,42},{3,43},{4,44},{5,45},{6,46},{7,47},{8,48},{9,... | collective-permute-start | bytes 122888 | tf_op jit(solution)/shard_map/weight_sums/ppermute | solution.py:315
  125.7 9.7 %collective-permute-start.16 = (bf16[80,256]{1,0:T(8,128)(2,1)S(1)}, bf16[80,256]{1,0:T(8,128)(2,1)S(1)}, u32[]{:S(2)}, u32[]{:S(2)}) collective-permute-start(bf16[80,256]{1,0:T(8,128)(2,1)S(1)} %add_convert_fusion.1), channel_id=1, source_target_pairs={{0,24},{1,25},{2,26},{3,27},{4,28},{5,29},{6,30},{7,31},{8,32},{9,... | collective-permute-start | bytes 122888 | tf_op jit(solution)/shard_map/weight_sums/ppermute | solution.py:315
  160.6 16.5 %collective-permute-start.18 = (bf16[64,256]{1,0:T(8,128)(2,1)S(1)}, bf16[64,256]{1,0:T(8,128)(2,1)S(1)}, u32[]{:S(2)}, u32[]{:S(2)}) collective-permute-start(bf16[64,256]{1,0:T(8,128)(2,1)S(1)} %slice.35.refs_0_), channel_id=1, source_target_pairs={{0,1},{1,2},{2,3},{3,4},{4,5},{5,6},{6,7},{7,0},{8,9},{9,10},{10,1... | collective-permute-start | bytes 98312 | tf_op jit(solution)/shard_map/weight_sums/ppermute | solution.py:315
  162.8 15.6 %collective-permute-start.19 = (bf16[64,256]{1,0:T(8,128)(2,1)S(1)}, bf16[64,256]{1,0:T(8,128)(2,1)S(1)}, u32[]{:S(2)}, u32[]{:S(2)}) collective-permute-start(bf16[64,256]{1,0:T(8,128)(2,1)S(1)} %slice.35.refs_0_), channel_id=1, source_target_pairs={{0,2},{1,3},{2,4},{3,5},{4,6},{5,7},{6,0},{7,1},{8,10},{9,11},{10,... | collective-permute-start | bytes 98312 | tf_op jit(solution)/shard_map/weight_sums/ppermute | solution.py:315
  165.7 20.2 %collective-permute-start.20 = (bf16[64,256]{1,0:T(8,128)(2,1)S(1)}, bf16[64,256]{1,0:T(8,128)(2,1)S(1)}, u32[]{:S(2)}, u32[]{:S(2)}) collective-permute-start(bf16[64,256]{1,0:T(8,128)(2,1)S(1)} %slice.35.refs_0_), channel_id=1, source_target_pairs={{0,3},{1,4},{2,5},{3,6},{4,7},{5,0},{6,1},{7,2},{8,11},{9,12},{10,... | collective-permute-start | bytes 98312 | tf_op jit(solution)/shard_map/weight_sums/ppermute | solution.py:315
  172.6 17.7 %collective-permute-start.21 = (bf16[64,256]{1,0:T(8,128)(2,1)S(1)}, bf16[64,256]{1,0:T(8,128)(2,1)S(1)}, u32[]{:S(2)}, u32[]{:S(2)}) collective-permute-start(bf16[64,256]{1,0:T(8,128)(2,1)S(1)} %slice.35.refs_0_), channel_id=1, source_target_pairs={{0,4},{1,5},{2,6},{3,7},{4,0},{5,1},{6,2},{7,3},{8,12},{9,13},{10,... | collective-permute-start | bytes 98312 | tf_op jit(solution)/shard_map/weight_sums/ppermute | solution.py:315
  174.5 21.3 %collective-permute-start.2 = (bf16[128,256]{1,0:T(8,128)(2,1)S(1)}, bf16[128,256]{1,0:T(8,128)(2,1)S(1)}, u32[]{:S(2)}, u32[]{:S(2)}) collective-permute-start(bf16[128,256]{1,0:T(8,128)(2,1)S(1)} %copy-done.7), channel_id=1, source_target_pairs={{0,1},{1,2},{2,3},{3,4},{4,5},{5,6},{6,7},{7,8},{8,9},{9,10},{10,1... | collective-permute-start | bytes 196616 | tf_op jit(solution)/shard_map/return_rims/ppermute | solution.py:276
  177.1 18.6 %collective-permute-start.3 = (bf16[128,256]{1,0:T(8,128)(2,1)S(1)}, bf16[128,256]{1,0:T(8,128)(2,1)S(1)}, u32[]{:S(2)}, u32[]{:S(2)}) collective-permute-start(bf16[128,256]{1,0:T(8,128)(2,1)S(1)} %copy-done.6), channel_id=1, source_target_pairs={{1,0},{2,1},{3,2},{4,3},{5,4},{6,5},{7,6},{8,7},{9,8},{10,9},{11,1... | collective-permute-start | bytes 196616 | tf_op jit(solution)/shard_map/return_rims/ppermute | solution.py:276
  178.5 14.7 %collective-permute-start.22 = (bf16[64,256]{1,0:T(8,128)(2,1)S(1)}, bf16[64,256]{1,0:T(8,128)(2,1)S(1)}, u32[]{:S(2)}, u32[]{:S(2)}) collective-permute-start(bf16[64,256]{1,0:T(8,128)(2,1)S(1)} %slice.35.refs_0_), channel_id=1, source_target_pairs={{0,5},{1,6},{2,7},{3,0},{4,1},{5,2},{6,3},{7,4},{8,13},{9,14},{10,... | collective-permute-start | bytes 98312 | tf_op jit(solution)/shard_map/weight_sums/ppermute | solution.py:315
  186.0 7.2 %collective-permute-start.23 = (bf16[64,256]{1,0:T(8,128)(2,1)S(1)}, bf16[64,256]{1,0:T(8,128)(2,1)S(1)}, u32[]{:S(2)}, u32[]{:S(2)}) collective-permute-start(bf16[64,256]{1,0:T(8,128)(2,1)S(1)} %slice.35.refs_0_), channel_id=1, source_target_pairs={{0,6},{1,7},{2,0},{3,1},{4,2},{5,3},{6,4},{7,5},{8,14},{9,15},{10,... | collective-permute-start | bytes 98312 | tf_op jit(solution)/shard_map/weight_sums/ppermute | solution.py:315
  (10 other events, 498.2 us)

commit v4 on v2

v4 whole, which is shorter than its diff:
```python
import functools
import math

import jax
import jax.numpy as jnp
from jax import lax
from jax.experimental import pallas as pl
from jax.experimental.pallas import tpu as pltpu
from jax.sharding import PartitionSpec as P

BLK = 128
PAD = 16
SCALE = 8192.0
F32 = jnp.float32
BF16 = jnp.bfloat16
ROWS_T = (((0,), (0,)), ((), ()))
COLS_T = (((1,), (1,)), ((), ()))


def dot(a, b, dims=(((1,), (0,)), ((), ()))):
    return lax.dot_general(a, b, dims, preferred_element_type=F32)


def block(t):
    return pl.ds(pl.multiple_of(t * BLK, BLK), BLK)


def live_entries(plan_ref, blocks_n, links_n, peers_n, per_peer):
    halo = blocks_n + 2
    slots_n = peers_n * per_peer
    entries = []
    for b in range(blocks_n):
        count = plan_ref[slots_n + b]
        for k in range(links_n):
            entry = plan_ref[slots_n + blocks_n + b * links_n + k]
            slot = jnp.maximum(entry - halo, 0)
            dead = (k >= count) | ((entry >= halo) & (plan_ref[slot] < 0))
            entries.append(jnp.where(dead, halo + slots_n, entry))
    return entries


def column_spread(degree_ref, b, width):
    line = degree_ref[pl.ds(b, 1), :].astype(F32)
    column = jnp.transpose(jnp.broadcast_to(line, (BLK, BLK)))
    return jnp.concatenate([column] * (width // BLK), axis=1)


def layer_kernel(
    blocks_n,
    links_n,
    peers_n,
    per_peer,
    plan_ref,
    gathered_ref,
    below_ref,
    above_ref,
    rows_hbm,
    tiles_hbm,
    degree_hbm,
    w_self_hbm,
    w_nbr_hbm,
    bias_hbm,
    cot_hbm,
    hidden_ref,
    self_grad_ref,
    sum_grad_ref,
    weights_ref,
    tiles_ref,
    degree_ref,
    w_self_ref,
    w_nbr_ref,
    bias_ref,
    cot_ref,
    table,
    own_sems,
    tile_sems,
    table_sems,
):
    rows_n, width = cot_ref.shape
    halo = blocks_n + 2
    slots_n = peers_n * per_peer
    table_n = halo + slots_n
    rows_ref = table.at[pl.ds(0, rows_n)]
    own = [
        pltpu.make_async_copy(source, target, own_sems.at[i])
        for i, (source, target) in enumerate(
            (
                (rows_hbm, rows_ref),
                (w_self_hbm, w_self_ref),
                (degree_hbm, degree_ref),
                (bias_hbm, bias_ref),
                (w_nbr_hbm, w_nbr_ref),
                (cot_hbm, cot_ref),
            )
        )
    ]
    tile_copies = [
        pltpu.make_async_copy(
            tiles_hbm.at[pl.ds(b * links_n, links_n)],
            tiles_ref.at[pl.ds(b * links_n, links_n)],
            tile_sems.at[b],
        )
        for b in range(blocks_n)
    ]
    table_copies = []
    for slot in range(slots_n):
        source = (slot // per_peer) * (rows_n + PAD) + jnp.maximum(plan_ref[slot], 0) * BLK
        table_copies.append(
            pltpu.make_async_copy(
                gathered_ref.at[pl.ds(pl.multiple_of(source, PAD), BLK)],
                table.at[pl.ds((halo + slot) * BLK, BLK)],
                table_sems.at[slot],
            )
        )
    for copy in own + table_copies + tile_copies:
        copy.start()

    table[pl.ds(blocks_n * BLK, BLK)] = below_ref[...]
    table[pl.ds((blocks_n + 1) * BLK, BLK)] = above_ref[...]
    table[pl.ds(table_n * BLK, BLK)] = jnp.zeros((BLK, width), BF16)
    entries = live_entries(plan_ref, blocks_n, links_n, peers_n, per_peer)

    for copy in own:
        copy.wait()
    rows = rows_ref[...]
    self_act = dot(rows, w_self_ref[...]) + bias_ref[...]
    spreads = [column_spread(degree_ref, b, width) for b in range(blocks_n)]
    for copy in table_copies:
        copy.wait()

    means = []
    for b in range(blocks_n):
        tile_copies[b].wait()
        total = None
        for k in range(0, links_n, 2):
            at = b * links_n + k
            left = jnp.concatenate([tiles_ref[at], tiles_ref[at + 1]], axis=1)
            right = jnp.concatenate([table[block(entries[at])], table[block(entries[at + 1])]], axis=0)
            term = dot(left, right)
            total = term if total is None else total + term
        means.append((total / spreads[b]).astype(BF16))
    mean_rows = jnp.concatenate(means, axis=0)
    pre_act = self_act + dot(mean_rows, w_nbr_ref[...])
    gate = jax.nn.sigmoid(pre_act)
    hidden_ref[...] = (pre_act * gate).astype(BF16)
    slope = gate * (1.0 + pre_act * (1.0 - gate))
    pre_grad = (cot_ref[...].astype(F32) * slope).astype(BF16)

    grad_all = jnp.concatenate([dot(rows, pre_grad, ROWS_T), dot(mean_rows, pre_grad, ROWS_T)], axis=0)
    grad_all = grad_all.astype(BF16)
    bias_sum = jnp.sum(pre_grad.astype(F32), axis=0, keepdims=True)
    bias_rows = jnp.concatenate([bias_sum, jnp.zeros((PAD - 1, width), F32)], axis=0).astype(BF16)
    parts = weights_ref.shape[0]
    each = 2 * width // parts
    for part in range(parts):
        weights_ref[part, pl.ds(0, each)] = grad_all[part * each : (part + 1) * each]
        weights_ref[part, pl.ds(each, PAD)] = bias_rows

    self_grad_ref[...] = dot(pre_grad, w_self_ref[...], COLS_T)
    mean_grad = dot(pre_grad, w_nbr_ref[...], COLS_T)
    for b in range(blocks_n):
        part = mean_grad[b * BLK : (b + 1) * BLK] / spreads[b]
        sum_grad_ref[pl.ds(b * BLK, BLK)] = part.astype(BF16)


def layer(dims, plan, gathered, below, above, rows, tiles, degree, w_self, w_nbr, bias, cot, parts):
    blocks_n, links_n, peers_n, per_peer = dims
    slots_n = peers_n * per_peer
    rows_n, width = rows.shape
    table_n = blocks_n + 2 + slots_n
    smem = pl.BlockSpec(memory_space=pltpu.SMEM)
    hbm = pl.BlockSpec(memory_space=pl.ANY)
    vmem = pl.BlockSpec(memory_space=pltpu.VMEM)
    return pl.pallas_call(
        functools.partial(layer_kernel, *dims),
        out_shape=(
            jax.ShapeDtypeStruct((rows_n, width), BF16),
            jax.ShapeDtypeStruct((rows_n, width), F32),
            jax.ShapeDtypeStruct((rows_n, width), BF16),
            jax.ShapeDtypeStruct((parts, 2 * width // parts + PAD, width), BF16),
        ),
        in_specs=[smem, hbm, vmem, vmem] + [hbm] * 7,
        out_specs=(vmem,) * 4,
        scratch_shapes=[
            pltpu.VMEM(tiles.shape, BF16),
            pltpu.VMEM(degree.shape, degree.dtype),
            pltpu.VMEM(w_self.shape, BF16),
            pltpu.VMEM(w_nbr.shape, BF16),
            pltpu.VMEM(bias.shape, F32),
            pltpu.VMEM(cot.shape, BF16),
            pltpu.VMEM(((table_n + 1) * BLK, width), BF16),
            pltpu.SemaphoreType.DMA((6,)),
            pltpu.SemaphoreType.DMA((blocks_n,)),
            pltpu.SemaphoreType.DMA((slots_n,)),
        ],
        compiler_params=pltpu.CompilerParams(vmem_limit_bytes=56 * 2**20),
        cost_estimate=pl.CostEstimate(
            flops=800_000_000, bytes_accessed=8_000_000, transcendentals=rows_n * width
        ),
        name="layer",
    )(plan, gathered, below, above, rows, tiles, degree, w_self, w_nbr, bias, cot)


def links_kernel(
    blocks_n,
    links_n,
    peers_n,
    per_peer,
    plan_ref,
    tiles_hbm,
    self_grad_ref,
    sum_grad_ref,
    base_ref,
    to_above_ref,
    to_below_ref,
    slots_ref,
    tiles_ref,
    grads,
    tile_sems,
):
    rows_n, width = base_ref.shape
    halo = blocks_n + 2
    slots_n = peers_n * per_peer
    tile_copies = [
        pltpu.make_async_copy(
            tiles_hbm.at[pl.ds(b * links_n, links_n)],
            tiles_ref.at[pl.ds(b * links_n, links_n)],
            tile_sems.at[b],
        )
        for b in range(blocks_n)
    ]
    for copy in tile_copies:
        copy.start()
    grads[...] = jnp.zeros_like(grads)
    entries = live_entries(plan_ref, blocks_n, links_n, peers_n, per_peer)
    for b in range(blocks_n):
        tile_copies[b].wait()
        sum_grad = sum_grad_ref[pl.ds(b * BLK, BLK)]
        for k in range(links_n):
            at = b * links_n + k
            where = block(entries[at])
            grads[where] += dot(tiles_ref[at], sum_grad, ROWS_T)
    base_ref[...] = self_grad_ref[...] + grads[pl.ds(0, rows_n)]
    to_below_ref[...] = grads[pl.ds(rows_n, BLK)].astype(BF16)
    to_above_ref[...] = grads[pl.ds(rows_n + BLK, BLK)].astype(BF16)
    for slot in range(slots_n):
        slots_ref[pl.ds(slot * BLK, BLK)] = grads[pl.ds((halo + slot) * BLK, BLK)].astype(BF16)


def links(dims, plan, tiles, self_grad, sum_grad):
    blocks_n, links_n, peers_n, per_peer = dims
    slots_n = peers_n * per_peer
    rows_n, width = self_grad.shape
    table_n = blocks_n + 2 + slots_n
    smem = pl.BlockSpec(memory_space=pltpu.SMEM)
    hbm = pl.BlockSpec(memory_space=pl.ANY)
    vmem = pl.BlockSpec(memory_space=pltpu.VMEM)
    return pl.pallas_call(
        functools.partial(links_kernel, *dims),
        out_shape=(
            jax.ShapeDtypeStruct((rows_n, width), F32),
            jax.ShapeDtypeStruct((BLK, width), BF16),
            jax.ShapeDtypeStruct((BLK, width), BF16),
            jax.ShapeDtypeStruct((slots_n * BLK, width), BF16),
        ),
        in_specs=[smem, hbm, vmem, vmem],
        out_specs=(vmem,) * 4,
        scratch_shapes=[
            pltpu.VMEM(tiles.shape, BF16),
            pltpu.VMEM(((table_n + 1) * BLK, width), F32),
            pltpu.SemaphoreType.DMA((blocks_n,)),
        ],
        compiler_params=pltpu.CompilerParams(vmem_limit_bytes=56 * 2**20),
        cost_estimate=pl.CostEstimate(flops=400_000_000, bytes_accessed=6_000_000, transcendentals=0),
        name="links",
    )(plan, tiles, self_grad, sum_grad)


def collect_kernel(blocks_n, sent_ref, base_ref, returned_ref, below_ref, above_ref, out_ref, total):
    rows_n, width = base_ref.shape
    total[pl.ds(0, rows_n)] = base_ref[...]
    total[pl.ds(rows_n, BLK)] = jnp.zeros((BLK, width), F32)
    total[pl.ds(0, BLK)] += below_ref[...].astype(F32)
    total[pl.ds(rows_n - BLK, BLK)] += above_ref[...].astype(F32)
    peers_n, per_peer = sent_ref.shape
    for p in range(peers_n):
        for s in range(per_peer):
            owner = sent_ref[p, s]
            where = block(jnp.where(owner < 0, blocks_n, owner))
            total[where] += returned_ref[pl.ds((p * per_peer + s) * BLK, BLK)].astype(F32)
    out_ref[...] = total[pl.ds(0, rows_n)]


def collect(sent, base, returned, below, above):
    rows_n, width = base.shape
    smem = pl.BlockSpec(memory_space=pltpu.SMEM)
    vmem = pl.BlockSpec(memory_space=pltpu.VMEM)
    return pl.pallas_call(
        functools.partial(collect_kernel, rows_n // BLK),
        out_shape=jax.ShapeDtypeStruct((rows_n, width), F32),
        in_specs=[smem] + [vmem] * 4,
        out_specs=vmem,
        scratch_shapes=[pltpu.VMEM((rows_n + BLK, width), F32)],
        compiler_params=pltpu.CompilerParams(vmem_limit_bytes=16 * 2**20),
        cost_estimate=pl.CostEstimate(flops=5_000_000, bytes_accessed=4_000_000, transcendentals=0),
        name="collect",
    )(sent, base, returned, below, above)


def row_sum(terms):
    terms = [terms[i].astype(F32) for i in range(terms.shape[0])]
    while len(terms) > 1:
        terms = [terms[i] + terms[i + 1] for i in range(0, len(terms), 2)]
    return terms[0]


def shift(block_rows, axis, step):
    count = lax.axis_size(axis)
    pairs = [(i, i + step) for i in range(count) if 0 <= i + step < count]
    return lax.ppermute(block_rows, axis, pairs)


def swap(array, axis, rings=None):
    return lax.all_to_all(
        array, axis, split_axis=0, concat_axis=0, tiled=True, axis_index_groups=rings
    )


def on_device(
    features, send_list, nbr_count, nbr_index, tiles, degree, w_self, w_nbr, bias, cotangent
):
    rows = features[0]
    rows_n, width = rows.shape
    blocks_n = rows_n // BLK
    links_n = nbr_index.shape[-1]
    groups = lax.axis_size("grp")
    doms = lax.axis_size("dom")

    with jax.named_scope("gather_rows"):
        slots = send_list.shape[-1]
        lists = jnp.pad(send_list[0, 0].T.astype(BF16), ((0, PAD - slots), (0, width - doms)))
        wide = jnp.concatenate([rows, lists], axis=0).astype(F32) * SCALE
        packed = lax.all_gather(wide.astype(jnp.float16), "dom", tiled=True)
        gathered = (packed.astype(F32) * (1.0 / SCALE)).astype(BF16)
        lists = packed.reshape(doms, rows_n + PAD, width)[:, rows_n : rows_n + slots]
        recv = lax.dynamic_slice_in_dim(lists, lax.axis_index("dom"), 1, axis=2)
        recv = jnp.round(recv.astype(F32) * (1.0 / SCALE)).astype(jnp.int32)
    with jax.named_scope("rims"):
        below = shift(rows[rows_n - BLK :], "grp", 1)
        above = shift(rows[:BLK], "grp", -1)

    inner = 1 << ((groups.bit_length()) // 2)
    outer = groups // inner

    rings_z = [[y * inner + z for z in range(inner)] for y in range(outer)]
    rings_y = [[y * inner + z for y in range(outer)] for z in range(inner)]
    dims = (blocks_n, links_n, doms, slots)
    plan = jnp.concatenate([recv.reshape(-1), nbr_count.reshape(-1), nbr_index.reshape(-1)])
    flat_tiles = tiles.reshape(blocks_n * links_n, BLK, BLK)
    hidden, self_grad, sum_grad, partial = layer(
        dims,
        plan,
        gathered,
        below,
        above,
        rows,
        flat_tiles,
        degree.reshape(blocks_n, BLK),
        w_self,
        w_nbr,
        bias.reshape(1, width),
        cotangent[0],
        inner,
    )
    with jax.named_scope("weight_sums_z"):
        chunk = swap(partial, "grp", rings_z)
    base, to_above, to_below, slot_grads = links(dims, plan, flat_tiles, self_grad, sum_grad)
    with jax.named_scope("weight_sums"):
        chunk = row_sum(chunk).astype(BF16)
        chunk, slot_grads = lax.optimization_barrier((chunk, slot_grads))
    with jax.named_scope("return_slots"):
        returned = swap(slot_grads, "dom")
    with jax.named_scope("return_rims"):
        from_above = shift(to_below, "grp", -1)
        from_below = shift(to_above, "grp", 1)
    with jax.named_scope("weight_sums"):
        chunk = row_sum(lax.all_gather(chunk, "grp", axis_index_groups=rings_y)).astype(BF16)
        chunk = row_sum(lax.all_gather(chunk, "dom"))
        chunk = chunk * (1.0 / math.sqrt(rows_n * doms * groups))
        each = chunk.shape[0] - PAD
        bias_grad = chunk[each]
        finished, returned = lax.optimization_barrier((chunk[:each].astype(BF16), returned))
        whole = jnp.broadcast_to(finished[None], (inner, each, width))
        whole = swap(whole, "grp", rings_z).reshape(2 * width, width).astype(F32)
    feat_grad = collect(send_list[0, 0], base, returned, from_below, from_above)
    return hidden[None], feat_grad[None], whole[:width], whole[width:], bias_grad


def solution(mesh):
    in_specs = (
        P("dom", "grp", None),
        P("dom", "grp", None, None),
        P("dom", "grp", None),
        P("dom", "grp", None, None),
        P("dom", "grp", None, None, None),
        P("dom", "grp"),
        P(),
        P(),
        P(),
        P("dom", "grp", None),
    )
    out_specs = (P("dom", "grp", None), P("dom", "grp", None), P(), P(), P())
    return jax.shard_map(
        on_device, mesh=mesh, in_specs=in_specs, out_specs=out_specs, check_vma=False
    )
```

time: 153 us -> 170 us (1.11)
  between operations: 14.2 us -> 0.82 us
  blocking collectives: 91.2 us -> 103 us
  starting transfers between devices: 16.9 us -> 28.4 us
  waiting for transfers between devices: 8.55 us -> 13.4 us
  Pallas kernels: 9.25 us -> 13.8 us
  other arithmetic: 7.7 us -> 5.06 us
    all_gather x1 -> x2, blocking collectives: 17.9 us -> 61.6 us  [the longest x1 37.2 us: on_device(): chunk = row_sum(lax.all_gather(chunk, 'dom'))]
    all_to_all x1 -> x0, blocking collectives: 31.6 us -> none  [swap(): return lax.all_to_all(array, axis, split_axis=0, concat_axis=0, tiled=True)]
    all_to_all x1 -> x3, starting transfers between devices: 5.65 us -> 16.9 us  [swap(): lax.all_to_all(array, axis, split_axis=0, concat_axis=0, tiled=True, axis...]
    pallas_call x1 -> x3, Pallas kernels: 9.25 us -> 13.8 us  [the longest x1 6.51 us: layer(): pl.pallas_call(functools.partial(layer_kernel, *dims), out_shape=(jax.Sha...]
    ppermute x4, waiting for transfers between devices: 0.01 us -> 3.94 us  [shift(): return lax.ppermute(block_rows, axis, pairs)]
    broadcast_in_dim x1 -> x0, other arithmetic: 1.88 us -> none  [on_device(): feat_grad[None]]
    all_to_all x1 -> x3, waiting for transfers between devices: 8.51 us -> 9.49 us  [swap(): lax.all_to_all(array, axis, split_axis=0, concat_axis=0, tiled=True, axis...]
  transfers between devices with their start and end apart: 6 -> 7, of which waited for: 1 -> 4; matrix products, arithmetic and copies ran while one was open for 5% -> 4% of each run, Pallas kernels for 0% -> 4%
where the time goes in v4:
time: 170 us; the launch traced here: 169 us
  blocking collectives  103 us (61%)
  starting transfers between devices  28.4 us (17%)
  Pallas kernels  13.8 us (8%)
  waiting for transfers between devices  13.4 us (8%)
  other arithmetic  5.06 us (3%)
  local copies, waits for them, and re-layouts  4.23 us (2%)
    all_gather x1, blocking collectives, on_device(): packed = lax.all_gather(wide.astype(jnp.float16), 'dom', tiled=True)  41.7 us
    all_gather x1, blocking collectives, on_device(): chunk = row_sum(lax.all_gather(chunk, 'dom'))  37.2 us
    all_gather x1, blocking collectives, on_device(): lax.all_gather(chunk, 'grp', axis_index_groups=rings_y)  24.4 us
    all_to_all x3, starting transfers between devices, swap(): lax.all_to_all(array, axis, split_axis=0, concat_axis=0, tiled=True, axis...  16.9 us
    ppermute x4, starting transfers between devices, shift(): return lax.ppermute(block_rows, axis, pairs)  11.6 us
    all_to_all x3, waiting for transfers between devices, swap(): lax.all_to_all(array, axis, split_axis=0, concat_axis=0, tiled=True, axis...  9.49 us
    pallas_call x1, Pallas kernels, layer(): pl.pallas_call(functools.partial(layer_kernel, *dims), out_shape=(jax.Sha...  6.51 us
    pallas_call x1, Pallas kernels, links(): pl.pallas_call(functools.partial(links_kernel, *dims), out_shape=(jax.Sha...  5.37 us
  transfers between devices with their start and end apart: 7, of which 4 were waited for; matrix products, arithmetic and copies ran while one was open for 4% of the time, Pallas kernels for 4%

profile of v4, /device:TPU:1, one launch (start us, length us, event | category | flops | bytes accessed | tf_op | source)
XLA Modules:
  0.0 169.1 jit_solution(15219679736151708604)
XLA Ops:
  0.6 0.9 slice_bitcast_fusion
  1.5 5.7 %collective-permute-start = (bf16[128,256]{1,0:T(8,128)(2,1)S(1)}, bf16[128,256]{1,0:T(8,128)(2,1)S(1)}, u32[]{:S(2)}, u32[]{:S(2)}) collective-permute-start(bf16[128,256]{1,0:T(8,128)(2,1)S(1)} %get-tuple-element.32), channel_id=1, source_target_pairs={{0,1},{1,2},{2,3},{3,4},{4,5},{5,6},{6,7},{7,8},{8,9},{9,10},{10,1... | collective-permute-start | bytes 196616 | tf_op jit(solution)/shard_map/rims/ppermute | solution.py:320
  7.3 1.3 collective-permute-start.1
  8.6 0.7 convert_bitcast_fusion
  9.3 1.0 multiply_convert_fusion.1
  10.3 41.7 %all-gather.2 = f16[8448,256]{1,0:T(8,128)(2,1)S(1)} all-gather(f16[528,256]{1,0:T(8,128)(2,1)S(1)} %multiply_convert_fusion.1), channel_id=1, replica_groups=mesh['dom'=16,'grp'=64] {'dom'}, dimensions={0}, use_global_device_ids=true | all-gather | bytes 4595712 | tf_op jit(solution)/shard_map/gather_rows/all_gather | solution.py:343
  52.0 2.6 %multiply_convert_fusion.gathered_ref = bf16[8448,256]{1,0:T(8,128)(2,1)} fusion(f16[8448,256]{1,0:T(8,128)(2,1)S(1)} %all-gather.2), kind=kLoop, calls=%fused_computation | loop fusion | flops 6488064 | bytes 8650752 | tf_op jit(solution)/shard_map/gather_rows/convert_element_type | solution.py:344
  55.7 0.6 copy-done.1
  56.3 6.5 %layer.1 = (bf16[512,256]{1,0:T(8,128)(2,1)}, f32[512,256]{1,0:T(8,128)}, bf16[512,256]{1,0:T(8,128)(2,1)}, bf16[8,80,256]{2,1,0:T(8,128)(2,1)}) custom-call(s32[84]{0:T(128)} %pad_add_fusion.plan_ref, bf16[8448,256]{1,0:T(8,128)(2,1)} %multiply_convert_fusion.gathered_ref, bf16[128,256]{1,0:T(8,128)(2,1)} %copy-done.1, bf16[128,256]{1,0:T(8,128)(2,1)} %copy-done.2, ...), custom_call_target="tpu_custom_call" | custom-call | flops 800000000 | bytes 8000000 | tf_op jit(solution)/shard_map/layer/pallas_call | solution.py:174
  62.8 7.8 %all-to-all-start = ((bf16[8,80,256]{2,1,0:T(8,128)(2,1)}), bf16[8,80,256]{2,1,0:T(8,128)(2,1)S(1)}, u32[]{:S(2)}, u32[]{:S(2)}) async-start(bf16[8,80,256]{2,1,0:T(8,128)(2,1)} %get-tuple-element.21), calls=%async_computation | async-start | bytes 655360 | tf_op jit(solution)/shard_map/weight_sums_z/all_to_all | solution.py:324
  70.7 5.4 %links.1 = (f32[512,256]{1,0:T(8,128)}, bf16[128,256]{1,0:T(8,128)(2,1)}, bf16[128,256]{1,0:T(8,128)(2,1)}, bf16[4096,256]{1,0:T(8,128)(2,1)}) custom-call(s32[84]{0:T(128)} %pad_add_fusion.plan_ref, bf16[48,128,128]{2,1,0:T(8,128)(2,1)} %bitcast.33, f32[512,256]{1,0:T(8,128)} %get-tuple-element.18.self_grad_ref, bf16[512,256]{1,0:T(8,128)(2,1)} %get-tuple-element.19.sum_grad_ref), custom_call_target="tpu_custom_call" | custom-call | flops 400000000 | bytes 6000000 | tf_op jit(solution)/shard_map/links/pallas_call | solution.py:258
  76.1 8.3 %all-to-all-done = bf16[8,80,256]{2,1,0:T(8,128)(2,1)S(1)} async-done(((bf16[8,80,256]{2,1,0:T(8,128)(2,1)}), bf16[8,80,256]{2,1,0:T(8,128)(2,1)S(1)}, u32[]{:S(2)}, u32[]{:S(2)}) %all-to-all-start) | async-done | bytes 327712 | tf_op jit(solution)/shard_map/weight_sums_z/all_to_all | solution.py:324
  84.5 5.6 %all-to-all-start.1 = ((bf16[16,256,256]{2,1,0:T(8,128)(2,1)}), bf16[16,256,256]{2,1,0:T(8,128)(2,1)S(1)}, u32[]{:S(2)}, u32[]{:S(2)}) async-start(bf16[16,256,256]{2,1,0:T(8,128)(2,1)} %bitcast.34), calls=%async_computation.1 | async-start | bytes 4194304 | tf_op jit(solution)/shard_map/return_slots/all_to_all | solution.py:324
  90.1 24.4 %all-gather = bf16[640,256]{1,0:T(8,128)(2,1)S(1)} all-gather(bf16[80,256]{1,0:T(8,128)(2,1)S(1)} %fusion.2), channel_id=2, replica_groups={{0,8,16,24,32,40,48,56},{1,9,17,25,33,41,49,57},{2,10,18,26,34,42,50,58..., dimensions={0}, use_global_device_ids=true | all-gather | bytes 368640 | tf_op jit(solution)/shard_map/weight_sums/all_gather | solution.py:387
  114.6 37.2 %all_gather.16 = bf16[16,80,256]{2,1,0:T(8,128)(2,1)S(1)} all-gather(bf16[1,80,256]{2,1,0:T(8,128)(2,1)S(1)} %fusion.3), channel_id=1, replica_groups=mesh['dom'=16,'grp'=64] {'dom'}, dimensions={0}, use_global_device_ids=true | all-gather | bytes 696320 | tf_op jit(solution)/shard_map/weight_sums/all_gather | solution.py:388
  151.8 0.7 broadcast_in_dim.14
  152.6 3.4 %all-to-all-start.2 = ((bf16[8,64,256]{2,1,0:T(8,128)(2,1)}), bf16[8,64,256]{2,1,0:T(8,128)(2,1)S(1)}, u32[]{:S(2)}, u32[]{:S(2)}) async-start(bf16[8,64,256]{2,1,0:T(8,128)(2,1)} %broadcast_in_dim.14), calls=%async_computation.2 | async-start | bytes 524288 | tf_op jit(solution)/shard_map/weight_sums/all_to_all | solution.py:324
  156.0 3.2 %collective-permute-start.2 = (bf16[128,256]{1,0:T(8,128)(2,1)S(1)}, bf16[128,256]{1,0:T(8,128)(2,1)S(1)}, u32[]{:S(2)}, u32[]{:S(2)}) collective-permute-start(bf16[128,256]{1,0:T(8,128)(2,1)S(1)} %copy-done.7), channel_id=1, source_target_pairs={{0,1},{1,2},{2,3},{3,4},{4,5},{5,6},{6,7},{7,8},{8,9},{9,10},{10,1... | collective-permute-start | bytes 196616 | tf_op jit(solution)/shard_map/return_rims/ppermute | solution.py:320
  159.3 1.3 collective-permute-start.3
  161.2 1.0 collective-permute-done.2.below_ref
  162.2 2.9 %collective-permute-done.3.above_ref = bf16[128,256]{1,0:T(8,128)(2,1)S(1)} collective-permute-done((bf16[128,256]{1,0:T(8,128)(2,1)S(1)}, bf16[128,256]{1,0:T(8,128)(2,1)S(1)}, u32[]{:S(2)}, u32[]{:S(2)}) %collective-permute-start.3) | collective-permute-done | bytes 65568 | tf_op jit(solution)/shard_map/return_rims/ppermute | solution.py:320
  165.2 1.9 %collect.1 = f32[512,256]{1,0:T(8,128)} custom-call(s32[16,2]{1,0:T(8,128)S(1)} %copy.20.sent_ref, f32[512,256]{1,0:T(8,128)S(1)} %copy-done, bf16[4096,256]{1,0:T(8,128)(2,1)S(1)} %bitcast.30, bf16[128,256]{1,0:T(8,128)(2,1)S(1)} %collective-permute-done.2.below_ref, bf16[128,256]{1,0:T(8,128)(2,1)S(1)} %collective-permute-done.3.above_ref), custom_call_target="tpu_custom_call" | custom-call | flops 5000000 | bytes 4000000 | tf_op jit(solution)/shard_map/collect/pallas_call | solution.py:298
  167.1 1.1 all-to-all-done.2
  168.2 0.8 fusion.5
  (31 shorter events, 2.0 us)
Async XLA Ops:
  1.5 54.2 %collective-permute-start = (bf16[128,256]{1,0:T(8,128)(2,1)S(1)}, bf16[128,256]{1,0:T(8,128)(2,1)S(1)}, u32[]{:S(2)}, u32[]{:S(2)}) collective-permute-start(bf16[128,256]{1,0:T(8,128)(2,1)S(1)} %get-tuple-element.32), channel_id=1, source_target_pairs={{0,1},{1,2},{2,3},{3,4},{4,5},{5,6},{6,7},{7,8},{8,9},{9,10},{10,1... | collective-permute-start | bytes 196616 | tf_op jit(solution)/shard_map/rims/ppermute | solution.py:320
  7.3 48.4 %collective-permute-start.1 = (bf16[128,256]{1,0:T(8,128)(2,1)S(1)}, bf16[128,256]{1,0:T(8,128)(2,1)S(1)}, u32[]{:S(2)}, u32[]{:S(2)}) collective-permute-start(bf16[128,256]{1,0:T(8,128)(2,1)S(1)} %get-tuple-element.31), channel_id=1, source_target_pairs={{1,0},{2,1},{3,2},{4,3},{5,4},{6,5},{7,6},{8,7},{9,8},{10,9},{11,1... | collective-permute-start | bytes 196616 | tf_op jit(solution)/shard_map/rims/ppermute | solution.py:320
  52.0 3.0 %copy-start.3 = (s32[1,1,4,12]{3,2,1,0:T(4,128)S(1)}, s32[1,1,4,12]{3,2,1,0:T(4,128)}, u32[]{:S(2)}) copy-start(s32[1,1,4,12]{3,2,1,0:T(4,128)} %param.13) | copy-start | bytes 580
  52.0 3.1 %copy-start.5 = (s32[1,1,4]{2,1,0:T(1,128)S(1)}, s32[1,1,4]{2,1,0:T(1,128)}, u32[]{:S(2)}) copy-start(s32[1,1,4]{2,1,0:T(1,128)} %param.12) | copy-start | bytes 52
  55.7 0.6 copy-start.1
  55.7 0.6 copy-start.2
  62.8 21.6 %all-to-all-start = ((bf16[8,80,256]{2,1,0:T(8,128)(2,1)}), bf16[8,80,256]{2,1,0:T(8,128)(2,1)S(1)}, u32[]{:S(2)}, u32[]{:S(2)}) async-start(bf16[8,80,256]{2,1,0:T(8,128)(2,1)} %get-tuple-element.21), calls=%async_computation | async-start | bytes 655360 | tf_op jit(solution)/shard_map/weight_sums_z/all_to_all | solution.py:324
  76.0 79.9 %copy-start.7 = (bf16[128,256]{1,0:T(8,128)(2,1)S(1)}, bf16[128,256]{1,0:T(8,128)(2,1)}, u32[]{:S(2)}) copy-start(bf16[128,256]{1,0:T(8,128)(2,1)} %get-tuple-element.26) | copy-start | bytes 196612
  76.1 83.2 %copy-start.6 = (bf16[128,256]{1,0:T(8,128)(2,1)S(1)}, bf16[128,256]{1,0:T(8,128)(2,1)}, u32[]{:S(2)}) copy-start(bf16[128,256]{1,0:T(8,128)(2,1)} %get-tuple-element.27) | copy-start | bytes 196612
  76.1 84.5 %copy-start.4 = (s32[1,1,16,2]{2,3,1,0:T(2,128)S(1)}, s32[1,1,16,2]{2,3,1,0:T(2,128)}, u32[]{:S(2)}) copy-start(s32[1,1,16,2]{2,3,1,0:T(2,128)} %param.11) | copy-start | bytes 388
  76.1 89.1 %copy-start = (f32[512,256]{1,0:T(8,128)S(1)}, f32[512,256]{1,0:T(8,128)}, u32[]{:S(2)}) copy-start(f32[512,256]{1,0:T(8,128)} %get-tuple-element.20.base_ref) | copy-start | bytes 1572868
  84.5 67.3 %all-to-all-start.1 = ((bf16[16,256,256]{2,1,0:T(8,128)(2,1)}), bf16[16,256,256]{2,1,0:T(8,128)(2,1)S(1)}, u32[]{:S(2)}, u32[]{:S(2)}) async-start(bf16[16,256,256]{2,1,0:T(8,128)(2,1)} %bitcast.34), calls=%async_computation.1 | async-start | bytes 4194304 | tf_op jit(solution)/shard_map/return_slots/all_to_all | solution.py:324
  152.6 15.7 %all-to-all-start.2 = ((bf16[8,64,256]{2,1,0:T(8,128)(2,1)}), bf16[8,64,256]{2,1,0:T(8,128)(2,1)S(1)}, u32[]{:S(2)}, u32[]{:S(2)}) async-start(bf16[8,64,256]{2,1,0:T(8,128)(2,1)} %broadcast_in_dim.14), calls=%async_computation.2 | async-start | bytes 524288 | tf_op jit(solution)/shard_map/weight_sums/all_to_all | solution.py:324
  156.0 6.2 %collective-permute-start.2 = (bf16[128,256]{1,0:T(8,128)(2,1)S(1)}, bf16[128,256]{1,0:T(8,128)(2,1)S(1)}, u32[]{:S(2)}, u32[]{:S(2)}) collective-permute-start(bf16[128,256]{1,0:T(8,128)(2,1)S(1)} %copy-done.7), channel_id=1, source_target_pairs={{0,1},{1,2},{2,3},{3,4},{4,5},{5,6},{6,7},{7,8},{8,9},{9,10},{10,1... | collective-permute-start | bytes 196616 | tf_op jit(solution)/shard_map/return_rims/ppermute | solution.py:320
  159.3 5.9 %collective-permute-start.3 = (bf16[128,256]{1,0:T(8,128)(2,1)S(1)}, bf16[128,256]{1,0:T(8,128)(2,1)S(1)}, u32[]{:S(2)}, u32[]{:S(2)}) collective-permute-start(bf16[128,256]{1,0:T(8,128)(2,1)S(1)} %copy-done.6), channel_id=1, source_target_pairs={{1,0},{2,1},{3,2},{4,3},{5,4},{6,5},{7,6},{8,7},{9,8},{10,9},{11,1... | collective-permute-start | bytes 196616 | tf_op jit(solution)/shard_map/return_rims/ppermute | solution.py:320

commit v5 on v2

--- a/solution.py
+++ b/solution.py
@@ -6,11 +6,13 @@
 from jax import lax
 from jax.experimental import pallas as pl
 from jax.experimental.pallas import tpu as pltpu
+from jax.sharding import Mesh
 from jax.sharding import PartitionSpec as P
 
 BLK = 128
 PAD = 16
 SCALE = 8192.0
+GRP = ("hi", "lo")
 F32 = jnp.float32
 BF16 = jnp.bfloat16
 ROWS_T = (((0,), (0,)), ((), ()))
@@ -44,8 +46,10 @@
     hidden_ref,
     base_ref,
     rims_ref,
-    sends_ref,
-    weights_ref,
+    keep_ref,
+    give_ref,
+    mean_ref,
+    pre_grad_ref,
     tiles_ref,
     degree_ref,
     w_self_ref,
@@ -145,19 +149,8 @@
     hidden_ref[...] = (pre_act * gate).astype(BF16)
     slope = gate * (1.0 + pre_act * (1.0 - gate))
     pre_grad = (cot_ref[...].astype(F32) * slope).astype(BF16)
-    grad_all = jnp.concatenate([dot(rows, pre_grad, ROWS_T), dot(mean_rows, pre_grad, ROWS_T)], axis=0)
-    grad_all = grad_all.astype(BF16)
-    bias_sum = jnp.sum(pre_grad.astype(F32), axis=0, keepdims=True)
-    parts, each = weights_ref.shape[0], weights_ref.shape[1] // 2
-    halves = width // BLK
-    lines = [bias_sum[:, i * BLK : (i + 1) * BLK] for i in range(halves)]
-    lines.append(jnp.zeros((each - halves, BLK), F32))
-    bias_tile = jnp.concatenate(lines, axis=0).astype(BF16)
-    stride = parts // halves
-    for i in range(halves):
-        chunk = grad_all[:, i * BLK : (i + 1) * BLK].reshape(stride, each, BLK)
-        weights_ref[pl.ds(i * stride, stride), pl.ds(0, each), :] = chunk
-    weights_ref[:, pl.ds(each, each), :] = jnp.broadcast_to(bias_tile[None], (parts, each, BLK))
+    mean_ref[...] = mean_rows
+    pre_grad_ref[...] = pre_grad
 
     mean_grad = dot(pre_grad, w_nbr_ref[...], COLS_T)
     for b in range(blocks_n):
@@ -168,32 +161,37 @@
             grads[where] += dot(tiles_ref[at], sum_grad, ROWS_T)
     base_ref[...] = dot(pre_grad, w_self_ref[...], COLS_T) + grads[pl.ds(0, rows_n)]
     rims_ref[...] = grads[pl.ds(rows_n, 2 * BLK)].astype(BF16)
-    for p in range(peers_n):
-        sends_ref[pl.ds(p * rows_n, rows_n)] = grads[pl.ds(halo * BLK + p * rows_n, rows_n)].astype(BF16)
-
-
-def layer(recv, count, index, gathered, below, above, rows, tiles, degree, w_self, w_nbr, bias, cot, parts):
+    core = plan_ref[slots_n + blocks_n + blocks_n * links_n]
+    for chip in range(peers_n // 2):
+        here = pl.ds(chip * rows_n, rows_n)
+        for target, side in ((give_ref, 1 - core), (keep_ref, core)):
+            start = halo * BLK + (2 * chip + side) * rows_n
+            target[here] = grads[pl.ds(pl.multiple_of(start, BLK), rows_n)].astype(BF16)
+
+
+def layer(recv, count, index, core, gathered, below, above, rows, tiles, degree, w_self, w_nbr, bias, cot):
     blocks_n, links_n = index.shape
     peers_n, per_peer = recv.shape
     rows_n, width = rows.shape
     table_n = blocks_n + 2 + recv.size
     owners_n = blocks_n + 2 + peers_n * blocks_n
-    plan = jnp.concatenate([recv.reshape(-1), count, index.reshape(-1)])
+    plan = jnp.concatenate([recv.reshape(-1), count, index.reshape(-1), core.reshape(1)])
     smem = pl.BlockSpec(memory_space=pltpu.SMEM)
     hbm = pl.BlockSpec(memory_space=pl.ANY)
     vmem = pl.BlockSpec(memory_space=pltpu.VMEM)
-    each = 2 * width * (width // BLK) // parts
     return pl.pallas_call(
         functools.partial(layer_kernel, blocks_n, links_n, peers_n, per_peer),
         out_shape=(
             jax.ShapeDtypeStruct((rows_n, width), BF16),
             jax.ShapeDtypeStruct((rows_n, width), F32),
             jax.ShapeDtypeStruct((2 * BLK, width), BF16),
-            jax.ShapeDtypeStruct((peers_n * rows_n, width), BF16),
-            jax.ShapeDtypeStruct((parts, 2 * each, BLK), BF16),
+            jax.ShapeDtypeStruct((peers_n // 2 * rows_n, width), BF16),
+            jax.ShapeDtypeStruct((peers_n // 2 * rows_n, width), BF16),
+            jax.ShapeDtypeStruct((rows_n, width), BF16),
+            jax.ShapeDtypeStruct((rows_n, width), BF16),
         ),
         in_specs=[smem] + [hbm] * 10,
-        out_specs=(vmem,) * 5,
+        out_specs=(vmem,) * 7,
         scratch_shapes=[
             pltpu.VMEM(tiles.shape, BF16),
             pltpu.VMEM(degree.shape, degree.dtype),
@@ -215,8 +213,43 @@
     )(plan, gathered, below, above, rows, tiles, degree, w_self, w_nbr, bias, cot)
 
 
+def weights_kernel(rows_ref, mean_ref, pre_grad_ref, out_ref):
+    width = rows_ref.shape[1]
+    pre_grad = pre_grad_ref[...]
+    bias_sum = jnp.sum(pre_grad.astype(F32), axis=0, keepdims=True)
+    grads = [dot(rows_ref[...], pre_grad, ROWS_T), dot(mean_ref[...], pre_grad, ROWS_T)]
+    grad_all = jnp.concatenate(grads, axis=0).astype(BF16)
+    parts, each = out_ref.shape[0], out_ref.shape[1] - PAD
+    halves = width // BLK
+    lines = [bias_sum[:, i * BLK : (i + 1) * BLK] for i in range(halves)]
+    lines.append(jnp.zeros((PAD - halves, BLK), F32))
+    bias_tile = jnp.concatenate(lines, axis=0).astype(BF16)
+    stride = parts // halves
+    for i in range(halves):
+        chunk = grad_all[:, i * BLK : (i + 1) * BLK].reshape(stride, each, BLK)
+        out_ref[pl.ds(i * stride, stride), pl.ds(0, each), :] = chunk
+    out_ref[:, pl.ds(each, PAD), :] = jnp.broadcast_to(bias_tile[None], (parts, PAD, BLK))
+
+
+def weights(rows, mean_rows, pre_grad, parts):
+    rows_n, width = rows.shape
+    each = 2 * width * (width // BLK) // parts
+    vmem = pl.BlockSpec(memory_space=pltpu.VMEM)
+    return pl.pallas_call(
+        weights_kernel,
+        out_shape=jax.ShapeDtypeStruct((parts, each + PAD, BLK), BF16),
+        in_specs=[vmem] * 3,
+        out_specs=vmem,
+        compiler_params=pltpu.CompilerParams(vmem_limit_bytes=16 * 2**20),
+        cost_estimate=pl.CostEstimate(
+            flops=4 * rows_n * width * width, bytes_accessed=1_200_000, transcendentals=0
+        ),
+        name="weights",
+    )(rows, mean_rows, pre_grad)
+
+
 def shift(block_rows, axis, step):
-    count = lax.axis_size(axis)
+    count = math.prod(lax.axis_size(name) for name in axis)
     pairs = [(i, i + step) for i in range(count) if 0 <= i + step < count]
     return lax.ppermute(block_rows, axis, pairs)
 
@@ -232,7 +265,7 @@
     rows_n, width = rows.shape
     blocks_n = rows_n // BLK
     links_n = nbr_index.shape[-1]
-    groups = lax.axis_size("grp")
+    groups = lax.axis_size("hi") * lax.axis_size("lo")
     doms = lax.axis_size("dom")
 
     with jax.named_scope("gather_rows"):
@@ -245,13 +278,14 @@
         recv = lax.dynamic_slice_in_dim(lists, lax.axis_index("dom") * slots, slots, axis=1)
         recv = jnp.round(recv.astype(F32) * (1.0 / SCALE)).astype(jnp.int32)
     with jax.named_scope("rims"):
-        below = shift(rows[rows_n - BLK :], "grp", 1)
-        above = shift(rows[:BLK], "grp", -1)
-
-    hidden, base, rims, sends, partial = layer(
+        below = shift(rows[rows_n - BLK :], GRP, 1)
+        above = shift(rows[:BLK], GRP, -1)
+
+    hidden, base, rims, keep, give, mean_rows, pre_grad = layer(
         recv,
         nbr_count[0, 0],
         nbr_index[0, 0],
+        lax.axis_index("dom") % 2,
         gathered,
         below,
         above,
@@ -262,23 +296,27 @@
         w_nbr,
         bias.reshape(1, width),
         cotangent[0],
-        groups,
     )
 
     with jax.named_scope("return_slots"):
-        returned = lax.psum_scatter(sends, "dom", tiled=True)
+        taken = lax.ppermute(give, "dom", [(i, i ^ 1) for i in range(doms)])
+        partial = weights(rows, mean_rows, pre_grad, lax.axis_size("lo"))
+        taken, partial = lax.optimization_barrier((taken, partial))
+        merged = (keep.astype(F32) + taken.astype(F32)).astype(BF16)
+        rings = [list(range(core, doms, 2)) for core in range(2)]
+        returned = lax.psum_scatter(merged, "dom", tiled=True, axis_index_groups=rings)
     with jax.named_scope("return_rims"):
-        from_above = shift(rims[:BLK], "grp", -1)
-        from_below = shift(rims[BLK:], "grp", 1)
+        from_above = shift(rims[:BLK], GRP, -1)
+        from_below = shift(rims[BLK:], GRP, 1)
     with jax.named_scope("weight_sums"):
-        chunk = jnp.sum(swap(partial, "grp").astype(F32), axis=0)
-        chunk = jnp.sum(lax.all_gather(chunk, "dom"), axis=0)
+        chunk = jnp.sum(swap(partial, "lo").astype(F32), axis=0)
+        chunk = jnp.sum(lax.all_gather(chunk, ("dom", "hi")), axis=0)
         chunk = chunk * (1.0 / math.sqrt(rows_n * doms * groups))
         halves = width // BLK
-        each = chunk.shape[0] // 2
+        each = chunk.shape[0] - PAD
         bias_grad = chunk[each : each + halves].reshape(width)
         finished = chunk[:each].astype(BF16)
-        whole = swap(jnp.broadcast_to(finished[None], (groups, each, BLK)), "grp")
+        whole = swap(jnp.broadcast_to(finished[None], (lax.axis_size("lo"), each, BLK)), "lo")
         whole = whole.reshape(halves, 2 * width, BLK).astype(F32)
         whole = jnp.concatenate([whole[i] for i in range(halves)], axis=1)
     edges = jnp.concatenate(
@@ -289,19 +327,21 @@
 
 
 def solution(mesh):
+    doms, groups = mesh.devices.shape
+    split = Mesh(mesh.devices.reshape(doms, 2, groups // 2), ("dom",) + GRP)
     in_specs = (
-        P("dom", "grp", None),
-        P("dom", "grp", None, None),
-        P("dom", "grp", None),
-        P("dom", "grp", None, None),
-        P("dom", "grp", None, None, None),
-        P("dom", "grp"),
+        P("dom", GRP, None),
+        P("dom", GRP, None, None),
+        P("dom", GRP, None),
+        P("dom", GRP, None, None),
+        P("dom", GRP, None, None, None),
+        P("dom", GRP),
         P(),
         P(),
         P(),
-        P("dom", "grp", None),
+        P("dom", GRP, None),
     )
-    out_specs = (P("dom", "grp", None), P("dom", "grp", None), P(), P(), P())
+    out_specs = (P("dom", GRP, None), P("dom", GRP, None), P(), P(), P())
     return jax.shard_map(
-        on_device, mesh=mesh, in_specs=in_specs, out_specs=out_specs, check_vma=False
+        on_device, mesh=split, in_specs=in_specs, out_specs=out_specs, check_vma=False
     )

time: 153 us -> 227 us (1.48)
  blocking collectives: 91.2 us -> 159 us
  other arithmetic: 7.7 us -> 11.2 us
    all_gather x1, blocking collectives: 17.9 us -> 92.1 us  [on_device(): chunk = jnp.sum(lax.all_gather(chunk, ('dom', 'hi')), axis=0)]
    all_to_all x1, blocking collectives: 31.6 us -> 24.9 us  [swap(): return lax.all_to_all(array, axis, split_axis=0, concat_axis=0, tiled=True)]
    convert_element_type x0 -> x1, other arithmetic: none -> 3.46 us  [on_device(): merged = (keep.astype(F32) + taken.astype(F32)).astype(BF16)]
    all_to_all x1, waiting for transfers between devices: 8.51 us -> 5.31 us  [swap(): return lax.all_to_all(array, axis, split_axis=0, concat_axis=0, tiled=True)]
  transfers between devices with their start and end apart: 6 -> 7, of which waited for: 1 -> 2; matrix products, arithmetic and copies ran while one was open for 5% -> 3% of each run, Pallas kernels for 0% -> 0%
where the time goes in v5:
time: 227 us; the launch traced here: 225 us
  blocking collectives  159 us (70%)
  starting transfers between devices  19 us (8%)
  between operations  14.2 us (6%)
  other arithmetic  11.2 us (5%)
  Pallas kernels  9.29 us (4%)
  waiting for transfers between devices  7.3 us (3%)
  local copies, waits for them, and re-layouts  5.28 us (2%)
    all_gather x1, blocking collectives, on_device(): chunk = jnp.sum(lax.all_gather(chunk, ('dom', 'hi')), axis=0)  92.1 us
    all_gather x1, blocking collectives, on_device(): packed = lax.all_gather(wide.astype(jnp.float16), 'dom', tiled=True)  41.7 us
    all_to_all x1, blocking collectives, swap(): return lax.all_to_all(array, axis, split_axis=0, concat_axis=0, tiled=True)  24.9 us
    ppermute x4, starting transfers between devices, shift(): return lax.ppermute(block_rows, axis, pairs)  11.5 us
    pallas_call x1, Pallas kernels, layer(): pl.pallas_call(functools.partial(layer_kernel, blocks_n, links_n, peers_n...  8.94 us
    all_to_all x1, starting transfers between devices, swap(): return lax.all_to_all(array, axis, split_axis=0, concat_axis=0, tiled=True)  5.43 us
    all_to_all x1, waiting for transfers between devices, swap(): return lax.all_to_all(array, axis, split_axis=0, concat_axis=0, tiled=True)  5.31 us
  transfers between devices with their start and end apart: 7, of which 2 were waited for; matrix products, arithmetic and copies ran while one was open for 3% of the time, Pallas kernels for 0%

profile of v5, /device:TPU:1, one launch (start us, length us, event | category | flops | bytes accessed | tf_op | source)
XLA Modules:
  0.0 225.0 jit_solution(9299406000943599709)
XLA Ops:
  7.2 0.9 slice_bitcast_fusion
  8.1 5.7 %collective-permute-start = (bf16[128,256]{1,0:T(8,128)(2,1)S(1)}, bf16[128,256]{1,0:T(8,128)(2,1)S(1)}, u32[]{:S(2)}, u32[]{:S(2)}) collective-permute-start(bf16[128,256]{1,0:T(8,128)(2,1)S(1)} %get-tuple-element.28), channel_id=1, source_target_pairs={{0,1},{1,2},{2,3},{3,4},{4,5},{5,6},{6,7},{7,8},{8,9},{9,10},{10,1... | collective-permute-start | bytes 196616 | tf_op jit(solution)/shard_map/rims/ppermute | solution.py:254
  13.8 1.3 collective-permute-start.1
  15.2 0.7 convert_element_type.63
  16.0 1.0 multiply_convert_fusion.1
  17.1 41.7 %all-gather.2 = f16[8448,256]{1,0:T(8,128)(2,1)S(1)} all-gather(f16[528,256]{1,0:T(8,128)(2,1)S(1)} %multiply_convert_fusion.1), channel_id=1, replica_groups=mesh['dom'=16,'hi'=2,'lo'=32] {'dom'}, dimensions={0}, use_global_device_ids=true | all-gather | bytes 4595712 | tf_op jit(solution)/shard_map/gather_rows/all_gather | solution.py:274
  58.8 2.6 %multiply_convert_fusion.gathered_ref = bf16[8448,256]{1,0:T(8,128)(2,1)} fusion(f16[8448,256]{1,0:T(8,128)(2,1)S(1)} %all-gather.2), kind=kLoop, calls=%fused_computation | loop fusion | flops 6488064 | bytes 8650752 | tf_op jit(solution)/shard_map/gather_rows/convert_element_type | solution.py:275
  61.6 0.7 pad_add_fusion.plan_ref
  62.3 0.6 copy-done.5
  63.0 8.9 %layer.1 = (bf16[512,256]{1,0:T(8,128)(2,1)}, f32[512,256]{1,0:T(8,128)}, bf16[256,256]{1,0:T(8,128)(2,1)}, bf16[4096,256]{1,0:T(8,128)(2,1)}, bf16[4096,256]{1,...) custom-call(s32[85]{0:T(128)} %pad_add_fusion.plan_ref, ...), custom_call_target="tpu_custom_call" | custom-call | flops 1300000000 | bytes 12000000 | tf_op jit(solution)/shard_map/layer/pallas_call | solution.py:182
  71.9 2.0 collective-permute-start.2
  74.0 0.9 copy-done.1
  74.9 0.9 copy-done.2
  76.2 1.9 collective-permute-done.2
  78.2 3.5 %add_convert_fusion = bf16[4096,256]{1,0:T(8,128)(2,1)} fusion(bf16[4096,256]{1,0:T(8,128)(2,1)S(1)} %collective-permute-done.2, bf16[4096,256]{1,0:T(8,128)(2,1)} %get-tuple-element.16), kind=kLoop, calls=%fused_computation.1 | loop fusion | flops 4194304 | bytes 6291456 | tf_op jit(solution)/shard_map/return_slots/convert_element_type | solution.py:305
  81.7 24.9 %all_to_all.10 = bf16[32,48,128]{2,1,0:T(8,128)(2,1)S(1)} all-to-all(bf16[32,48,128]{2,1,0:T(8,128)(2,1)S(1)} %weights.1), channel_id=1, replica_groups=mesh['dom'=16,'hi'=2,'lo'=32] {'lo'}, dimensions={0} | all-to-all | bytes 786432 | tf_op jit(solution)/shard_map/weight_sums/all_to_all | solution.py:258
  106.6 92.1 %all-gather = f32[1536,128]{1,0:T(8,128)S(1)} all-gather(f32[48,128]{1,0:T(8,128)S(1)} %convert_reduce_fusion), channel_id=2, replica_groups=mesh['dom'=16,'hi'=2,'lo'=32] {'dom','hi'}, dimensions={0}, use_global_device_ids=true | all-gather | bytes 811008 | tf_op jit(solution)/shard_map/weight_sums/all_gather | solution.py:313
  198.8 0.7 broadcast_in_dim.18
  199.5 5.4 %all-to-all-start.1 = ((bf16[32,32,128]{2,1,0:T(8,128)(2,1)}), bf16[32,32,128]{2,1,0:T(8,128)(2,1)S(1)}, u32[]{:S(2)}, u32[]{:S(2)}) async-start(bf16[32,32,128]{2,1,0:T(8,128)(2,1)} %broadcast_in_dim.18), calls=%async_computation.2 | async-start | bytes 524288 | tf_op jit(solution)/shard_map/weight_sums/all_to_all | solution.py:258
  205.0 3.1 %collective-permute-start.3 = (bf16[128,256]{1,0:T(8,128)(2,1)S(1)}, bf16[128,256]{1,0:T(8,128)(2,1)S(1)}, u32[]{:S(2)}, u32[]{:S(2)}) collective-permute-start(bf16[128,256]{1,0:T(8,128)(2,1)S(1)} %get-tuple-element.29), channel_id=1, source_target_pairs={{0,1},{1,2},{2,3},{3,4},{4,5},{5,6},{6,7},{7,8},{8,9},{9,10},{10,1... | collective-permute-start | bytes 196616 | tf_op jit(solution)/shard_map/return_rims/ppermute | solution.py:254
  208.2 1.3 collective-permute-start.4
  210.0 5.3 %all-to-all-done.1 = bf16[32,32,128]{2,1,0:T(8,128)(2,1)S(1)} async-done(((bf16[32,32,128]{2,1,0:T(8,128)(2,1)}), bf16[32,32,128]{2,1,0:T(8,128)(2,1)S(1)}, u32[]{:S(2)}, u32[]{:S(2)}) %all-to-all-start.1) | async-done | bytes 262176 | tf_op jit(solution)/shard_map/weight_sums/all_to_all | solution.py:258
  215.4 0.8 pad_maximum_fusion
  216.3 1.9 add_bitcast_fusion
  (39 shorter events, 1.7 us)
Async XLA Ops:
  7.2 209.1 %reduce-scatter.2.cloned.1.call-start = ((), (), s32[]{:S(2)}) async-start(), calls=%async_computation.3 | async-start | bytes 2359296 | tf_op jit(solution)/shard_map/return_slots/reduce_scatter | solution.py:307
  8.1 54.2 %collective-permute-start = (bf16[128,256]{1,0:T(8,128)(2,1)S(1)}, bf16[128,256]{1,0:T(8,128)(2,1)S(1)}, u32[]{:S(2)}, u32[]{:S(2)}) collective-permute-start(bf16[128,256]{1,0:T(8,128)(2,1)S(1)} %get-tuple-element.28), channel_id=1, source_target_pairs={{0,1},{1,2},{2,3},{3,4},{4,5},{5,6},{6,7},{7,8},{8,9},{9,10},{10,1... | collective-permute-start | bytes 196616 | tf_op jit(solution)/shard_map/rims/ppermute | solution.py:254
  13.8 48.5 %collective-permute-start.1 = (bf16[128,256]{1,0:T(8,128)(2,1)S(1)}, bf16[128,256]{1,0:T(8,128)(2,1)S(1)}, u32[]{:S(2)}, u32[]{:S(2)}) collective-permute-start(bf16[128,256]{1,0:T(8,128)(2,1)S(1)} %get-tuple-element.27), channel_id=1, source_target_pairs={{1,0},{2,1},{3,2},{4,3},{5,4},{6,5},{7,6},{8,7},{9,8},{10,9},{11,1... | collective-permute-start | bytes 196616 | tf_op jit(solution)/shard_map/rims/ppermute | solution.py:254
  58.8 2.8 %copy-start.7 = (s32[1,1,4,12]{3,2,1,0:T(4,128)S(1)}, s32[1,1,4,12]{3,2,1,0:T(4,128)}, u32[]{:S(2)}) copy-start(s32[1,1,4,12]{3,2,1,0:T(4,128)} %param.13) | copy-start | bytes 580
  58.8 2.9 %copy-start.8 = (s32[1,1,4]{2,1,0:T(1,128)S(1)}, s32[1,1,4]{2,1,0:T(1,128)}, u32[]{:S(2)}) copy-start(s32[1,1,4]{2,1,0:T(1,128)} %param.12) | copy-start | bytes 52
  61.3 12.6 %copy-start = (bf16[1,512,256]{2,1,0:T(8,128)(2,1)S(1)}, bf16[1,512,256]{2,1,0:T(8,128)(2,1)}, u32[]{:S(2)}) copy-start(bf16[1,512,256]{2,1,0:T(8,128)(2,1)} %param.10) | copy-start | bytes 786436
  62.3 0.6 copy-start.5
  62.3 0.6 copy-start.6
  71.9 6.3 %collective-permute-start.2 = (bf16[4096,256]{1,0:T(8,128)(2,1)}, bf16[4096,256]{1,0:T(8,128)(2,1)S(1)}, u32[]{:S(2)}, u32[]{:S(2)}) collective-permute-start(bf16[4096,256]{1,0:T(8,128)(2,1)} %get-tuple-element.17), channel_id=1, source_target_pairs={{0,64},{64,0},{128,192},{192,128},{256,320},{320,256},{384,448},{4... | collective-permute-start | bytes 6291464 | tf_op jit(solution)/shard_map/return_slots/ppermute | solution.py:302
  74.0 1.0 copy-start.1
  74.9 0.9 copy-start.2
  81.6 123.4 %copy-start.4 = (bf16[256,256]{1,0:T(8,128)(2,1)S(1)}, bf16[256,256]{1,0:T(8,128)(2,1)}, u32[]{:S(2)}) copy-start(bf16[256,256]{1,0:T(8,128)(2,1)} %get-tuple-element.21) | copy-start | bytes 393220
  81.6 134.6 %copy-start.3 = (f32[512,256]{1,0:T(8,128)S(1)}, f32[512,256]{1,0:T(8,128)}, u32[]{:S(2)}) copy-start(f32[512,256]{1,0:T(8,128)} %get-tuple-element.15) | copy-start | bytes 1572868
  199.5 15.8 %all-to-all-start.1 = ((bf16[32,32,128]{2,1,0:T(8,128)(2,1)}), bf16[32,32,128]{2,1,0:T(8,128)(2,1)S(1)}, u32[]{:S(2)}, u32[]{:S(2)}) async-start(bf16[32,32,128]{2,1,0:T(8,128)(2,1)} %broadcast_in_dim.18), calls=%async_computation.2 | async-start | bytes 524288 | tf_op jit(solution)/shard_map/weight_sums/all_to_all | solution.py:258
  205.0 11.2 %collective-permute-start.3 = (bf16[128,256]{1,0:T(8,128)(2,1)S(1)}, bf16[128,256]{1,0:T(8,128)(2,1)S(1)}, u32[]{:S(2)}, u32[]{:S(2)}) collective-permute-start(bf16[128,256]{1,0:T(8,128)(2,1)S(1)} %get-tuple-element.29), channel_id=1, source_target_pairs={{0,1},{1,2},{2,3},{3,4},{4,5},{5,6},{6,7},{7,8},{8,9},{9,10},{10,1... | collective-permute-start | bytes 196616 | tf_op jit(solution)/shard_map/return_rims/ppermute | solution.py:254
  208.2 8.1 %collective-permute-start.4 = (bf16[128,256]{1,0:T(8,128)(2,1)S(1)}, bf16[128,256]{1,0:T(8,128)(2,1)S(1)}, u32[]{:S(2)}, u32[]{:S(2)}) collective-permute-start(bf16[128,256]{1,0:T(8,128)(2,1)S(1)} %get-tuple-element.30), channel_id=1, source_target_pairs={{1,0},{2,1},{3,2},{4,3},{5,4},{6,5},{7,6},{8,7},{9,8},{10,9},{11,1... | collective-permute-start | bytes 196616 | tf_op jit(solution)/shard_map/return_rims/ppermute | solution.py:254
Sparse Core Ops, SparseCore 0:
  81.8 43.6 reduce-scatter.1

commit v6 on v2

--- a/solution.py
+++ b/solution.py
@@ -41,6 +41,11 @@
     w_nbr_hbm,
     bias_hbm,
     cot_hbm,
+    hidden_hbm,
+    base_hbm,
+    rims_hbm,
+    sends_hbm,
+    weights_hbm,
     hidden_ref,
     base_ref,
     rims_ref,
@@ -57,6 +62,8 @@
     own_sems,
     tile_sems,
     table_sems,
+    out_sems,
+    send_sems,
 ):
     rows_n, width = cot_ref.shape
     halo = blocks_n + 2
@@ -99,6 +106,11 @@
         )
     for copy in own + table_copies + tile_copies:
         copy.start()
+    outs = []
+
+    def write_out(source, target, sem):
+        outs.append(pltpu.make_async_copy(source, target, sem))
+        outs[-1].start()
 
     table[pl.ds(table_n * BLK, BLK)] = jnp.zeros((BLK, width), BF16)
     grads[...] = jnp.zeros_like(grads)
@@ -143,6 +155,7 @@
     pre_act = self_act + dot(mean_rows, w_nbr_ref[...])
     gate = jax.nn.sigmoid(pre_act)
     hidden_ref[...] = (pre_act * gate).astype(BF16)
+    write_out(hidden_ref, hidden_hbm, out_sems.at[0])
     slope = gate * (1.0 + pre_act * (1.0 - gate))
     pre_grad = (cot_ref[...].astype(F32) * slope).astype(BF16)
     grad_all = jnp.concatenate([dot(rows, pre_grad, ROWS_T), dot(mean_rows, pre_grad, ROWS_T)], axis=0)
@@ -158,18 +171,25 @@
         chunk = grad_all[:, i * BLK : (i + 1) * BLK].reshape(stride, each, BLK)
         weights_ref[pl.ds(i * stride, stride), pl.ds(0, each), :] = chunk
     weights_ref[:, pl.ds(each, each), :] = jnp.broadcast_to(bias_tile[None], (parts, each, BLK))
+    write_out(weights_ref, weights_hbm, out_sems.at[1])
 
     mean_grad = dot(pre_grad, w_nbr_ref[...], COLS_T)
     for b in range(blocks_n):
         sum_grad = (mean_grad[b * BLK : (b + 1) * BLK] / spreads[b]).astype(BF16)
+        side_by_side = jnp.concatenate([tiles_ref[b * links_n + k] for k in range(links_n)], axis=1)
+        products = dot(side_by_side, sum_grad, ROWS_T)
         for k in range(links_n):
-            at = b * links_n + k
-            where = block(owners[at])
-            grads[where] += dot(tiles_ref[at], sum_grad, ROWS_T)
+            grads[block(owners[b * links_n + k])] += products[k * BLK : (k + 1) * BLK]
+    for p in range(peers_n):
+        here = pl.ds(p * rows_n, rows_n)
+        sends_ref[here] = grads[pl.ds(halo * BLK + p * rows_n, rows_n)].astype(BF16)
+        write_out(sends_ref.at[here], sends_hbm.at[here], send_sems.at[p])
+    rims_ref[...] = grads[pl.ds(rows_n, 2 * BLK)].astype(BF16)
+    write_out(rims_ref, rims_hbm, out_sems.at[2])
     base_ref[...] = dot(pre_grad, w_self_ref[...], COLS_T) + grads[pl.ds(0, rows_n)]
-    rims_ref[...] = grads[pl.ds(rows_n, 2 * BLK)].astype(BF16)
-    for p in range(peers_n):
-        sends_ref[pl.ds(p * rows_n, rows_n)] = grads[pl.ds(halo * BLK + p * rows_n, rows_n)].astype(BF16)
+    write_out(base_ref, base_hbm, out_sems.at[3])
+    for copy in outs:
+        copy.wait()
 
 
 def layer(recv, count, index, gathered, below, above, rows, tiles, degree, w_self, w_nbr, bias, cot, parts):
@@ -181,20 +201,21 @@
     plan = jnp.concatenate([recv.reshape(-1), count, index.reshape(-1)])
     smem = pl.BlockSpec(memory_space=pltpu.SMEM)
     hbm = pl.BlockSpec(memory_space=pl.ANY)
-    vmem = pl.BlockSpec(memory_space=pltpu.VMEM)
     each = 2 * width * (width // BLK) // parts
+    outs = (
+        jax.ShapeDtypeStruct((rows_n, width), BF16),
+        jax.ShapeDtypeStruct((rows_n, width), F32),
+        jax.ShapeDtypeStruct((2 * BLK, width), BF16),
+        jax.ShapeDtypeStruct((peers_n * rows_n, width), BF16),
+        jax.ShapeDtypeStruct((parts, 2 * each, BLK), BF16),
+    )
     return pl.pallas_call(
         functools.partial(layer_kernel, blocks_n, links_n, peers_n, per_peer),
-        out_shape=(
-            jax.ShapeDtypeStruct((rows_n, width), BF16),
-            jax.ShapeDtypeStruct((rows_n, width), F32),
-            jax.ShapeDtypeStruct((2 * BLK, width), BF16),
-            jax.ShapeDtypeStruct((peers_n * rows_n, width), BF16),
-            jax.ShapeDtypeStruct((parts, 2 * each, BLK), BF16),
-        ),
+        out_shape=outs,
         in_specs=[smem] + [hbm] * 10,
-        out_specs=(vmem,) * 5,
-        scratch_shapes=[
+        out_specs=(hbm,) * 5,
+        scratch_shapes=[pltpu.VMEM(out.shape, out.dtype) for out in outs]
+        + [
             pltpu.VMEM(tiles.shape, BF16),
             pltpu.VMEM(degree.shape, degree.dtype),
             pltpu.VMEM(w_self.shape, BF16),
@@ -206,6 +227,8 @@
             pltpu.SemaphoreType.DMA((6,)),
             pltpu.SemaphoreType.DMA((blocks_n,)),
             pltpu.SemaphoreType.DMA((2 + recv.size,)),
+            pltpu.SemaphoreType.DMA((4,)),
+            pltpu.SemaphoreType.DMA((peers_n,)),
         ],
         compiler_params=pltpu.CompilerParams(vmem_limit_bytes=56 * 2**20),
         cost_estimate=pl.CostEstimate(
@@ -239,15 +262,14 @@
         lists = jnp.pad(send_list.reshape(1, -1).astype(BF16), ((0, PAD - 1), (0, width - send_list.size)))
         wide = jnp.concatenate([rows, lists], axis=0).astype(F32) * SCALE
         packed = lax.all_gather(wide.astype(jnp.float16), "dom", tiled=True)
+        below = shift(rows[rows_n - BLK :], "grp", 1)
+        above = shift(rows[:BLK], "grp", -1)
+        packed, below, above = lax.optimization_barrier((packed, below, above))
         gathered = (packed.astype(F32) * (1.0 / SCALE)).astype(BF16)
         lists = packed.reshape(doms, rows_n + PAD, width)[:, rows_n]
         slots = send_list.shape[-1]
         recv = lax.dynamic_slice_in_dim(lists, lax.axis_index("dom") * slots, slots, axis=1)
         recv = jnp.round(recv.astype(F32) * (1.0 / SCALE)).astype(jnp.int32)
-    with jax.named_scope("rims"):
-        below = shift(rows[rows_n - BLK :], "grp", 1)
-        above = shift(rows[:BLK], "grp", -1)
-
     hidden, base, rims, sends, partial = layer(
         recv,
         nbr_count[0, 0],

time: 153 us -> 157 us (1.026)
  transfers between devices with their start and end apart: 6 -> 6, of which waited for: 1 -> 1; matrix products, arithmetic and copies ran while one was open for 5% -> 3% of each run, Pallas kernels for 0% -> 0%
where the time goes in v6:
time: 157 us; the launch traced here: 155 us
  blocking collectives  92.6 us (59%)
  starting transfers between devices  16.7 us (11%)
  between operations  14.2 us (9%)
  Pallas kernels  9.3 us (6%)
  other arithmetic  9.26 us (6%)
  waiting for transfers between devices  8.55 us (5%)
  local copies, waits for them, and re-layouts  4.57 us (3%)
    all_gather x1, blocking collectives, on_device(): packed = lax.all_gather(wide.astype(jnp.float16), 'dom', tiled=True)  43.1 us
    all_to_all x1, blocking collectives, swap(): return lax.all_to_all(array, axis, split_axis=0, concat_axis=0, tiled=True)  31.8 us
    all_gather x1, blocking collectives, on_device(): chunk = jnp.sum(lax.all_gather(chunk, 'dom'), axis=0)  17.7 us
    ppermute x4, starting transfers between devices, shift(): return lax.ppermute(block_rows, axis, pairs)  11.2 us
    pallas_call x1, Pallas kernels, layer(): pl.pallas_call(functools.partial(layer_kernel, blocks_n, links_n, peers_n...  9.3 us
    all_to_all x1, waiting for transfers between devices, swap(): return lax.all_to_all(array, axis, split_axis=0, concat_axis=0, tiled=True)  8.51 us
    all_to_all x1, starting transfers between devices, swap(): return lax.all_to_all(array, axis, split_axis=0, concat_axis=0, tiled=True)  5.47 us
    convert_element_type x1, other arithmetic, on_device(): gathered = (packed.astype(F32) * (1.0 / SCALE)).astype(BF16)  4.13 us
  transfers between devices with their start and end apart: 6, of which 1 were waited for; matrix products, arithmetic and copies ran while one was open for 3% of the time, Pallas kernels for 0%

profile of v6, /device:TPU:1, one launch (start us, length us, event | category | flops | bytes accessed | tf_op | source)
XLA Modules:
  0.0 155.3 jit_solution(8442478710834392423)
XLA Ops:
  7.2 0.9 slice_bitcast_fusion
  8.1 5.7 %collective-permute-start = (bf16[128,256]{1,0:T(8,128)(2,1)S(1)}, bf16[128,256]{1,0:T(8,128)(2,1)S(1)}, u32[]{:S(2)}, u32[]{:S(2)}) collective-permute-start(bf16[128,256]{1,0:T(8,128)(2,1)S(1)} %get-tuple-element.26), channel_id=1, source_target_pairs={{0,1},{1,2},{2,3},{3,4},{4,5},{5,6},{6,7},{7,8},{8,9},{9,10},{10,1... | collective-permute-start | bytes 196616 | tf_op jit(solution)/shard_map/gather_rows/ppermute | solution.py:244
  13.9 1.3 collective-permute-start.1
  15.2 0.7 convert_element_type.54
  15.8 0.1 copy.19
  15.9 0.1 convert_element_type.55
  16.0 1.0 multiply_convert_fusion.1
  17.1 43.1 %all-gather.2 = f16[8448,256]{1,0:T(8,128)(2,1)} all-gather(f16[528,256]{1,0:T(8,128)(2,1)S(1)} %multiply_convert_fusion.1), channel_id=1, replica_groups=mesh['dom'=16,'grp'=64] {'dom'}, dimensions={0}, use_global_device_ids=true | all-gather | bytes 4595712 | tf_op jit(solution)/shard_map/gather_rows/all_gather | solution.py:264
  60.3 4.1 %multiply_convert_fusion.gathered_ref = bf16[8448,256]{1,0:T(8,128)(2,1)} fusion(f16[8448,256]{1,0:T(8,128)(2,1)} %all-gather.2), kind=kLoop, calls=%fused_computation | loop fusion | flops 6488064 | bytes 8650752 | tf_op jit(solution)/shard_map/gather_rows/convert_element_type | solution.py:268
  64.4 0.9 slice.55
  65.5 0.6 pad_add_fusion.plan_ref
  66.1 9.3 %layer.1 = (bf16[512,256]{1,0:T(8,128)(2,1)}, f32[512,256]{1,0:T(8,128)}, bf16[256,256]{1,0:T(8,128)(2,1)}, bf16[8192,256]{1,0:T(8,128)(2,1)}, bf16[64,32,128]{2,1,0:T(8,128)(2,1)}) custom-call(s32[84]{0:T(128)} %pad_add_fusion.plan_ref, bf16[8448,256]{1,0:T(8,128)(2,1)} %multiply_convert_fusion.gathered_ref, bf16[128,256]{1,0:T(8,128)(2,1)} %copy-done.3, ...), custom_call_target="tpu_custom_call" | custom-call | flops 1300000000 | bytes 12000000 | tf_op jit(solution)/shard_map/layer/pallas_call | solution.py:212
  75.5 1.0 copy-done.1
  76.5 31.8 %all_to_all.10 = bf16[64,32,128]{2,1,0:T(8,128)(2,1)S(1)} all-to-all(bf16[64,32,128]{2,1,0:T(8,128)(2,1)S(1)} %copy-done.1), channel_id=1, replica_groups=mesh['dom'=16,'grp'=64] {'grp'}, dimensions={0} | all-to-all | bytes 1048576 | tf_op jit(solution)/shard_map/weight_sums/all_to_all | solution.py:248
  108.3 0.1 convert_reduce_fusion
  108.4 17.7 %all-gather = f32[512,128]{1,0:T(8,128)S(1)} all-gather(f32[32,128]{1,0:T(8,128)S(1)} %convert_reduce_fusion), channel_id=2, replica_groups=mesh['dom'=16,'grp'=64] {'dom'}, dimensions={0}, use_global_device_ids=true | all-gather | bytes 278528 | tf_op jit(solution)/shard_map/weight_sums/all_gather | solution.py:297
  126.1 0.7 broadcast_in_dim.18
  126.9 5.5 %all-to-all-start.1 = ((bf16[64,16,128]{2,1,0:T(8,128)(2,1)}), bf16[64,16,128]{2,1,0:T(8,128)(2,1)S(1)}, u32[]{:S(2)}, u32[]{:S(2)}) async-start(bf16[64,16,128]{2,1,0:T(8,128)(2,1)} %broadcast_in_dim.18), calls=%async_computation.2 | async-start | bytes 524288 | tf_op jit(solution)/shard_map/weight_sums/all_to_all | solution.py:248
  132.4 2.9 %collective-permute-start.2 = (bf16[128,256]{1,0:T(8,128)(2,1)S(1)}, bf16[128,256]{1,0:T(8,128)(2,1)S(1)}, u32[]{:S(2)}, u32[]{:S(2)}) collective-permute-start(bf16[128,256]{1,0:T(8,128)(2,1)S(1)} %get-tuple-element.27), channel_id=1, source_target_pairs={{0,1},{1,2},{2,3},{3,4},{4,5},{5,6},{6,7},{7,8},{8,9},{9,10},{10,1... | collective-permute-start | bytes 196616 | tf_op jit(solution)/shard_map/return_rims/ppermute | solution.py:244
  135.3 1.3 collective-permute-start.3
  136.6 0.6 slice_bitcast_fusion.2
  137.2 8.5 %all-to-all-done.1 = bf16[64,16,128]{2,1,0:T(8,128)(2,1)S(1)} async-done(((bf16[64,16,128]{2,1,0:T(8,128)(2,1)}), bf16[64,16,128]{2,1,0:T(8,128)(2,1)S(1)}, u32[]{:S(2)}, u32[]{:S(2)}) %all-to-all-start.1) | async-done | bytes 262176 | tf_op jit(solution)/shard_map/weight_sums/all_to_all | solution.py:248
  145.7 0.8 pad_maximum_fusion
  146.6 1.9 %add_bitcast_fusion = f32[1,512,256]{2,1,0:T(8,128)} fusion(f32[512,256]{1,0:T(8,128)S(1)} %copy-done, bf16[512,256]{1,0:T(8,128)(2,1)} %reduce-scatter.2.cloned.1.call-done, bf16[128,256]{1,0:T(8,128)(2,1)S(1)} %collective-permute-done.3, bf16[128,256]{1,0:T(8,128)(2,1)S(1)} %collective-permute-done.2, bf16[512]{0:T(512)(128)(2,1)S(1)} %pad.8.clone), kind=kLoop, calls=%fused_computation.7 | loop fusion | flops 1179648 | bytes 1442816 | tf_op jit(solution)/shard_map/broadcast_in_dim | solution.py:310
  (31 shorter events, 0.5 us)
Async XLA Ops:
  7.2 53.0 %copy-start.5 = (s32[1,1,4,12]{3,2,1,0:T(4,128)S(1)}, s32[1,1,4,12]{3,2,1,0:T(4,128)}, u32[]{:S(2)}) copy-start(s32[1,1,4,12]{3,2,1,0:T(4,128)} %param.13) | copy-start | bytes 580
  7.2 139.4 %reduce-scatter.2.cloned.1.call-start = ((), (), s32[]{:S(2)}) async-start(), calls=%async_computation.3 | async-start | bytes 4456448 | tf_op jit(solution)/shard_map/return_slots/reduce_scatter | solution.py:291
  8.1 52.2 %collective-permute-start = (bf16[128,256]{1,0:T(8,128)(2,1)S(1)}, bf16[128,256]{1,0:T(8,128)(2,1)S(1)}, u32[]{:S(2)}, u32[]{:S(2)}) collective-permute-start(bf16[128,256]{1,0:T(8,128)(2,1)S(1)} %get-tuple-element.26), channel_id=1, source_target_pairs={{0,1},{1,2},{2,3},{3,4},{4,5},{5,6},{6,7},{7,8},{8,9},{9,10},{10,1... | collective-permute-start | bytes 196616 | tf_op jit(solution)/shard_map/gather_rows/ppermute | solution.py:244
  13.9 46.4 %collective-permute-start.1 = (bf16[128,256]{1,0:T(8,128)(2,1)S(1)}, bf16[128,256]{1,0:T(8,128)(2,1)S(1)}, u32[]{:S(2)}, u32[]{:S(2)}) collective-permute-start(bf16[128,256]{1,0:T(8,128)(2,1)S(1)} %get-tuple-element.25), channel_id=1, source_target_pairs={{1,0},{2,1},{3,2},{4,3},{5,4},{6,5},{7,6},{8,7},{9,8},{10,9},{11,1... | collective-permute-start | bytes 196616 | tf_op jit(solution)/shard_map/gather_rows/ppermute | solution.py:244
  60.3 5.2 %copy-start.6 = (s32[1,1,4]{2,1,0:T(1,128)S(1)}, s32[1,1,4]{2,1,0:T(1,128)}, u32[]{:S(2)}) copy-start(s32[1,1,4]{2,1,0:T(1,128)} %param.12) | copy-start | bytes 52
  60.3 4.2 %copy-start.3 = (bf16[128,256]{1,0:T(8,128)(2,1)}, bf16[128,256]{1,0:T(8,128)(2,1)S(1)}, u32[]{:S(2)}) copy-start(bf16[128,256]{1,0:T(8,128)(2,1)S(1)} %collective-permute-done.below_ref) | copy-start | bytes 196612
  60.3 4.2 %copy-start.4 = (bf16[128,256]{1,0:T(8,128)(2,1)}, bf16[128,256]{1,0:T(8,128)(2,1)S(1)}, u32[]{:S(2)}) copy-start(bf16[128,256]{1,0:T(8,128)(2,1)S(1)} %collective-permute-done.1.above_ref) | copy-start | bytes 196612
  75.4 1.0 copy-start.1
  75.4 56.9 %copy-start.2 = (bf16[256,256]{1,0:T(8,128)(2,1)S(1)}, bf16[256,256]{1,0:T(8,128)(2,1)}, u32[]{:S(2)}) copy-start(bf16[256,256]{1,0:T(8,128)(2,1)} %get-tuple-element.19) | copy-start | bytes 393220
  75.4 71.1 %copy-start = (f32[512,256]{1,0:T(8,128)S(1)}, f32[512,256]{1,0:T(8,128)}, u32[]{:S(2)}) copy-start(f32[512,256]{1,0:T(8,128)} %get-tuple-element.17) | copy-start | bytes 1572868
  126.9 18.8 %all-to-all-start.1 = ((bf16[64,16,128]{2,1,0:T(8,128)(2,1)}), bf16[64,16,128]{2,1,0:T(8,128)(2,1)S(1)}, u32[]{:S(2)}, u32[]{:S(2)}) async-start(bf16[64,16,128]{2,1,0:T(8,128)(2,1)} %broadcast_in_dim.18), calls=%async_computation.2 | async-start | bytes 524288 | tf_op jit(solution)/shard_map/weight_sums/all_to_all | solution.py:248
  132.4 14.2 %collective-permute-start.2 = (bf16[128,256]{1,0:T(8,128)(2,1)S(1)}, bf16[128,256]{1,0:T(8,128)(2,1)S(1)}, u32[]{:S(2)}, u32[]{:S(2)}) collective-permute-start(bf16[128,256]{1,0:T(8,128)(2,1)S(1)} %get-tuple-element.27), channel_id=1, source_target_pairs={{0,1},{1,2},{2,3},{3,4},{4,5},{5,6},{6,7},{7,8},{8,9},{9,10},{10,1... | collective-permute-start | bytes 196616 | tf_op jit(solution)/shard_map/return_rims/ppermute | solution.py:244
  135.3 11.2 %collective-permute-start.3 = (bf16[128,256]{1,0:T(8,128)(2,1)S(1)}, bf16[128,256]{1,0:T(8,128)(2,1)S(1)}, u32[]{:S(2)}, u32[]{:S(2)}) collective-permute-start(bf16[128,256]{1,0:T(8,128)(2,1)S(1)} %get-tuple-element.28), channel_id=1, source_target_pairs={{1,0},{2,1},{3,2},{4,3},{5,4},{6,5},{7,6},{8,7},{9,8},{10,9},{11,1... | collective-permute-start | bytes 196616 | tf_op jit(solution)/shard_map/return_rims/ppermute | solution.py:244
Sparse Core Ops, SparseCore 0:
  75.6 68.3 reduce-scatter.1
